TPU v7x, 32 devices: a whole 2x2x4 slice. The times are simulated.
32 devices in a mesh: pb: 8 (over z, core), ka: 2 (over y), ha: 2 (over x).
Axes of the slice: x: 2, y: 2, z: 4, core: 2. Of those that a mesh axis runs over, the one named last changes fastest.
Arguments:
- context: bfloat16 [8192, 512], P(('pb', 'ka')), may hold values from -6 to 6
- item_owner: int32 [8192, 1], P(('pb', 'ka')), may hold values from 0 to 15; in each aligned block of 512 rows (0 to 511, 512 to 1023, ...) at most 64 rows name the same one
- item_offset: int32 [8192], P(('pb', 'ka')), may hold values from 0 to 8191
- lengths: int32 [8, 4, 4], P('pb'), may hold values from 1 to 253, as said below
- times: int32 [8, 4, 256], P('pb'), may hold values from 0 to 255
- table: bfloat16 [131072, 512], P(('pb', 'ka')), may hold values from -4 to 4
- cotangent: bfloat16 [8192, 512], P(('pb', 'ka')), may hold values from -6 to 6
- ln_in_gain: float32 [512], replicated, may hold values from 0.5 to 1.5
- w_uvqk: bfloat16 [512, 4, 512], P('pb', None, 'ha'), may hold values from -0.25 to 0.25
- b_uvqk: float32 [4, 512], P(None, 'ha'), may hold values from -2 to 2
- rel_bias: float32 [8, 256], P('ha'), may hold values from -4 to 4
- time_bias: float32 [8, 128], P('ha'), may hold values from -4 to 4
- ln_out_gain: float32 [512], P('ha'), may hold values from 0.5 to 1.5
- w_out: bfloat16 [512, 512], P('ha', 'pb'), may hold values from -0.25 to 0.25
- b_out: float32 [512], replicated, may hold values from -2 to 2
Outputs:
- mixed: bfloat16 [8192, 512], P(('pb', 'ka'), 'ha')
- input_grad: bfloat16 [8192, 512], P(('pb', 'ka'))
- table_grad: float32 [131072, 512], P(('pb', 'ka'))
- grad_ln_in_gain: float32 [512], replicated
- grad_w_uvqk: float32 [512, 4, 512], P(('pb', 'ka'), None, 'ha')
- grad_b_uvqk: float32 [4, 512], P(None, 'ha')
- grad_rel_bias: float32 [8, 256], P('ha')
- grad_time_bias: float32 [8, 128], P('ha')
- grad_ln_out_gain: float32 [512], P('ha')
- grad_w_out: float32 [512, 512], P('ha', ('pb', 'ka'))
- grad_b_out: float32 [512], replicated
Inputs may be any that keep to these rules, and one draw needn't show every extreme that they name: `item_owner`: among the 512 rows of one device (aligned blocks), no owner is named more than 64 times. The 4 lengths of a stream sum to at most 256; positions after their sum are padding.
All inputs are finite; a program needn't handle non-finite values.
Results may differ from a plain program's by a relative error of at most 0.0094.
Values may be sent and summed in bfloat16 or wider, within the bound.
A program may use at most 192 MiB of HBM per device.

v0:
```python
import jax
import jax.numpy as jnp
from jax import lax
from jax.sharding import PartitionSpec as P

DH = 64
TOK_DEV = 128
MB = 4
SEQ_GRP = 4


epsilon = 1e-05


def silu_slope(values):
    sigma = jax.nn.sigmoid(values)
    return sigma * (1.0 + values * (1.0 - sigma))


def norm_rows(values, gain):
    centered = values - jnp.mean(values, axis=-1, keepdims=True)
    inverse = lax.rsqrt(jnp.mean(centered * centered, axis=-1, keepdims=True) + epsilon)
    unit_rows = centered * inverse
    return (unit_rows * gain, unit_rows, inverse)


def norm_back(grad_unit, unit_rows, inverse):
    first_mean = jnp.mean(grad_unit, axis=-1, keepdims=True)
    second_mean = jnp.mean(grad_unit * unit_rows, axis=-1, keepdims=True)
    return inverse * (grad_unit - first_mean - unit_rows * second_mean)


def stream_layout(lengths_row, group):
    places = jnp.arange(group, dtype=jnp.int32)
    ends = jnp.cumsum(lengths_row, dtype=jnp.int32)
    member = jnp.sum((ends[None, :] <= places[:, None]).astype(jnp.int32), axis=1)
    onehot = (member[:, None] == jnp.arange(SEQ_GRP, dtype=jnp.int32)[None, :]).astype(jnp.float32)
    counted = jnp.maximum(jnp.sum(onehot * lengths_row.astype(jnp.float32)[None, :], axis=1), 1.0)
    return (places, member, counted)


def diagonal_bias(rel_bias, query_first, key_first, query_len, key_len):
    heads, group = rel_bias.shape
    span = query_len + key_len - 1
    padded = jnp.concatenate([jnp.zeros((heads, group), jnp.float32), rel_bias], axis=1)
    window = lax.dynamic_slice_in_dim(
        padded, query_first - key_first - key_len + 1 + group, span, 1
    )
    flipped = jnp.concatenate([window[:, ::-1], jnp.zeros((heads, 1), jnp.float32)], axis=1)
    skewed = jnp.tile(flipped, (1, query_len))[:, : query_len * span].reshape(
        heads, query_len, span
    )
    return skewed[:, :, query_len - 1 : query_len - 1 + key_len]


def diagonal_sums(grad_scores, query_first, key_first, group):
    heads, query_len, key_len = grad_scores.shape
    span = query_len + key_len - 1
    widened = jnp.pad(grad_scores.astype(jnp.float32), ((0, 0), (0, 0), (query_len - 1, 0)))
    flat = jnp.pad(widened.reshape(heads, query_len * span), ((0, 0), (0, query_len)))
    totals = jnp.sum(flat.reshape(heads, query_len, span + 1), axis=1)
    window = totals[:, :span][:, ::-1]
    placed = lax.dynamic_update_slice_in_dim(
        jnp.zeros((heads, 2 * group), jnp.float32),
        window,
        query_first - key_first - key_len + 1 + group,
        1,
    )
    return placed[:, group:]


def bucket_lookup(time_bias, bucket_hot):
    high = time_bias.astype(jnp.bfloat16)
    rest = time_bias - high.astype(jnp.float32)
    middle = rest.astype(jnp.bfloat16)
    lowest = (rest - middle.astype(jnp.float32)).astype(jnp.bfloat16)
    pieces = jnp.einsum(
        "phb,qkb->phqk",
        jnp.stack([high, middle, lowest]),
        bucket_hot,
        preferred_element_type=jnp.float32,
    )
    return pieces[0] + pieces[1] + pieces[2]


def tile_scores(query_heads, key_heads, query_info, key_info, rel_bias, time_bias):
    query_pos, query_member, query_count, query_stamp = query_info
    key_pos, key_member, key_stamp = key_info
    distance = query_pos[:, None] - key_pos[None, :]
    time_index = jnp.clip(query_stamp[:, None] - key_stamp[None, :], 0, time_bias.shape[1] - 1)
    bucket_hot = (
        time_index[:, :, None] == jnp.arange(time_bias.shape[1], dtype=jnp.int32)[None, None, :]
    ).astype(jnp.bfloat16)
    scores = jnp.einsum(
        "qhd,khd->hqk", query_heads, key_heads, preferred_element_type=jnp.float32
    ) * DH ** (-0.5)
    scores = (
        scores
        + diagonal_bias(rel_bias, query_pos[0], key_pos[0], query_pos.shape[0], key_pos.shape[0])
        + bucket_lookup(time_bias, bucket_hot)
    )
    allowed = (
        (query_member[:, None] == key_member[None, :])
        & (query_member[:, None] < SEQ_GRP)
        & (distance >= 0)
    )[None]
    weights = (jnp.where(allowed, jax.nn.silu(scores), 0.0) / query_count[None, :, None]).astype(
        jnp.bfloat16
    )
    return (scores, allowed, weights, bucket_hot)


def score_grads(grad_weights, scores, allowed, query_count):
    return (
        jnp.where(allowed, grad_weights / query_count[None, :, None], 0.0) * silu_slope(scores)
    ).astype(jnp.bfloat16)


def local(
    context,
    item_owner,
    item_offset,
    lengths,
    times,
    table,
    cotangent,
    ln_in_gain,
    w_uvqk,
    b_uvqk,
    rel_bias,
    time_bias,
    ln_out_gain,
    w_out,
    b_out,
):
    owners = lax.axis_size(("pb", "ka"))
    row_count = context.shape[0]
    width = context.shape[1]
    capacity = max(2, 2 * row_count // owners)
    owner_ids = item_owner[:, 0]
    owner_hits = (owner_ids[:, None] == jnp.arange(owners, dtype=jnp.int32)[None, :]).astype(
        jnp.int32
    )
    earlier = jnp.sum((jnp.cumsum(owner_hits, axis=0) - owner_hits) * owner_hits, axis=1)
    slot_index = owner_ids * capacity + earlier
    requests = jnp.zeros((owners * capacity,), jnp.int32).at[slot_index].set(item_offset + 1)
    arrived = lax.all_to_all(
        requests.reshape(owners, capacity), ("pb", "ka"), split_axis=0, concat_axis=0, tiled=True
    ).reshape(-1)
    present = arrived > 0
    local_rows = jnp.maximum(arrived - 1, 0)
    fetched = jnp.where(present[:, None], table[local_rows], jnp.zeros((), jnp.bfloat16))
    returned = lax.all_to_all(
        fetched.reshape(owners, capacity, width),
        ("pb", "ka"),
        split_axis=0,
        concat_axis=0,
        tiled=True,
    )
    embedded = returned.reshape(owners * capacity, width)[slot_index]
    start = context.astype(jnp.float32) + embedded.astype(jnp.float32)
    group = lax.axis_size("ka") * TOK_DEV
    block_start = lax.axis_index("ka") * TOK_DEV
    half_cols = w_out.shape[0]
    heads = half_cols // DH
    full_cols = half_cols * lax.axis_size("ha")
    out_cols = width // lax.axis_size("ha")
    out_start = lax.axis_index("ha") * out_cols
    bias_half = lax.dynamic_slice_in_dim(b_out, out_start, out_cols)
    scale = DH ** (-0.5)
    grad_gain_in = jnp.zeros(ln_in_gain.shape, jnp.float32)
    grad_bias_proj = jnp.zeros(b_uvqk.shape, jnp.float32)
    grad_rel = jnp.zeros(rel_bias.shape, jnp.float32)
    grad_time = jnp.zeros(time_bias.shape, jnp.float32)
    grad_gain_out = jnp.zeros(ln_out_gain.shape, jnp.float32)
    grad_bias_out = jnp.zeros(b_out.shape, jnp.float32)
    weight_total = None
    mixed_parts = []
    grad_parts = []
    for micro in range(MB):
        w_full, w_final = (
            lax.all_gather(w_uvqk, "pb", axis=0, tiled=True),
            lax.all_gather(w_out, "pb", axis=1, tiled=True),
        )
        x_in = start[micro * TOK_DEV : (micro + 1) * TOK_DEV]
        cot_rows = cotangent[micro * TOK_DEV : (micro + 1) * TOK_DEV]
        stamps = times[0, micro]
        places, member, counted = stream_layout(lengths[0, micro], group)
        query_pos = lax.dynamic_slice_in_dim(places, block_start, TOK_DEV)
        query_member = lax.dynamic_slice_in_dim(member, block_start, TOK_DEV)
        query_count = lax.dynamic_slice_in_dim(counted, block_start, TOK_DEV)
        query_stamp = lax.dynamic_slice_in_dim(stamps, block_start, TOK_DEV)
        normed_float, unit_in, inverse_in = norm_rows(x_in, ln_in_gain)
        normed = normed_float.astype(jnp.bfloat16)
        pre_act = (
            jnp.einsum("td,dgc->tgc", normed, w_full, preferred_element_type=jnp.float32) + b_uvqk
        )
        activated = jax.nn.silu(pre_act)
        gate_part = activated[:, 0]
        values = activated[:, 1].astype(jnp.bfloat16)
        queries = activated[:, 2].astype(jnp.bfloat16)
        key_rows = activated[:, 3].astype(jnp.bfloat16)
        key_pair = lax.all_gather(jnp.stack([key_rows, values]), "ka", axis=1, tiled=True)
        all_keys = key_pair[0].reshape(group, heads, DH)
        all_values = key_pair[1].reshape(group, heads, DH)
        query_heads = queries.reshape(TOK_DEV, heads, DH)
        scores, allowed, weights, bucket_hot = tile_scores(
            query_heads,
            all_keys,
            (query_pos, query_member, query_count, query_stamp),
            (places, member, stamps),
            rel_bias,
            time_bias,
        )
        attended = jnp.einsum(
            "hqk,khd->qhd", weights, all_values, preferred_element_type=jnp.float32
        ).reshape(TOK_DEV, half_cols)
        row_total, row_square = lax.psum(
            (jnp.sum(attended, axis=1), jnp.sum(attended * attended, axis=1)), "ha"
        )
        row_mean = row_total / full_cols
        inverse_out = lax.rsqrt(row_square / full_cols - row_mean * row_mean + epsilon)[:, None]
        unit_out = (attended - row_mean[:, None]) * inverse_out
        mixed_in = (unit_out * ln_out_gain * gate_part).astype(jnp.bfloat16)
        partial_out = jnp.dot(mixed_in, w_final, preferred_element_type=jnp.float32)
        summed_out = lax.psum_scatter(partial_out, "ha", scatter_dimension=1, tiled=True)
        residual = lax.dynamic_slice_in_dim(x_in, out_start, out_cols, 1)
        mixed_parts.append((summed_out + bias_half + residual).astype(jnp.bfloat16))
        grad_final_part = jnp.einsum(
            "tc,td->cd", mixed_in, cot_rows, preferred_element_type=jnp.float32
        )
        grad_bias_out = grad_bias_out + jnp.sum(cot_rows.astype(jnp.float32), axis=0)
        grad_mixed = jnp.einsum("td,cd->tc", cot_rows, w_final, preferred_element_type=jnp.float32)
        grad_gate = grad_mixed * unit_out * ln_out_gain
        grad_gain_out = grad_gain_out + jnp.sum(grad_mixed * unit_out * gate_part, axis=0)
        grad_unit = grad_mixed * gate_part * ln_out_gain
        first_total, second_total = lax.psum(
            (jnp.sum(grad_unit, axis=1), jnp.sum(grad_unit * unit_out, axis=1)), "ha"
        )
        grad_attended = (
            inverse_out
            * (
                grad_unit
                - first_total[:, None] / full_cols
                - unit_out * second_total[:, None] / full_cols
            )
        ).astype(jnp.bfloat16)
        grad_heads = grad_attended.reshape(TOK_DEV, heads, DH)
        grad_weights = jnp.einsum(
            "qhd,khd->hqk", grad_heads, all_values, preferred_element_type=jnp.float32
        )
        grad_scores = score_grads(grad_weights, scores, allowed, query_count)
        grad_rel = grad_rel + diagonal_sums(grad_scores, query_pos[0], places[0], rel_bias.shape[1])
        grad_time = grad_time + jnp.einsum(
            "hqk,qkb->hb", grad_scores, bucket_hot, preferred_element_type=jnp.float32
        )
        grad_queries = (
            jnp.einsum("hqk,khd->qhd", grad_scores, all_keys, preferred_element_type=jnp.float32)
            * scale
        ).reshape(TOK_DEV, half_cols)
        key_part = (
            jnp.einsum("hqk,qhd->khd", grad_scores, query_heads, preferred_element_type=jnp.float32)
            * scale
        )
        value_part = jnp.einsum(
            "hqk,qhd->khd", weights, grad_heads, preferred_element_type=jnp.float32
        )
        stacked = jnp.stack(
            [key_part.reshape(group, half_cols), value_part.reshape(group, half_cols)]
        )
        owned_grads = lax.psum_scatter(stacked, "ka", scatter_dimension=1, tiled=True)
        grad_keys = owned_grads[0]
        grad_values = owned_grads[1]
        grad_act = jnp.stack([grad_gate, grad_values, grad_queries, grad_keys], axis=1)
        grad_pre = (grad_act * silu_slope(pre_act)).astype(jnp.bfloat16)
        grad_proj_part = jnp.einsum(
            "td,tgc->dgc", normed, grad_pre, preferred_element_type=jnp.float32
        )
        grad_bias_proj = grad_bias_proj + jnp.sum(grad_pre.astype(jnp.float32), axis=0)
        grad_normed = lax.psum(
            jnp.einsum("tgc,dgc->td", grad_pre, w_full, preferred_element_type=jnp.float32), "ha"
        )
        grad_gain_in = grad_gain_in + jnp.sum(grad_normed * unit_in, axis=0)
        grad_parts.append(
            cot_rows.astype(jnp.float32) + norm_back(grad_normed * ln_in_gain, unit_in, inverse_in)
        )
        local_pair = (grad_proj_part, grad_final_part)
        local_pair = (
            lax.psum_scatter(local_pair[0], ("pb", "ka"), scatter_dimension=0, tiled=True),
            lax.psum_scatter(local_pair[1], ("pb", "ka"), scatter_dimension=1, tiled=True),
        )
        weight_total = (
            local_pair if weight_total is None else jax.tree.map(jnp.add, weight_total, local_pair)
        )
    grad_start = jnp.concatenate(grad_parts, axis=0)
    outgoing = jnp.zeros((owners * capacity, width), jnp.float32).at[slot_index].set(grad_start)
    incoming = lax.all_to_all(
        outgoing.reshape(owners, capacity, width),
        ("pb", "ka"),
        split_axis=0,
        concat_axis=0,
        tiled=True,
    ).reshape(owners * capacity, width)
    table_grad = jax.ops.segment_sum(
        jnp.where(present[:, None], incoming, 0.0), local_rows, num_segments=table.shape[0]
    )
    small_total = lax.psum(
        (grad_gain_in, grad_bias_proj, grad_rel, grad_time, grad_gain_out, grad_bias_out),
        ("pb", "ka"),
    )
    mixed = jnp.concatenate(mixed_parts, axis=0)
    return (
        mixed,
        grad_start.astype(jnp.bfloat16),
        table_grad,
        small_total[0],
        weight_total[0],
        small_total[1],
        small_total[2],
        small_total[3],
        small_total[4],
        weight_total[1],
        small_total[5],
    )


def solution(mesh):
    return jax.shard_map(
        local,
        mesh=mesh,
        in_specs=(
            P(("pb", "ka"), None),
            P(("pb", "ka"), None),
            P(("pb", "ka")),
            P("pb", None, None),
            P("pb", None, None),
            P(("pb", "ka"), None),
            P(("pb", "ka"), None),
            P(),
            P("pb", None, "ha"),
            P(None, "ha"),
            P("ha", None),
            P("ha", None),
            P("ha"),
            P("ha", "pb"),
            P(),
        ),
        out_specs=(
            P(("pb", "ka"), "ha"),
            P(("pb", "ka"), None),
            P(("pb", "ka"), None),
            P(),
            P(("pb", "ka"), None, "ha"),
            P(None, "ha"),
            P("ha", None),
            P("ha", None),
            P("ha"),
            P("ha", ("pb", "ka")),
            P(),
        ),
        check_vma=False,
    )
```

profile of v0, /device:TPU:0, one launch (start us, length us, event | category | flops | bytes accessed | tf_op | source)
XLA Modules:
  0.0 587.4 jit_solution(8028452712634609710)
XLA Ops:
  11.4 2.4 scatter_custom_fusion
  14.5 7.4 %all-to-all-start = ((s32[16,1,64]{2,1,0:T(1,128)}), s32[16,1,64]{2,1,0:T(1,128)S(1)}, u32[]{:S(2)}, u32[]{:S(2)}) async-start(s32[16,1,64]{2,1,0:T(1,128)} %all_to_all.12), calls=%async_computation | async-start | bytes 16384 | tf_op jit(solution)/shard_map/all_to_all | solution.py:147
  30.9 15.3 %all_gather.26 = bf16[256,512]{0,1:T(8,128)(2,1)S(1)} all-gather(bf16[256,64]{0,1:T(8,128)(2,1)} %param.28), channel_id=1, replica_groups=mesh['pb'=8,'ka'=2,'ha'=2] {'pb'}, dimensions={1}, use_global_device_ids=true | all-gather | bytes 294912 | tf_op jit(solution)/shard_map/all_gather | solution.py:183
  46.2 5.6 iota_compare_fusion.2
  51.9 9.4 %fusion.4 = f32[3,4,128,256]{3,1,2,0:T(4,128)S(1)} fusion(pred[128,256,128]{2,0,1:T(32,128)(4,1)S(1)} %iota_compare_fusion.2, bf16[1,4,128]{2,1,0:T(4,128)(2,1)S(1)} %get-tuple-element.228, bf16[1,4,128]{2,1,0:T(4,128)(2,1)S(1)} %get-tuple-element.229, bf16[1,4,128]{2,1,0:T(4,128)(2,1)S(1)} %get-tuple-element.227), kind=kOutput, calls=%fused_computation.13 | convolution fusion | flops 100672512 | bytes 5770240 | tf_op jit(solution)/shard_map/phb,qkb->phqk/dot_general | solution.py:77
  62.6 5.8 iota_compare_fusion
  68.5 10.7 %fusion = f32[3,4,128,256]{3,1,2,0:T(4,128)} fusion(pred[128,256,128]{2,0,1:T(32,128)(4,1)S(1)} %iota_compare_fusion, bf16[1,4,128]{2,1,0:T(4,128)(2,1)S(1)} %get-tuple-element.228, bf16[1,4,128]{2,1,0:T(4,128)(2,1)S(1)} %get-tuple-element.229, bf16[1,4,128]{2,1,0:T(4,128)(2,1)S(1)} %get-tuple-element.227), kind=kOutput, calls=%fused_computation.9 | convolution fusion | flops 100672512 | bytes 5770240 | tf_op jit(solution)/shard_map/phb,qkb->phqk/dot_general | solution.py:77
  79.2 6.1 %iota_compare_fusion.1 = pred[128,256,128]{2,0,1:T(32,128)(4,1)S(1)} fusion(s32[128,256]{0,1:T(8,128)S(1)} %copy.320), kind=kLoop, calls=%fused_computation.6 | loop fusion | flops 4194304 | bytes 4325376 | tf_op jit(solution)/shard_map/eq | solution.py:92
  85.3 10.6 %fusion.2 = f32[3,4,128,256]{3,1,2,0:T(4,128)} fusion(pred[128,256,128]{2,0,1:T(32,128)(4,1)S(1)} %iota_compare_fusion.1, bf16[1,4,128]{2,1,0:T(4,128)(2,1)S(1)} %get-tuple-element.228, bf16[1,4,128]{2,1,0:T(4,128)(2,1)S(1)} %get-tuple-element.229, bf16[1,4,128]{2,1,0:T(4,128)(2,1)S(1)} %get-tuple-element.227), kind=kOutput, calls=%fused_computation.11 | convolution fusion | flops 100672512 | bytes 5770240 | tf_op jit(solution)/shard_map/phb,qkb->phqk/dot_general | solution.py:77
  101.1 8.6 %gather_fusion = bf16[1024,512]{1,0:T(8,128)(2,1)S(1)} fusion(bf16[8192,512]{1,0:T(8,128)(2,1)} %param.20, s32[1024]{0:T(1024)S(1)} %broadcast_clamp_fusion), kind=kCustom, calls=%fused_computation | custom fusion | bytes 2101248 | tf_op jit(solution)/shard_map/gather | solution.py:152
  110.9 6.2 %all-to-all-start.1 = ((bf16[16,64,512]{2,1,0:T(8,128)(2,1)}), bf16[16,64,512]{2,1,0:T(8,128)(2,1)S(1)}, u32[]{:S(2)}, u32[]{:S(2)}) async-start(bf16[16,64,512]{2,1,0:T(8,128)(2,1)} %broadcast_select_fusion), calls=%async_computation.1 | async-start | bytes 2097152 | tf_op jit(solution)/shard_map/all_to_all | solution.py:153
  117.2 2.6 fusion.127
  119.8 2.6 fusion.128
  122.3 6.4 %iota_compare_fusion.3 = pred[128,256,128]{2,0,1:T(32,128)(4,1)} fusion(s32[128,256]{0,1:T(8,128)S(1)} %copy.302), kind=kLoop, calls=%fused_computation.8 | loop fusion | flops 4194304 | bytes 4325376 | tf_op jit(solution)/shard_map/eq | solution.py:92
  128.8 12.0 %all-to-all-done.1 = bf16[16,64,512]{2,1,0:T(8,128)(2,1)S(1)} async-done(((bf16[16,64,512]{2,1,0:T(8,128)(2,1)}), bf16[16,64,512]{2,1,0:T(8,128)(2,1)S(1)}, u32[]{:S(2)}, u32[]{:S(2)}) %all-to-all-start.1) | async-done | bytes 1048608 | tf_op jit(solution)/shard_map/all_to_all | solution.py:153
  140.8 2.0 gather_fusion.1
  143.3 2.6 fusion.123
  146.0 6.8 %all_gather.28 = bf16[2,256,256]{2,1,0:T(8,128)(2,1)S(1)} all-gather(bf16[2,128,256]{2,1,0:T(8,128)(2,1)S(1)} %pad_maximum_fusion.9), channel_id=1, replica_groups=mesh['pb'=8,'ka'=2,'ha'=2] {'ka'}, dimensions={1}, use_global_device_ids=true | all-gather | bytes 393216 | tf_op jit(solution)/shard_map/all_gather | solution.py:203
  153.1 3.0 divide_convert_fusion.1
  156.5 4.9 all-reduce.14
  161.4 2.3 multiply_reduce_fusion.17
  163.7 4.9 all-reduce.13
  172.4 10.6 %fusion.6 = f32[3,4,128,256]{3,1,2,0:T(4,128)S(1)} fusion(pred[128,256,128]{2,0,1:T(32,128)(4,1)} %iota_compare_fusion.3, bf16[1,4,128]{2,1,0:T(4,128)(2,1)S(1)} %get-tuple-element.228, bf16[1,4,128]{2,1,0:T(4,128)(2,1)S(1)} %get-tuple-element.229, bf16[1,4,128]{2,1,0:T(4,128)(2,1)S(1)} %get-tuple-element.227), kind=kOutput, calls=%fused_computation.15 | convolution fusion | flops 100672512 | bytes 5770240 | tf_op jit(solution)/shard_map/phb,qkb->phqk/dot_general | solution.py:77
  184.6 2.9 reduce-scatter.23.cloned.1.call-done
  199.9 15.7 %all-reduce.19.cloned.1.call-done = f32[128,512]{1,0:T(8,128)} async-done(((f32[128,512]{1,0:T(8,128)}), f32[128,512]{1,0:T(8,128)}) %all-reduce.19.cloned.1.call-update) | async-done | bytes 262160 | tf_op jit(solution)/shard_map/psum | solution.py:280
  218.8 2.0 fusion.121
  221.6 6.0 %all_gather.29 = bf16[2,256,256]{2,1,0:T(8,128)(2,1)S(1)} all-gather(bf16[2,128,256]{2,1,0:T(8,128)(2,1)S(1)} %pad_maximum_fusion.10), channel_id=1, replica_groups=mesh['pb'=8,'ka'=2,'ha'=2] {'ka'}, dimensions={1}, use_global_device_ids=true | all-gather | bytes 393216 | tf_op jit(solution)/shard_map/all_gather | solution.py:203
  227.9 3.1 divide_convert_fusion
  233.1 2.0 fusion.119
  235.9 5.6 all_gather.27
  243.4 3.1 divide_convert_fusion.2
  248.7 2.1 fusion.117
  253.0 5.6 all_gather.25
  262.1 3.1 divide_convert_fusion.3
  268.3 5.7 all-reduce.12
  276.0 2.4 multiply_reduce_fusion.16
  278.5 2.7 multiply_reduce_fusion.19
  281.1 5.7 all-reduce.11
  327.5 1.9 pad_maximum_fusion.5
  331.3 1.9 convolution_multiply_fusion.10
  342.7 2.7 convert_reduce_fusion.3
  345.4 2.6 convert_reduce_fusion.2
  348.0 9.5 %reduce-scatter.25.cloned.1.call-done = f32[2,128,256]{2,1,0:T(8,128)} async-done(((f32[2,256,256]{2,1,0:T(8,128)}), f32[2,128,256]{2,1,0:T(8,128)}) %reduce-scatter.25.cloned.1.call-update) | async-done | bytes 262160 | tf_op jit(solution)/shard_map/reduce_scatter | solution.py:271
  361.7 2.1 convolution_bitcast_fusion.2
  365.0 2.1 pad_convert_fusion.1
  371.2 2.8 fusion.96
  375.2 2.7 reshape.907
  379.4 2.1 pad_convert_fusion
  381.5 2.1 pad_convert_fusion.2
  386.4 2.1 pad_convert_fusion.3
  392.8 3.7 add_add_fusion
  396.5 3.4 all-reduce.21.cloned.1.call-done
  399.9 2.1 multiply_reduce_fusion
  404.0 2.3 convert_add_fusion.4
  406.3 4.0 scatter_custom_fusion.1
  410.3 5.6 all-to-all-start.2
  427.3 5.6 convolution_bitcast_fusion.7
  432.9 4.6 fusion.36
  437.6 4.8 fusion.35
  442.5 4.6 fusion.34
  447.3 64.7 %all-reduce.10 = (f32[512]{0:T(512)}, f32[4,256]{1,0:T(4,128)}, f32[4,256]{1,0:T(4,128)}, f32[4,128]{1,0:T(4,128)}, f32[256]{0:T(256)}, /*index=5*/f32[512]{0:T(512)}) all-reduce(f32[512]{0:T(512)S(1)} %add_add_fusion.3, f32[4,256]{1,0:T(4,128)S(1)} %add_add_fusion.1, ...), channel_id=1, replica_groups=mesh['pb'=8,'ka'=2,'ha'=2] {'pb','ka'}, use_global_device_ids=true, to_apply=%region_82.83 | all-reduce | flops 3840 | bytes 30720 | tf_op jit(solution)/shard_map/psum | solution.py:307
  515.0 6.2 %reduce-scatter.27.cloned.1.call-done = f32[32,4,256]{2,0,1:T(8,128)} async-done(((f32[512,4,256]{2,0,1:T(8,128)}), f32[32,4,256]{2,0,1:T(8,128)}) %reduce-scatter.27.cloned.1.call-update) | async-done | bytes 131088 | tf_op jit(solution)/shard_map/reduce_scatter | solution.py:289
  524.4 14.9 %scatter_custom_fusion.2 = f32[8192,512]{1,0:T(8,128)} fusion(s32[1024]{0:T(1024)} %copy-done.65, f32[1024,512]{1,0:T(8,128)} %bitcast_select_fusion, f32[]{:T(128)} %constant.114.clone.1), kind=kCustom, calls=%fused_computation.21 | custom fusion | flops 524288 | bytes 16777728 | tf_op jit(solution)/shard_map/scatter-add | solution.py:304
  539.4 41.1 %reduce-scatter.29.cloned.1.call-done = f32[256,32]{0,1:T(8,128)} async-done(((f32[256,512]{0,1:T(8,128)}), f32[256,32]{0,1:T(8,128)}) %reduce-scatter.29.cloned.1.call-update) | async-done | bytes 32784 | tf_op jit(solution)/shard_map/reduce_scatter | solution.py:290
  (481 shorter events, 151.7 us)
Async XLA Ops:
  11.4 105.7 %copy-start.75 = (s32[512,1]{0,1:T(1,128)}, s32[512,1]{0,1:T(1,128)S(1)}, u32[]{:S(2)}) copy-start(s32[512,1]{0,1:T(1,128)S(1)} %compare_select_fusion) | copy-start | bytes 6148
  14.5 86.4 %all-to-all-start = ((s32[16,1,64]{2,1,0:T(1,128)}), s32[16,1,64]{2,1,0:T(1,128)S(1)}, u32[]{:S(2)}, u32[]{:S(2)}) async-start(s32[16,1,64]{2,1,0:T(1,128)} %all_to_all.12), calls=%async_computation | async-start | bytes 16384 | tf_op jit(solution)/shard_map/all_to_all | solution.py:147
  21.9 121.4 %all-gather.2.cloned.1.call-start = ((), (), s32[]{:S(2)}) async-start(), calls=%async_computation.13 | async-start | bytes 1179648 | tf_op jit(solution)/shard_map/all_gather | solution.py:182
  30.4 48.7 %copy-start.34 = (s32[128,256]{0,1:T(8,128)}, s32[128,256]{0,1:T(8,128)S(1)}, u32[]{:S(2)}) copy-start(s32[128,256]{0,1:T(8,128)S(1)} %copy.320) | copy-start | bytes 393220
  30.6 32.0 %copy-start.36 = (s32[128,256]{0,1:T(8,128)}, s32[128,256]{0,1:T(8,128)S(1)}, u32[]{:S(2)}) copy-start(s32[128,256]{0,1:T(8,128)S(1)} %copy.329) | copy-start | bytes 393220
  30.9 30.5 %copy-start.38 = (s32[128,256]{0,1:T(8,128)}, s32[128,256]{0,1:T(8,128)S(1)}, u32[]{:S(2)}) copy-start(s32[128,256]{0,1:T(8,128)S(1)} %copy.311) | copy-start | bytes 393220
  85.3 10.8 %copy-start.1 = (bf16[512,512]{1,0:T(8,128)(2,1)S(1)}, bf16[512,512]{1,0:T(8,128)(2,1)}, u32[]{:S(2)}) copy-start(bf16[512,512]{1,0:T(8,128)(2,1)} %param.21) | copy-start | bytes 1572868
  98.6 23.8 %copy-start.40 = (s32[128,256]{0,1:T(8,128)}, s32[128,256]{0,1:T(8,128)S(1)}, u32[]{:S(2)}) copy-start(s32[128,256]{0,1:T(8,128)S(1)} %copy.302) | copy-start | bytes 393220
  110.9 29.9 %all-to-all-start.1 = ((bf16[16,64,512]{2,1,0:T(8,128)(2,1)}), bf16[16,64,512]{2,1,0:T(8,128)(2,1)S(1)}, u32[]{:S(2)}, u32[]{:S(2)}) async-start(bf16[16,64,512]{2,1,0:T(8,128)(2,1)} %broadcast_select_fusion), calls=%async_computation.1 | async-start | bytes 2097152 | tf_op jit(solution)/shard_map/all_to_all | solution.py:153
  117.1 70.5 %reduce-scatter.23.cloned.1.call-start = ((), (), s32[]{:S(2)}) async-start(), calls=%async_computation.20 | async-start | bytes 786432 | tf_op jit(solution)/shard_map/reduce_scatter | solution.py:271
  122.3 20.4 %copy-start.49 = (bf16[512,512]{1,0:T(8,128)(2,1)S(1)}, bf16[512,512]{1,0:T(8,128)(2,1)}, u32[]{:S(2)}) copy-start(bf16[512,512]{1,0:T(8,128)(2,1)} %param.15) | copy-start | bytes 1572868
  128.8 14.5 %copy-start.58 = (f32[512]{0:T(512)S(1)}, f32[512]{0:T(512)}, u32[]{:S(2)}) copy-start(f32[512]{0:T(512)} %param.22) | copy-start | bytes 6148
  128.8 14.5 %copy-start.105 = (f32[4,256]{1,0:T(4,128)S(1)}, f32[4,256]{1,0:T(4,128)}, u32[]{:S(2)}) copy-start(f32[4,256]{1,0:T(4,128)} %param.24) | copy-start | bytes 12292
  143.1 13.0 %copy-start.76 = (f32[128]{0:T(128)}, f32[128]{0:T(128)S(1)}, u32[]{:S(2)}) copy-start(f32[128]{0:T(128)S(1)} %broadcast_multiply_fusion.15) | copy-start | bytes 1540
  143.3 12.8 %copy-start.88 = (f32[128]{0:T(128)}, f32[128]{0:T(128)S(1)}, u32[]{:S(2)}) copy-start(f32[128]{0:T(128)S(1)} %add_rsqrt_fusion.3) | copy-start | bytes 1540
  145.9 15.5 %copy-start.66 = (f32[256]{0:T(256)S(1)}, f32[256]{0:T(256)}, u32[]{:S(2)}) copy-start(f32[256]{0:T(256)} %param.27) | copy-start | bytes 3076
  171.8 43.8 %all-reduce.19.cloned.1.call-start = ((), (), s32[]{:S(2)}) async-start(), calls=%async_computation.21 | async-start | bytes 524288 | tf_op jit(solution)/shard_map/psum | solution.py:280
  192.3 147.7 %reduce-scatter.19.cloned.1.call-start = ((), (), s32[]{:S(2)}) async-start(), calls=%async_computation.18 | async-start | bytes 786432 | tf_op jit(solution)/shard_map/reduce_scatter | solution.py:271
  217.4 15.7 %copy-start.78 = (f32[128]{0:T(128)}, f32[128]{0:T(128)S(1)}, u32[]{:S(2)}) copy-start(f32[128]{0:T(128)S(1)} %broadcast_multiply_fusion.17) | copy-start | bytes 1540
  235.2 13.5 %copy-start.91 = (f32[128]{0:T(128)S(1)}, f32[128]{0:T(128)}, u32[]{:S(2)}) copy-start(f32[128]{0:T(128)} %add_rsqrt_fusion.7) | copy-start | bytes 1540
  251.4 16.9 %copy-start.100 = (f32[128]{0:T(128)S(1)}, f32[128]{0:T(128)}, u32[]{:S(2)}) copy-start(f32[128]{0:T(128)} %get-tuple-element.260) | copy-start | bytes 1540
  290.1 10.0 %copy-start.52 = (bf16[128,256]{0,1:T(8,128)(2,1)}, bf16[128,256]{0,1:T(8,128)(2,1)S(1)}, u32[]{:S(2)}) copy-start(bf16[128,256]{0,1:T(8,128)(2,1)S(1)} %copy.347) | copy-start | bytes 196612
  308.8 32.9 %reduce-scatter.21.cloned.1.call-start = ((), (), s32[]{:S(2)}) async-start(), calls=%async_computation.19 | async-start | bytes 786432 | tf_op jit(solution)/shard_map/reduce_scatter | solution.py:271
  322.6 34.9 %reduce-scatter.25.cloned.1.call-start = ((), (), s32[]{:S(2)}) async-start(), calls=%async_computation.22 | async-start | bytes 786432 | tf_op jit(solution)/shard_map/reduce_scatter | solution.py:271
  327.5 31.1 %copy-start.33 = (f32[128,1,256]{2,0,1:T(8,128)S(1)}, f32[128,1,256]{2,0,1:T(8,128)}, u32[]{:S(2)}) copy-start(f32[128,1,256]{2,0,1:T(8,128)} %get-tuple-element.186) | copy-start | bytes 393220
  333.2 66.7 %all-reduce.21.cloned.1.call-start = ((), (), s32[]{:S(2)}) async-start(), calls=%async_computation.25 | async-start | bytes 1572864 | tf_op jit(solution)/shard_map/psum | solution.py:280
  360.5 10.6 %copy-start.77 = (f32[128]{0:T(128)S(1)}, f32[128]{0:T(128)}, u32[]{:S(2)}) copy-start(f32[128]{0:T(128)} %copy-done.76) | copy-start | bytes 1540
  360.5 10.6 %copy-start.89 = (f32[128]{0:T(128)S(1)}, f32[128]{0:T(128)}, u32[]{:S(2)}) copy-start(f32[128]{0:T(128)} %copy-done.88) | copy-start | bytes 1540
  365.0 10.0 %copy-start.5 = (bf16[4,128,256]{2,1,0:T(8,128)(2,1)S(1)}, bf16[4,128,256]{2,1,0:T(8,128)(2,1)}, u32[]{:S(2)}) copy-start(bf16[4,128,256]{2,1,0:T(8,128)(2,1)} %copy-done.4) | copy-start | bytes 786436
  365.0 147.0 %reduce-scatter.15.cloned.1.call-start = ((), (), s32[]{:S(2)}) async-start(), calls=%async_computation.16 | async-start | bytes 393216 | tf_op jit(solution)/shard_map/reduce_scatter | solution.py:226
  370.5 141.5 %reduce-scatter.11.cloned.1.call-start = ((), (), s32[]{:S(2)}) async-start(), calls=%async_computation.14 | async-start | bytes 393216 | tf_op jit(solution)/shard_map/reduce_scatter | solution.py:226
  371.2 14.2 %copy-start.28 = (bf16[128,256]{1,0:T(8,128)(2,1)S(1)}, bf16[128,256]{1,0:T(8,128)(2,1)}, u32[]{:S(2)}) copy-start(bf16[128,256]{1,0:T(8,128)(2,1)} %get-tuple-element.177) | copy-start | bytes 196612
  375.0 13.5 %copy-start.31 = (bf16[128,256]{1,0:T(8,128)(2,1)S(1)}, bf16[128,256]{1,0:T(8,128)(2,1)}, u32[]{:S(2)}) copy-start(bf16[128,256]{1,0:T(8,128)(2,1)} %get-tuple-element.179) | copy-start | bytes 196612
  375.2 14.3 %copy-start.102 = (f32[128]{0:T(128)S(1)}, f32[128]{0:T(128)}, u32[]{:S(2)}) copy-start(f32[128]{0:T(128)} %get-tuple-element.71) | copy-start | bytes 1540
  375.2 14.8 %copy-start.101 = (f32[128]{0:T(128)S(1)}, f32[128]{0:T(128)}, u32[]{:S(2)}) copy-start(f32[128]{0:T(128)} %get-tuple-element.88) | copy-start | bytes 1540
  375.2 15.3 %copy-start.26 = (bf16[128,256]{1,0:T(8,128)(2,1)S(1)}, bf16[128,256]{1,0:T(8,128)(2,1)}, u32[]{:S(2)}) copy-start(bf16[128,256]{1,0:T(8,128)(2,1)} %get-tuple-element.231) | copy-start | bytes 196612
  377.9 13.7 %copy-start.17 = (bf16[128,4,256]{2,0,1:T(8,128)(2,1)S(1)}, bf16[128,4,256]{2,0,1:T(8,128)(2,1)}, u32[]{:S(2)}) copy-start(bf16[128,4,256]{2,0,1:T(8,128)(2,1)} %get-tuple-element.132) | copy-start | bytes 786436
  377.9 13.7 %copy-start.92 = (f32[128]{0:T(128)S(1)}, f32[128]{0:T(128)}, u32[]{:S(2)}) copy-start(f32[128]{0:T(128)} %add_rsqrt_fusion.7) | copy-start | bytes 1540
  386.3 125.7 %reduce-scatter.17.cloned.1.call-start = ((), (), s32[]{:S(2)}) async-start(), calls=%async_computation.17 | async-start | bytes 393216 | tf_op jit(solution)/shard_map/reduce_scatter | solution.py:226
  389.5 122.6 %reduce-scatter.13.cloned.1.call-start = ((), (), s32[]{:S(2)}) async-start(), calls=%async_computation.15 | async-start | bytes 393216 | tf_op jit(solution)/shard_map/reduce_scatter | solution.py:226
  391.5 129.7 %reduce-scatter.27.cloned.1.call-start = ((), (), s32[]{:S(2)}) async-start(), calls=%async_computation.23 | async-start | bytes 2228224 | tf_op jit(solution)/shard_map/reduce_scatter | solution.py:289
  406.3 12.7 %copy-start.6 = (bf16[4,128,256]{2,1,0:T(8,128)(2,1)S(1)}, bf16[4,128,256]{2,1,0:T(8,128)(2,1)}, u32[]{:S(2)}) copy-start(bf16[4,128,256]{2,1,0:T(8,128)(2,1)} %copy-done.4) | copy-start | bytes 786436
  410.3 112.5 %all-to-all-start.2 = ((f32[16,64,512]{2,1,0:T(8,128)}), f32[16,64,512]{2,1,0:T(8,128)S(1)}, u32[]{:S(2)}, u32[]{:S(2)}) async-start(f32[16,64,512]{2,1,0:T(8,128)} %bitcast.426), calls=%async_computation.10 | async-start | bytes 4194304 | tf_op jit(solution)/shard_map/all_to_all | solution.py:297
  416.0 164.5 %reduce-scatter.29.cloned.1.call-start = ((), (), s32[]{:S(2)}) async-start(), calls=%async_computation.24 | async-start | bytes 557056 | tf_op jit(solution)/shard_map/reduce_scatter | solution.py:290
  417.2 10.0 %copy-start.60 = (f32[4,512]{1,0:T(4,128)S(1)}, f32[4,512]{1,0:T(4,128)}, u32[]{:S(2)}) copy-start(f32[4,512]{1,0:T(4,128)} %copy-done.59) | copy-start | bytes 24580
  427.2 10.2 %copy-start.35 = (s32[128,256]{0,1:T(8,128)S(1)}, s32[128,256]{0,1:T(8,128)}, u32[]{:S(2)}) copy-start(s32[128,256]{0,1:T(8,128)} %copy-done.34) | copy-start | bytes 393220
  427.2 10.2 %copy-start.55 = (bf16[4,128,256]{1,0,2:T(4,128)(2,1)S(1)}, bf16[4,128,256]{1,0,2:T(4,128)(2,1)}, u32[]{:S(2)}) copy-start(bf16[4,128,256]{1,0,2:T(4,128)(2,1)} %copy.357) | copy-start | bytes 786436
  437.5 9.6 %copy-start.61 = (f32[4,256]{1,0:T(4,128)S(1)}, f32[4,256]{1,0:T(4,128)}, u32[]{:S(2)}) copy-start(f32[4,256]{1,0:T(4,128)} %get-tuple-element.133) | copy-start | bytes 12292
  437.5 9.6 %copy-start.62 = (f32[4,256]{1,0:T(4,128)S(1)}, f32[4,256]{1,0:T(4,128)}, u32[]{:S(2)}) copy-start(f32[4,256]{1,0:T(4,128)} %get-tuple-element.131) | copy-start | bytes 12292
  437.5 9.6 %copy-start.67 = (f32[512]{0:T(512)S(1)}, f32[512]{0:T(512)}, u32[]{:S(2)}) copy-start(f32[512]{0:T(512)} %get-tuple-element.70) | copy-start | bytes 6148
  437.5 9.6 %copy-start.68 = (f32[512]{0:T(512)S(1)}, f32[512]{0:T(512)}, u32[]{:S(2)}) copy-start(f32[512]{0:T(512)} %get-tuple-element.72) | copy-start | bytes 6148
  437.5 9.6 %copy-start.69 = (f32[512]{0:T(512)S(1)}, f32[512]{0:T(512)}, u32[]{:S(2)}) copy-start(f32[512]{0:T(512)} %get-tuple-element.75) | copy-start | bytes 6148
  437.6 9.6 %copy-start.70 = (f32[512]{0:T(512)S(1)}, f32[512]{0:T(512)}, u32[]{:S(2)}) copy-start(f32[512]{0:T(512)} %get-tuple-element.77) | copy-start | bytes 6148
  437.6 9.7 %copy-start.71 = (f32[512]{0:T(512)S(1)}, f32[512]{0:T(512)}, u32[]{:S(2)}) copy-start(f32[512]{0:T(512)} %get-tuple-element.84) | copy-start | bytes 6148
  437.6 9.7 %copy-start.72 = (f32[512]{0:T(512)S(1)}, f32[512]{0:T(512)}, u32[]{:S(2)}) copy-start(f32[512]{0:T(512)} %get-tuple-element.85) | copy-start | bytes 6148
  437.6 9.7 %copy-start.73 = (f32[512]{0:T(512)S(1)}, f32[512]{0:T(512)}, u32[]{:S(2)}) copy-start(f32[512]{0:T(512)} %get-tuple-element.86) | copy-start | bytes 6148
  437.6 9.7 %copy-start.74 = (f32[512]{0:T(512)S(1)}, f32[512]{0:T(512)}, u32[]{:S(2)}) copy-start(f32[512]{0:T(512)} %get-tuple-element.87) | copy-start | bytes 6148
  437.6 74.4 %copy-start.27 = (f32[128,512]{1,0:T(8,128)S(1)}, f32[128,512]{1,0:T(8,128)}, u32[]{:S(2)}) copy-start(f32[128,512]{1,0:T(8,128)} %get-tuple-element.173) | copy-start | bytes 786436
  437.6 74.4 %copy-start.99 = (f32[256]{0:T(256)S(1)}, f32[256]{0:T(256)}, u32[]{:S(2)}) copy-start(f32[256]{0:T(256)} %dynamic_slice.68) | copy-start | bytes 3076
  442.5 71.7 %copy-start.8 = (f32[128,512]{1,0:T(8,128)S(1)}, f32[128,512]{1,0:T(8,128)}, u32[]{:S(2)}) copy-start(f32[128,512]{1,0:T(8,128)} %copy-done.7) | copy-start | bytes 786436
  442.5 71.6 %copy-start.10 = (f32[128,512]{1,0:T(8,128)S(1)}, f32[128,512]{1,0:T(8,128)}, u32[]{:S(2)}) copy-start(f32[128,512]{1,0:T(8,128)} %copy-done.9) | copy-start | bytes 786436
  442.5 71.6 %copy-start.12 = (f32[128,512]{1,0:T(8,128)S(1)}, f32[128,512]{1,0:T(8,128)}, u32[]{:S(2)}) copy-start(f32[128,512]{1,0:T(8,128)} %copy-done.11) | copy-start | bytes 786436
  442.5 71.6 %copy-start.14 = (f32[128,512]{1,0:T(8,128)S(1)}, f32[128,512]{1,0:T(8,128)}, u32[]{:S(2)}) copy-start(f32[128,512]{1,0:T(8,128)} %copy-done.13) | copy-start | bytes 786436
  442.5 80.3 %copy-start.98 = (pred[1024]{0:T(1024)(128)(4,1)S(1)}, pred[1024]{0:T(1024)(128)(4,1)}, u32[]{:S(2)}) copy-start(pred[1024]{0:T(1024)(128)(4,1)} %gt.16) | copy-start | bytes 3076
  (59 other events, 335.2 us)
Sparse Core Ops, SparseCore 0:
  24.9 24.9 all-gather.1
  171.9 15.5 reduce-scatter.22
  192.4 23.1 all-reduce.18
  308.9 14.5 reduce-scatter.18
  325.7 14.5 reduce-scatter.20
  343.0 14.5 reduce-scatter.24
  365.1 34.7 all-reduce.20
  402.1 11.6 reduce-scatter.14
  416.1 11.6 reduce-scatter.10
  429.9 11.6 reduce-scatter.16
  443.9 11.6 reduce-scatter.12
  459.2 61.9 reduce-scatter.26
  525.7 54.6 reduce-scatter.28
where the time goes:
time: 593 us; the launch traced here: 587 us
  matrix products  132 us (22%)
  blocking collectives  125 us (21%)
  other arithmetic  112 us (19%)
  waiting for transfers between devices  91.2 us (15%)
  local copies, waits for them, and re-layouts  89.8 us (15%)
  starting transfers between devices  19.9 us (3%)
  between operations  16.6 us (3%)
    psum x1, blocking collectives, local(): lax.psum((grad_gain_in, grad_bias_proj, grad_rel, grad_time, grad_gain_ou...  64.7 us
    dot_general x4, matrix products, bucket_lookup(): jnp.einsum('phb,qkb->phqk', jnp.stack([high, middle, lowest]), bucket_hot...  41.4 us
    reduce_scatter x1, waiting for transfers between devices, local(): lax.psum_scatter(local_pair[1], ('pb', 'ka'), scatter_dimension=1, tiled=...  41.1 us
    all_gather x4, blocking collectives, local(): lax.all_gather(jnp.stack([key_rows, values]), 'ka', axis=1, tiled=True)  24.1 us
    eq x4, other arithmetic, tile_scores(): time_index[:, :, None]  24 us
    dot_general x4, matrix products, local(): jnp.einsum('hqk,qkb->hb', grad_scores, bucket_hot, preferred_element_type...  19.6 us
    psum x2, waiting for transfers between devices, local(): lax.psum(jnp.einsum('tgc,dgc->td', grad_pre, w_full, preferred_element_ty...  19.2 us
    all_gather x1, blocking collectives, local(): lax.all_gather(w_out, 'pb', axis=1, tiled=True)  15.3 us
  transfers between devices with their start and end apart: 16, of which 7 were waited for; matrix products, arithmetic and copies ran while one was open for 40% of the time, Pallas kernels for 0%

commit v1 on v0

--- a/solution.py
+++ b/solution.py
@@ -1,12 +1,18 @@
+import functools
+
 import jax
 import jax.numpy as jnp
 from jax import lax
+from jax.experimental import pallas as pl
+from jax.experimental.pallas import tpu as pltpu
 from jax.sharding import PartitionSpec as P
 
 DH = 64
 TOK_DEV = 128
 MB = 4
 SEQ_GRP = 4
+F32 = jnp.float32
+BF16 = jnp.bfloat16
 
 
 epsilon = 1e-05
@@ -116,7 +122,7 @@
     ).astype(jnp.bfloat16)
 
 
-def local(
+def local_general(
     context,
     item_owner,
     item_offset,
@@ -324,9 +330,428 @@
     )
 
 
+def mm(a, b):
+    return jnp.dot(a, b, preferred_element_type=F32)
+
+
+def mm_nt(a, b):
+    return lax.dot_general(a, b, (((1,), (1,)), ((), ())), preferred_element_type=F32)
+
+
+def mm_tn(a, b):
+    return lax.dot_general(a, b, (((0,), (0,)), ((), ())), preferred_element_type=F32)
+
+
+def sigmoid(v):
+    return 0.5 * jnp.tanh(0.5 * v) + 0.5
+
+
+def layer_kernel(
+    lengths_ref, times_ref, emb_ref, ctx_ref, cot_ref, w_ref, wout_ref, small_ref, gain_in_ref, bout_ref,
+    mixed_ref, grad_start_ref, grad_w_ref, grad_small_ref,
+    slope_ref, qkv_ref, w_att_ref, sm_ref, gs_ref, grad_pre_ref, att_ref,
+):
+    group, width = ctx_ref.shape
+    half = width // 2
+    lane = lax.broadcasted_iota(jnp.int32, (group, group), 1)
+    row = lax.broadcasted_iota(jnp.int32, (group, group), 0)
+    ends = []
+    total = jnp.int32(0)
+    for i in range(SEQ_GRP):
+        total = total + lengths_ref[i]
+        ends.append(total)
+    member_row = jnp.zeros((group, group), jnp.int32)
+    member_col = jnp.zeros((group, group), jnp.int32)
+    for i in range(SEQ_GRP):
+        member_row = member_row + (ends[i] <= row).astype(jnp.int32)
+        member_col = member_col + (ends[i] <= lane).astype(jnp.int32)
+    inv_count = jnp.zeros((group, group), F32)
+    for i in range(SEQ_GRP):
+        count = jnp.maximum(lengths_ref[i], 1).astype(F32)
+        inv_count = jnp.where(member_row == i, 1.0 / jnp.full((group, group), count, F32), inv_count)
+    allowed = (member_row == member_col) & (member_row < SEQ_GRP) & (lane <= row)
+    maskscale = jnp.where(allowed, inv_count, 0.0)
+    times_row = jnp.broadcast_to(times_ref[...], (group, group))
+    times_col = jnp.sum(jnp.where(lane == row, times_row, 0).astype(F32), axis=1, keepdims=True).astype(jnp.int32)
+    buckets = small_ref.shape[2] // 2
+    time_index = jnp.clip(times_col - times_row, 0, buckets - 1)
+    hot_cols = (times_row == row).astype(F32).astype(BF16)
+
+    start = ctx_ref[...].astype(F32) + jnp.concatenate(
+        [
+            emb_ref[0].astype(F32) + emb_ref[1].astype(F32),
+            emb_ref[2].astype(F32) + emb_ref[3].astype(F32),
+        ],
+        axis=0,
+    )
+    centered = start - jnp.mean(start, axis=1, keepdims=True)
+    inv_in = lax.rsqrt(jnp.mean(centered * centered, axis=1, keepdims=True) + epsilon)
+    unit_in = centered * inv_in
+    normed = (unit_in * gain_in_ref[...]).astype(BF16)
+
+    gates = []
+    for hf in range(2):
+        for g in range(4):
+            cols = slice(g * half, (g + 1) * half)
+            pre = mm(normed, w_ref[hf, :, cols]) + small_ref[hf, g : g + 1, :]
+            sig = sigmoid(pre)
+            act = pre * sig
+            slope_ref[hf, :, cols] = sig + act * (1.0 - sig)
+            if g == 0:
+                gates.append(act)
+            elif g == 2:
+                qkv_ref[hf, 1] = (act * 0.125).astype(BF16).astype(BF16)
+            else:
+                qkv_ref[hf, {1: 0, 3: 2}[g]] = act.astype(BF16)
+    gate = jnp.concatenate(gates, axis=1)
+
+    lane_pair = lax.broadcasted_iota(jnp.int32, (group, 128), 1)
+    low_half = lane_pair < 64
+
+    def split(tile):
+        zero = jnp.zeros_like(tile)
+        return jnp.where(low_half, tile, zero), jnp.where(low_half, zero, tile)
+
+    for hf in range(2):
+        for pair in range(half // 128):
+            cols = slice(pair * 128, (pair + 1) * 128)
+            values = split(qkv_ref[hf, 0, :, cols])
+            queries = split(qkv_ref[hf, 1, :, cols])
+            keys = qkv_ref[hf, 2, :, cols]
+            attended = None
+            for sub in range(2):
+                head_in = pair * 2 + sub
+                head = hf * (half // 64) + head_in
+                rel = pltpu.roll(
+                    jnp.broadcast_to(small_ref[hf, 4 + head_in : 5 + head_in, :], (group, group)),
+                    0, 1, stride=1, stride_axis=0,
+                )
+                table = small_ref[hf, 8 + head_in // 2 : 9 + head_in // 2, (head_in % 2) * buckets : (head_in % 2 + 1) * buckets]
+                table = jnp.broadcast_to(table, (group, buckets))
+                scores = mm_nt(queries[sub], keys) + rel + jnp.concatenate(
+                    [
+                        jnp.take_along_axis(table, time_index[:, c : c + buckets], axis=1, mode="promise_in_bounds")
+                        for c in range(0, group, buckets)
+                    ],
+                    axis=1,
+                )
+                sig = sigmoid(scores)
+                act = scores * sig
+                weights = (act * maskscale).astype(BF16)
+                w_att_ref[head] = weights
+                sm_ref[head] = (sig + act * (1.0 - sig)) * maskscale
+                part = mm(weights, values[sub])
+                attended = part if attended is None else attended + part
+            att_ref[:, hf * half + pair * 128 : hf * half + (pair + 1) * 128] = attended
+
+    attended = att_ref[...]
+    centered = attended - jnp.mean(attended, axis=1, keepdims=True)
+    inv_out = lax.rsqrt(jnp.mean(centered * centered, axis=1, keepdims=True) + epsilon)
+    unit_out = centered * inv_out
+    gain_out = jnp.concatenate([small_ref[0, 10:11, :], small_ref[1, 10:11, :]], axis=1)
+    mixed_in = (unit_out * gain_out * gate).astype(BF16)
+    mixed_ref[...] = (mm(mixed_in, wout_ref[...]) + bout_ref[...] + start).astype(BF16)
+    cot = cot_ref[...]
+    grad_mixed = mm_nt(cot, wout_ref[...])
+    for hf in range(2):
+        grad_w_ref[hf, :, 4 * half : 5 * half] = mm_tn(cot, mixed_in[:, hf * half : (hf + 1) * half]).astype(grad_w_ref.dtype)
+    grad_unit_raw = grad_mixed * unit_out
+    grad_gate = grad_unit_raw * gain_out
+    grad_gain_out = jnp.sum(grad_unit_raw * gate, axis=0, keepdims=True)
+    grad_unit = grad_mixed * gate * gain_out
+    first = jnp.mean(grad_unit, axis=1, keepdims=True)
+    second = jnp.mean(grad_unit * unit_out, axis=1, keepdims=True)
+    grad_att = (inv_out * (grad_unit - first - unit_out * second)).astype(BF16)
+    for hf in range(2):
+        cols = slice(hf * half, (hf + 1) * half)
+        grad_pre_ref[hf, :, 0:half] = (grad_gate[:, cols] * slope_ref[hf, :, 0:half]).astype(BF16)
+        grad_small_ref[hf, 10:11, :] = grad_gain_out[:, cols]
+
+    for hf in range(2):
+        for pair in range(half // 128):
+            cols = slice(pair * 128, (pair + 1) * 128)
+            values = qkv_ref[hf, 0, :, cols]
+            queries = split(qkv_ref[hf, 1, :, cols])
+            keys = split(qkv_ref[hf, 2, :, cols])
+            grads = split(grad_att[:, hf * half + pair * 128 : hf * half + (pair + 1) * 128])
+            sums = None
+            for sub in range(2):
+                head_in = pair * 2 + sub
+                head = hf * (half // 64) + head_in
+                grad_scores = (mm_nt(grads[sub], values) * sm_ref[head]).astype(BF16)
+                gs_ref[:, head * group : (head + 1) * group] = grad_scores
+                parts = (
+                    mm_tn(w_att_ref[head], grads[sub]),
+                    mm(grad_scores, keys[sub]),
+                    mm_tn(grad_scores, queries[sub]),
+                )
+                sums = parts if sums is None else [a + b for a, b in zip(sums, parts)]
+            for g, part in ((1, sums[0]), (2, sums[1] * 0.125), (3, sums[2])):
+                place = slice(g * half + pair * 128, g * half + (pair + 1) * 128)
+                grad_pre_ref[hf, :, place] = (part * slope_ref[hf, :, place]).astype(BF16)
+
+    flip = (lane + row == group - 1).astype(F32)
+    kept_pairs = lane + row <= group - 1
+    hot_back = (times_row == group - 1 - row).astype(F32).astype(BF16)
+    folded = mm(jnp.concatenate([flip.astype(BF16), hot_back], axis=0), gs_ref[...])
+    rel_rows = []
+    time_rows = []
+    early_rows = []
+    for head in range(2 * (half // 64)):
+        places = slice(head * group, (head + 1) * group)
+        rel_rows.append(jnp.sum(skew(folded[:group, places]), axis=0, keepdims=True))
+        both = mm_nt(folded[group:, places].astype(BF16), hot_cols)
+        kept = jnp.where(kept_pairs, both, 0.0)
+        time_rows.append(jnp.sum(skew(kept), axis=0, keepdims=True))
+        early_rows.append(jnp.sum(both - kept, axis=0, keepdims=True))
+    flipped = jnp.dot(jnp.concatenate(rel_rows + time_rows, axis=0), flip, preferred_element_type=F32, precision=lax.Precision.HIGHEST)
+    early = jnp.sum(jnp.concatenate(early_rows, axis=0), axis=1, keepdims=True)
+    heads = 2 * (half // 64)
+    first_lane = lax.broadcasted_iota(jnp.int32, (heads, buckets), 1) == 0
+    last_lane = lax.broadcasted_iota(jnp.int32, (heads, buckets), 1) == buckets - 1
+    times_flipped = flipped[heads:]
+    late = jnp.sum(times_flipped[:, buckets:], axis=1, keepdims=True)
+    time_grad = times_flipped[:, :buckets] + jnp.where(first_lane, early, 0.0) + jnp.where(last_lane, late, 0.0)
+    for hf in range(2):
+        for head_in in range(half // 64):
+            head = hf * (half // 64) + head_in
+            grad_small_ref[hf, 4 + head_in : 5 + head_in, :] = flipped[head : head + 1]
+            grad_small_ref[hf, 8 + head_in // 2 : 9 + head_in // 2, (head_in % 2) * buckets : (head_in % 2 + 1) * buckets] = time_grad[head : head + 1]
+
+    grad_normed = None
+    for hf in range(2):
+        grad_pre = grad_pre_ref[hf]
+        part = mm_nt(grad_pre, w_ref[hf])
+        grad_normed = part if grad_normed is None else grad_normed + part
+    grad_unit_in = grad_normed * gain_in_ref[...]
+    first = jnp.mean(grad_unit_in, axis=1, keepdims=True)
+    second = jnp.mean(grad_unit_in * unit_in, axis=1, keepdims=True)
+    cot32 = cot.astype(F32)
+    grad_start_ref[...] = (cot32 + inv_in * (grad_unit_in - first - unit_in * second)).astype(BF16)
+    gain_grad = jnp.sum(grad_normed * unit_in, axis=0, keepdims=True)
+    bout_grad = jnp.sum(cot32, axis=0, keepdims=True)
+    for hf in range(2):
+        grad_pre = grad_pre_ref[hf]
+        sums = jnp.sum(grad_pre.astype(F32), axis=0, keepdims=True)
+        for g in range(4):
+            grad_small_ref[hf, g : g + 1, :] = sums[:, g * half : (g + 1) * half]
+            grad_w_ref[hf, :, g * half : (g + 1) * half] = mm_tn(normed, grad_pre[:, g * half : (g + 1) * half]).astype(grad_w_ref.dtype)
+        grad_small_ref[hf, 11:12, :] = gain_grad[:, hf * half : (hf + 1) * half]
+        grad_small_ref[hf, 12:13, :] = bout_grad[:, hf * half : (hf + 1) * half]
+        grad_small_ref[hf, 13:16, :] = jnp.zeros((3, half), F32)
+
+
+def skew(tile):
+    return pltpu.roll(tile, 0, 1, stride=1, stride_axis=0)
+
+
+def layer(lengths, times, emb, ctx, cot, w, wout, small, gain_in, bout, grad_dtype=F32):
+    group, width = ctx.shape
+    half = width // 2
+    heads = width // 64
+    vmem = pl.BlockSpec(memory_space=pltpu.VMEM)
+    return pl.pallas_call(
+        layer_kernel,
+        out_shape=(
+            jax.ShapeDtypeStruct((group, width), BF16),
+            jax.ShapeDtypeStruct((group, width), BF16),
+            jax.ShapeDtypeStruct((2, width, 5 * half), grad_dtype),
+            jax.ShapeDtypeStruct((2, 16, half), F32),
+        ),
+        in_specs=[pl.BlockSpec(memory_space=pltpu.SMEM)] + [vmem] * 9,
+        out_specs=(vmem,) * 4,
+        scratch_shapes=[
+            pltpu.VMEM((2, group, 4 * half), F32),
+            pltpu.VMEM((2, 3, group, half), BF16),
+            pltpu.VMEM((heads, group, group), BF16),
+            pltpu.VMEM((heads, group, group), F32),
+            pltpu.VMEM((group, heads * group), BF16),
+            pltpu.VMEM((2, group, 4 * half), BF16),
+            pltpu.VMEM((group, width), F32),
+        ],
+        compiler_params=pltpu.CompilerParams(vmem_limit_bytes=56 * 1024 * 1024),
+    )(lengths, times, emb, ctx, cot, w, wout, small, gain_in, bout)
+
+
+def gather_kernel(ids_ref, table_ref, out_ref, total):
+    step = pl.program_id(0)
+    rows = table_ref.shape[0]
+    lane = lax.broadcasted_iota(jnp.int32, (ids_ref.shape[0], rows), 1) + step * rows
+    hot = (ids_ref[...] == lane).astype(F32).astype(BF16)
+    part = mm(hot, table_ref[...])
+
+    @pl.when(step == 0)
+    def _():
+        total[...] = part
+
+    @pl.when(step > 0)
+    def _():
+        total[...] += part
+
+    @pl.when(step == pl.num_programs(0) - 1)
+    def _():
+        out_ref[...] = total[...].astype(BF16)
+
+
+def gather_rows(ids, table, tile=1024):
+    count, width = ids.shape[0], table.shape[1]
+    return pl.pallas_call(
+        gather_kernel,
+        grid=(table.shape[0] // tile,),
+        out_shape=jax.ShapeDtypeStruct((count, width), BF16),
+        in_specs=[
+            pl.BlockSpec((count, 1), lambda i: (0, 0)),
+            pl.BlockSpec((tile, width), lambda i: (i, 0)),
+        ],
+        out_specs=pl.BlockSpec((count, width), lambda i: (0, 0)),
+        scratch_shapes=[pltpu.VMEM((count, width), F32)],
+        compiler_params=pltpu.CompilerParams(vmem_limit_bytes=40 * 1024 * 1024),
+    )(ids, table)
+
+
+def scatter_kernel(ids_ref, rows_ref, out_ref):
+    tile = out_ref.shape[0]
+    row = lax.broadcasted_iota(jnp.int32, (tile, ids_ref.shape[1]), 0) + pl.program_id(0) * tile
+    hot = (ids_ref[...] == row).astype(F32).astype(BF16)
+    out_ref[...] = mm(hot, rows_ref[...])
+
+
+def scatter_rows(ids, rows, table_rows, tile=512):
+    count, width = rows.shape
+    return pl.pallas_call(
+        scatter_kernel,
+        grid=(table_rows // tile,),
+        out_shape=jax.ShapeDtypeStruct((table_rows, width), F32),
+        in_specs=[
+            pl.BlockSpec((1, count), lambda i: (0, 0)),
+            pl.BlockSpec((count, width), lambda i: (0, 0)),
+        ],
+        out_specs=pl.BlockSpec((tile, width), lambda i: (i, 0)),
+        compiler_params=pltpu.CompilerParams(vmem_limit_bytes=40 * 1024 * 1024),
+    )(ids, rows)
+
+
+def local_streams(
+    context,
+    item_owner,
+    item_offset,
+    lengths,
+    times,
+    table,
+    cotangent,
+    ln_in_gain,
+    w_uvqk,
+    b_uvqk,
+    rel_bias,
+    time_bias,
+    ln_out_gain,
+    w_out,
+    b_out,
+):
+    owners = lax.axis_size(("pb", "ka"))
+    pbs = lax.axis_size("pb")
+    row_count, width = context.shape
+    half = width // 2
+    group = 2 * TOK_DEV
+    capacity = max(2, 2 * row_count // owners)
+    share = capacity // 2
+    ka = lax.axis_index("ka")
+    ha = lax.axis_index("ha")
+    stream = 2 * ka + ha
+    owner_ids = item_owner[:, 0]
+    owner_hits = (owner_ids[:, None] == jnp.arange(owners, dtype=jnp.int32)[None, :]).astype(jnp.int32)
+    earlier = jnp.sum((jnp.cumsum(owner_hits, axis=0) - owner_hits) * owner_hits, axis=1)
+    slot_index = owner_ids * capacity + earlier
+    requests = jnp.full((owners * capacity,), -1, jnp.int32).at[slot_index].set(item_offset)
+    arrived = lax.all_to_all(
+        requests.reshape(owners, capacity), ("pb", "ka"), split_axis=0, concat_axis=0, tiled=True
+    )
+    mine = lax.dynamic_slice_in_dim(arrived, ha * share, share, 1).reshape(owners * share, 1)
+    fetched = gather_rows(mine, table).reshape(owners, share, width)
+    returned = lax.all_to_all(fetched, ("pb", "ka"), split_axis=0, concat_axis=0, tiled=True)
+    returned = returned.reshape(owners * share, width)
+    place = earlier - ha * share
+    place = jnp.where((place >= 0) & (place < share), owner_ids * share + place, -1)
+    hot = (place[:, None] == jnp.arange(owners * share, dtype=jnp.int32)[None, :]).astype(BF16)
+    embedded = jnp.dot(hot, returned, preferred_element_type=F32).astype(BF16)
+    emb = lax.all_to_all(
+        embedded.reshape(MB, TOK_DEV, width), ("ka", "ha"), split_axis=0, concat_axis=0, tiled=True
+    )
+
+    def both_halves(array):
+        away = lax.dynamic_slice_in_dim(array, (2 * (1 - ka) + ha) * TOK_DEV, TOK_DEV, 0)
+        own = lax.dynamic_slice_in_dim(array, stream * TOK_DEV, TOK_DEV, 0)
+        other = lax.ppermute(away, "ka", [(0, 1), (1, 0)])
+        first = jnp.where(ka == 0, own, other)
+        second = jnp.where(ka == 0, other, own)
+        return jnp.concatenate([first, second], axis=0)
+
+    ctx = both_halves(context)
+    cot = both_halves(cotangent)
+    w_full = lax.all_gather(w_uvqk.reshape(w_uvqk.shape[0], 4 * half), ("ha", "pb"), axis=0, tiled=True)
+    w_full = w_full.reshape(2, width, 4 * half)
+    w_final = lax.all_gather(w_out, "pb", axis=1, tiled=True)
+    w_final = lax.all_gather(w_final, "ha", axis=0, tiled=True)
+    small = jnp.concatenate(
+        [
+            b_uvqk,
+            jnp.roll(rel_bias[:, ::-1], 1, axis=1),
+            time_bias.reshape(2, half),
+            ln_out_gain.reshape(1, half),
+        ],
+        axis=0,
+    )
+    small = lax.all_gather(small, "ha", axis=0)
+    mixed, grad_start, grad_w, grad_small = layer(
+        lax.dynamic_index_in_dim(lengths[0], stream, 0, False),
+        lax.dynamic_slice_in_dim(times[0], stream, 1, 0),
+        emb,
+        ctx,
+        cot,
+        w_full,
+        w_final,
+        small,
+        ln_in_gain.reshape(1, width),
+        b_out.reshape(1, width),
+    )
+    mixed_out = lax.all_to_all(
+        mixed.reshape(2, TOK_DEV, 2, half).transpose(0, 2, 1, 3).reshape(4, TOK_DEV, half),
+        ("ka", "ha"), split_axis=0, concat_axis=0, tiled=True,
+    ).reshape(row_count, half)
+    grad_rows = lax.all_to_all(
+        jnp.broadcast_to(grad_start.reshape(2, 1, TOK_DEV, width), (2, 2, TOK_DEV, width)).reshape(4, TOK_DEV, width),
+        ("ka", "ha"), split_axis=0, concat_axis=0, tiled=True,
+    ).reshape(row_count, width)
+    outgoing = lax.dot_general(hot, grad_rows, (((0,), (0,)), ((), ())), preferred_element_type=F32).astype(BF16)
+    incoming = lax.all_to_all(
+        outgoing.reshape(owners, share, width), ("pb", "ka"), split_axis=0, concat_axis=0, tiled=True
+    ).reshape(owners * share, width)
+    incoming = lax.all_gather(incoming, "ha", axis=0, tiled=True)
+    ids = arrived.reshape(owners, 2, share).transpose(1, 0, 2).reshape(1, 2 * owners * share)
+    table_grad = scatter_rows(ids, incoming, table.shape[0])
+    grad_w = lax.psum_scatter(grad_w, "ha", scatter_dimension=0, tiled=True)
+    grad_w = lax.psum_scatter(grad_w[0], ("pb", "ka"), scatter_dimension=0, tiled=True)
+    grad_small = lax.psum(grad_small, ("pb", "ka", "ha"))
+    mine = lax.dynamic_index_in_dim(grad_small, ha, 0, False)
+    return (
+        mixed_out,
+        grad_rows,
+        table_grad,
+        grad_small[:, 11].reshape(width),
+        grad_w[:, : 4 * half].reshape(-1, 4, half),
+        mine[0:4],
+        mine[4:8],
+        mine[8:10].reshape(4, half // 2),
+        mine[10],
+        grad_w[:, 4 * half :].T,
+        grad_small[:, 12].reshape(width),
+    )
+
+
 def solution(mesh):
+    one_stream = mesh.shape["ka"] * mesh.shape["ha"] == MB and mesh.shape["ka"] == 2
     return jax.shard_map(
-        local,
+        local_streams if one_stream else local_general,
         mesh=mesh,
         in_specs=(
             P(("pb", "ka"), None),

time: 593 us -> 280 us (0.47)
  matrix products: 132 us -> 1.85 us
  other arithmetic: 112 us -> 5.05 us
  local copies, waits for them, and re-layouts: 89.8 us -> 22.4 us
  Pallas kernels: 0 us -> 33.9 us
  waiting for transfers between devices: 91.2 us -> 72.5 us
  blocking collectives: 125 us -> 109 us
    dot_general x56 -> x2, matrix products: 132 us -> 1.85 us  [the longest x1 1.28 us: local_streams(): embedded = jnp.dot(hot, returned, preferred_element_type=F32).astype(BF16)]
    psum x5 -> x1, blocking collectives: 85.9 us -> 40.6 us  [local_streams(): grad_small = lax.psum(grad_small, ('pb', 'ka', 'ha'))]
    pallas_call x0 -> x3, Pallas kernels: none -> 33.9 us  [the longest x1 14.1 us: scatter_rows(): pl.pallas_call(scatter_kernel, grid=(table_rows // tile,), out_shape=jax....]
    all_to_all x0 -> x2, blocking collectives: none -> 32.8 us  [the longest x1 19.1 us: local_streams(): lax.all_to_all(outgoing.reshape(owners, share, width), ('pb', 'ka'), spli...]
    eq x4 -> x0, other arithmetic: 24 us -> none  [tile_scores(): time_index[:, :, None]]
    reduce_sum x25 -> x1, other arithmetic: 23.9 us -> 0.78 us  [local_streams(): jnp.sum((jnp.cumsum(owner_hits, axis=0) - owner_hits) * owner_hits, axis=1)]
    another operation x21 -> x2, local copies, waits for them, and re-layouts: 20.8 us -> 0.22 us  [the longest x8 11 us: local(): jnp.stack([key_part.reshape(group, half_cols), value_part.reshape(group,...]
    psum x2 -> x0, waiting for transfers between devices: 19.2 us -> none  [local(): lax.psum(jnp.einsum('tgc,dgc->td', grad_pre, w_full, preferred_element_ty...]
  transfers between devices with their start and end apart: 16 -> 10, of which waited for: 7 -> 4; matrix products, arithmetic and copies ran while one was open for 40% -> 6% of each run, Pallas kernels for 0% -> 8%
where the time goes in v1:
time: 280 us; the launch traced here: 279 us
  blocking collectives  109 us (39%)
  waiting for transfers between devices  72.5 us (26%)
  Pallas kernels  33.9 us (12%)
  local copies, waits for them, and re-layouts  22.4 us (8%)
  starting transfers between devices  20.3 us (7%)
  between operations  14.1 us (5%)
  other arithmetic  5.05 us (2%)
    psum x1, blocking collectives, local_streams(): grad_small = lax.psum(grad_small, ('pb', 'ka', 'ha'))  40.6 us
    reduce_scatter x1, waiting for transfers between devices, local_streams(): grad_w = lax.psum_scatter(grad_w, 'ha', scatter_dimension=0, tiled=True)  33.4 us
    reduce_scatter x1, waiting for transfers between devices, local_streams(): lax.psum_scatter(grad_w[0], ('pb', 'ka'), scatter_dimension=0, tiled=True)  27.2 us
    all_gather x1, blocking collectives, local_streams(): w_final = lax.all_gather(w_out, 'pb', axis=1, tiled=True)  22.7 us
    all_to_all x1, blocking collectives, local_streams(): lax.all_to_all(outgoing.reshape(owners, share, width), ('pb', 'ka'), spli...  19.1 us
    pallas_call x1, Pallas kernels, scatter_rows(): pl.pallas_call(scatter_kernel, grid=(table_rows // tile,), out_shape=jax....  14.1 us
    all_to_all x1, blocking collectives, local_streams(): lax.all_to_all(jnp.broadcast_to(grad_start.reshape(2, 1, TOK_DEV, width),...  13.8 us
    pallas_call x1, Pallas kernels, layer(): pl.pallas_call(layer_kernel, out_shape=(jax.ShapeDtypeStruct((group, widt...  12.1 us
  transfers between devices with their start and end apart: 10, of which 4 were waited for; matrix products, arithmetic and copies ran while one was open for 6% of the time, Pallas kernels for 8%

profile of v1, /device:TPU:0, one launch (start us, length us, event | category | flops | bytes accessed | tf_op | source)
XLA Modules:
  0.0 278.8 jit_solution(10419068627440774858)
XLA Ops:
  7.2 0.0 all-gather.5.cloned.1.call-start
  7.2 1.6 copy.38
  8.8 0.7 fusion.5
  9.5 1.1 reduce-window.6
  10.7 0.2 slice_reduce_fusion
  10.9 0.8 fusion.4
  11.7 0.7 and_select_fusion
  12.4 2.6 scatter_custom_fusion
  15.0 0.7 all_to_all.21
  15.7 7.4 %all-to-all-start = ((s32[16,1,64]{2,1,0:T(1,128)}), s32[16,1,64]{2,1,0:T(1,128)S(1)}, u32[]{:S(2)}, u32[]{:S(2)}) async-start(s32[16,1,64]{2,1,0:T(1,128)} %all_to_all.21), calls=%async_computation | async-start | bytes 16384 | tf_op jit(solution)/shard_map/all_to_all | solution.py:666
  23.1 6.3 %all-to-all-done = s32[16,1,64]{2,1,0:T(1,128)S(1)} async-done(((s32[16,1,64]{2,1,0:T(1,128)}), s32[16,1,64]{2,1,0:T(1,128)S(1)}, u32[]{:S(2)}, u32[]{:S(2)}) %all-to-all-start) | async-done | bytes 4128 | tf_op jit(solution)/shard_map/all_to_all | solution.py:666
  29.4 0.1 dynamic-slice_reduce_fusion
  29.5 0.3 reshape.173.ids_ref
  29.8 3.4 %copy-done.1 = bf16[8192,512]{1,0:T(8,128)(2,1)S(1)} copy-done((bf16[8192,512]{1,0:T(8,128)(2,1)S(1)}, bf16[8192,512]{1,0:T(8,128)(2,1)}, u32[]{:S(2)}) %copy-start.1) | copy-done | bytes 8388632
  33.2 7.6 %shard_map.230 = bf16[512,512]{1,0:T(8,128)(2,1)} custom-call(s32[512,1]{1,0:T(8,128)S(1)} %reshape.173.ids_ref, bf16[8192,512]{1,0:T(8,128)(2,1)S(1)} %copy-done.1), custom_call_target="tpu_custom_call" | custom-call | tf_op jit(solution)/shard_map/pallas_call | solution.py:598
  40.9 3.6 %all-to-all-start.1 = ((bf16[16,32,512]{2,1,0:T(8,128)(2,1)}), bf16[16,32,512]{2,1,0:T(8,128)(2,1)S(1)}, u32[]{:S(2)}, u32[]{:S(2)}) async-start(bf16[16,32,512]{2,1,0:T(8,128)(2,1)} %bitcast.8), calls=%async_computation.1 | async-start | bytes 1048576 | tf_op jit(solution)/shard_map/all_to_all | solution.py:671
  44.5 1.9 collective-permute-start.1
  46.4 0.3 collective-permute-start
  46.7 0.1 slice.53
  46.7 0.2 reverse.2
  46.9 0.1 slice.72
  47.0 22.7 %all_gather.19 = bf16[256,512]{0,1:T(8,128)(2,1)S(1)} all-gather(bf16[256,64]{0,1:T(8,128)(2,1)S(1)} %copy-done.8), channel_id=1, replica_groups=mesh['pb'=8,'ka'=2,'ha'=2] {'pb'}, dimensions={1}, use_global_device_ids=true | all-gather | bytes 294912 | tf_op jit(solution)/shard_map/all_gather | solution.py:693
  69.7 0.1 copy.34
  69.9 0.1 maximum_bitcast_fusion
  70.0 4.5 %all-gather.1.small_ref = f32[2,11,256]{2,1,0:T(8,128)} all-gather(f32[1,11,256]{2,1,0:T(8,128)S(1)} %maximum_bitcast_fusion), channel_id=2, replica_groups=mesh['pb'=8,'ka'=2,'ha'=2] {'ha'}, dimensions={0}, use_global_device_ids=true | all-gather | bytes 33792 | tf_op jit(solution)/shard_map/all_gather | solution.py:704
  74.5 1.2 fusion.9.lengths_ref
  75.7 0.6 fusion.8.times_ref
  76.3 8.2 %all_gather.20.wout_ref = bf16[512,512]{1,0:T(8,128)(2,1)} all-gather(bf16[256,512]{1,0:T(8,128)(2,1)S(1)} %copy.34), channel_id=1, replica_groups=mesh['pb'=8,'ka'=2,'ha'=2] {'ha'}, dimensions={0}, use_global_device_ids=true | all-gather | bytes 786432 | tf_op jit(solution)/shard_map/all_gather | solution.py:694
  84.4 1.3 convolution_convert_fusion.1
  85.7 3.5 %all-to-all-start.2 = ((bf16[4,128,512]{2,1,0:T(8,128)(2,1)}), bf16[4,128,512]{2,1,0:T(8,128)(2,1)S(1)}, u32[]{:S(2)}, u32[]{:S(2)}) async-start(bf16[4,128,512]{2,1,0:T(8,128)(2,1)} %bitcast.10), calls=%async_computation.2 | async-start | bytes 1048576 | tf_op jit(solution)/shard_map/all_to_all | solution.py:677
  89.2 0.2 reduce-scatter.3.cloned.1.call-start
  89.5 0.1 broadcast_select_fusion.1
  89.5 0.1 broadcast_select_fusion.3
  89.6 0.8 pad_maximum_fusion
  90.4 5.5 %all-to-all-done.2.emb_ref = bf16[4,128,512]{2,1,0:T(8,128)(2,1)S(1)} async-done(((bf16[4,128,512]{2,1,0:T(8,128)(2,1)}), bf16[4,128,512]{2,1,0:T(8,128)(2,1)S(1)}, u32[]{:S(2)}, u32[]{:S(2)}) %all-to-all-start.2) | async-done | bytes 524320 | tf_op jit(solution)/shard_map/all_to_all | solution.py:677
  96.0 0.8 copy-done.3
  96.7 12.1 %shard_map.231 = (bf16[256,512]{1,0:T(8,128)(2,1)}, bf16[256,512]{1,0:T(8,128)(2,1)}, f32[2,512,1280]{2,1,0:T(8,128)}, f32[2,16,256]{2,1,0:T(8,128)}) custom-call(s32[4]{0:T(128)} %fusion.9.lengths_ref, s32[1,256]{1,0:T(1,128)} %fusion.8.times_ref, bf16[4,128,512]{2,1,0:T(8,128)(2,1)} %copy-done.3, bf16[256,512]{1,0:T(8,128)(2,1)} %get-tuple-element.29.ctx_ref, ...), custom_call_target="tpu_custom_call" | custom-call | tf_op jit(solution)/shard_map/pallas_call | solution.py:553
  108.9 0.0 all-gather.7.cloned.1.call-start
  108.9 0.9 copy-done.4
  109.8 13.8 %all_to_all.34 = bf16[4,128,512]{2,1,0:T(8,128)(2,1)S(1)} all-to-all(bf16[4,128,512]{2,1,0:T(8,128)(2,1)S(1)} %bitcast.68), channel_id=1, replica_groups=mesh['pb'=8,'ka'=2,'ha'=2] {'ka','ha'}, dimensions={0} | all-to-all | bytes 1048576 | tf_op jit(solution)/shard_map/all_to_all | solution.py:721
  123.6 0.6 convolution_convert_fusion
  124.1 19.1 %all_to_all.35 = bf16[16,32,512]{2,1,0:T(8,128)(2,1)} all-to-all(bf16[16,32,512]{2,1,0:T(8,128)(2,1)S(1)} %bitcast.71), channel_id=1, replica_groups=mesh['pb'=8,'ka'=2,'ha'=2] {'pb','ka'}, dimensions={0} | all-to-all | bytes 1048576 | tf_op jit(solution)/shard_map/all_to_all | solution.py:726
  143.2 0.0 reduce-scatter.5.cloned.1.call-start
  143.3 33.4 %reduce-scatter.3.cloned.1.call-done = f32[1,512,1280]{2,1,0:T(8,128)} async-done(((f32[2,512,1280]{2,1,0:T(8,128)}), f32[1,512,1280]{2,1,0:T(8,128)}) %reduce-scatter.3.cloned.1.call-update) | async-done | bytes 2621456 | tf_op jit(solution)/shard_map/reduce_scatter | solution.py:732
  176.7 0.5 broadcast.65
  177.2 0.7 reduce.9
  177.9 0.1 reshape.155
  178.0 0.1 reshape.156.ids_ref
  178.0 0.1 reshape.150
  178.1 0.7 copy.35
  178.8 3.4 %all-to-all-start.3 = ((bf16[4,128,256]{2,1,0:T(8,128)(2,1)}), bf16[4,128,256]{2,1,0:T(8,128)(2,1)S(1)}, u32[]{:S(2)}, u32[]{:S(2)}) async-start(bf16[4,128,256]{2,1,0:T(8,128)(2,1)} %bitcast.17), calls=%async_computation.3 | async-start | bytes 524288 | tf_op jit(solution)/shard_map/all_to_all | solution.py:717
  182.3 40.6 %psum.7 = f32[2,16,256]{2,1,0:T(8,128)S(1)} all-reduce(f32[2,16,256]{2,1,0:T(8,128)S(1)} %copy-done.9), channel_id=1, replica_groups=mesh['pb'=8,'ka'=2,'ha'=2] {'pb','ka','ha'}, use_global_device_ids=true, to_apply=%region_4.5 | all-reduce | flops 8192 | bytes 65536 | tf_op jit(solution)/shard_map/psum | solution.py:734
  222.9 0.6 reshape.160
  223.5 0.6 constant_dynamic-slice_fusion.1
  224.1 0.6 dynamic-slice_bitcast_fusion
  224.7 0.6 fusion.10
  225.3 1.2 copy-done.2
  226.5 14.1 %shard_map.232 = f32[8192,512]{1,0:T(8,128)} custom-call(s32[1,1024]{1,0:T(1,128)S(1)} %reshape.156.ids_ref, bf16[1024,512]{1,0:T(8,128)(2,1)S(1)} %copy-done.2), custom_call_target="tpu_custom_call" | custom-call | tf_op jit(solution)/shard_map/pallas_call | solution.py:621
  240.6 27.2 %reduce-scatter.5.cloned.1.call-done = f32[32,1280]{1,0:T(8,128)} async-done(((f32[512,1280]{1,0:T(8,128)}), f32[32,1280]{1,0:T(8,128)}) %reduce-scatter.5.cloned.1.call-update) | async-done | bytes 163856 | tf_op jit(solution)/shard_map/reduce_scatter | solution.py:733
  267.8 0.9 slice.67
  268.7 0.7 reshape.159
  269.4 1.4 slice_bitcast_fusion
  270.8 0.7 copy.42
  271.5 0.8 copy.43
  (44 shorter events, 0.3 us)
Async XLA Ops:
  7.2 68.5 %copy-start = (s32[1,4,256]{2,1,0:T(4,128)S(1)}, s32[1,4,256]{2,1,0:T(4,128)}, u32[]{:S(2)}) copy-start(s32[1,4,256]{2,1,0:T(4,128)} %param.19) | copy-start | bytes 12292
  7.2 88.8 %all-gather.5.cloned.1.call-start = ((), (), s32[]{:S(2)}) async-start(), calls=%async_computation.8 | async-start | bytes 2228224 | tf_op jit(solution)/shard_map/all_gather | solution.py:691
  15.7 13.7 %all-to-all-start = ((s32[16,1,64]{2,1,0:T(1,128)}), s32[16,1,64]{2,1,0:T(1,128)S(1)}, u32[]{:S(2)}, u32[]{:S(2)}) async-start(s32[16,1,64]{2,1,0:T(1,128)} %all_to_all.21), calls=%async_computation | async-start | bytes 16384 | tf_op jit(solution)/shard_map/all_to_all | solution.py:666
  29.8 3.4 %copy-start.1 = (bf16[8192,512]{1,0:T(8,128)(2,1)S(1)}, bf16[8192,512]{1,0:T(8,128)(2,1)}, u32[]{:S(2)}) copy-start(bf16[8192,512]{1,0:T(8,128)(2,1)} %table_ref.1) | copy-start | bytes 25165828
  33.2 11.3 %copy-start.6 = (bf16[512,512]{1,0:T(8,128)(2,1)S(1)}, bf16[512,512]{1,0:T(8,128)(2,1)}, u32[]{:S(2)}) copy-start(bf16[512,512]{1,0:T(8,128)(2,1)} %param.21) | copy-start | bytes 1572868
  33.2 13.2 %copy-start.7 = (bf16[512,512]{1,0:T(8,128)(2,1)S(1)}, bf16[512,512]{1,0:T(8,128)(2,1)}, u32[]{:S(2)}) copy-start(bf16[512,512]{1,0:T(8,128)(2,1)} %param.15) | copy-start | bytes 1572868
  33.2 13.5 %copy-start.10 = (f32[4,256]{1,0:T(4,128)S(1)}, f32[4,256]{1,0:T(4,128)}, u32[]{:S(2)}) copy-start(f32[4,256]{1,0:T(4,128)} %param.25) | copy-start | bytes 12292
  33.2 13.6 %copy-start.12 = (f32[4,128]{1,0:T(4,128)S(1)}, f32[4,128]{1,0:T(4,128)}, u32[]{:S(2)}) copy-start(f32[4,128]{1,0:T(4,128)} %param.26) | copy-start | bytes 6148
  33.2 13.8 %copy-start.8 = (bf16[256,64]{0,1:T(8,128)(2,1)S(1)}, bf16[256,64]{0,1:T(8,128)(2,1)}, u32[]{:S(2)}) copy-start(bf16[256,64]{0,1:T(8,128)(2,1)} %param.28) | copy-start | bytes 98308
  33.2 36.7 %slice-start = ((f32[4,256]{1,0:T(4,128)}), f32[4,1]{1,0:T(4,128)S(1)}, s32[]{:S(2)}) async-start(f32[4,256]{1,0:T(4,128)} %param.25), calls=%async_computation.12 | async-start | bytes 4096 | tf_op jit(solution)/shard_map/jit(_roll_static)/slice | solution.py:698
  33.2 36.7 %copy-start.11 = (f32[4,256]{1,0:T(4,128)S(1)}, f32[4,256]{1,0:T(4,128)}, u32[]{:S(2)}) copy-start(f32[4,256]{1,0:T(4,128)} %param.24) | copy-start | bytes 12292
  33.2 36.7 %copy-start.13 = (f32[256]{0:T(256)S(1)}, f32[256]{0:T(256)}, u32[]{:S(2)}) copy-start(f32[256]{0:T(256)} %param.27) | copy-start | bytes 3076
  40.9 43.6 %all-to-all-start.1 = ((bf16[16,32,512]{2,1,0:T(8,128)(2,1)}), bf16[16,32,512]{2,1,0:T(8,128)(2,1)S(1)}, u32[]{:S(2)}, u32[]{:S(2)}) async-start(bf16[16,32,512]{2,1,0:T(8,128)(2,1)} %bitcast.8), calls=%async_computation.1 | async-start | bytes 1048576 | tf_op jit(solution)/shard_map/all_to_all | solution.py:671
  44.5 45.0 %collective-permute-start.1 = (bf16[128,512]{1,0:T(8,128)(2,1)S(1)}, bf16[128,512]{1,0:T(8,128)(2,1)S(1)}, u32[]{:S(2)}, u32[]{:S(2)}) collective-permute-start(bf16[128,512]{1,0:T(8,128)(2,1)S(1)} %constant_dynamic-slice_fusion.2), channel_id=1, source_target_pairs={{0,2},{2,0},{1,3},{3,1},{4,6},{6,4},{5,7},{7,5},{8,10},{10,8},{9,1... | collective-permute-start | bytes 393224 | tf_op jit(solution)/shard_map/ppermute | solution.py:684
  46.4 43.2 %collective-permute-start = (bf16[128,512]{1,0:T(8,128)(2,1)S(1)}, bf16[128,512]{1,0:T(8,128)(2,1)S(1)}, u32[]{:S(2)}, u32[]{:S(2)}) collective-permute-start(bf16[128,512]{1,0:T(8,128)(2,1)S(1)} %constant_dynamic-slice_fusion.3), channel_id=1, source_target_pairs={{0,2},{2,0},{1,3},{3,1},{4,6},{6,4},{5,7},{7,5},{8,10},{10,8},{9,1... | collective-permute-start | bytes 393224 | tf_op jit(solution)/shard_map/ppermute | solution.py:684
  85.7 10.2 %all-to-all-start.2 = ((bf16[4,128,512]{2,1,0:T(8,128)(2,1)}), bf16[4,128,512]{2,1,0:T(8,128)(2,1)S(1)}, u32[]{:S(2)}, u32[]{:S(2)}) async-start(bf16[4,128,512]{2,1,0:T(8,128)(2,1)} %bitcast.10), calls=%async_computation.2 | async-start | bytes 1048576 | tf_op jit(solution)/shard_map/all_to_all | solution.py:677
  89.2 87.4 %reduce-scatter.3.cloned.1.call-start = ((), (), s32[]{:S(2)}) async-start(), calls=%async_computation.10 | async-start | bytes 7864320 | tf_op jit(solution)/shard_map/reduce_scatter | solution.py:732
  96.0 0.8 copy-start.3
  108.8 1.0 copy-start.4
  108.8 69.2 %copy-start.5 = (bf16[256,512]{1,0:T(8,128)(2,1)S(1)}, bf16[256,512]{1,0:T(8,128)(2,1)}, u32[]{:S(2)}) copy-start(bf16[256,512]{1,0:T(8,128)(2,1)} %get-tuple-element.15) | copy-start | bytes 786436
  108.9 73.4 %copy-start.9 = (f32[2,16,256]{2,1,0:T(8,128)S(1)}, f32[2,16,256]{2,1,0:T(8,128)}, u32[]{:S(2)}) copy-start(f32[2,16,256]{2,1,0:T(8,128)} %get-tuple-element.17) | copy-start | bytes 98308
  108.9 116.4 %all-gather.7.cloned.1.call-start = ((), (), s32[]{:S(2)}) async-start(), calls=%async_computation.9 | async-start | bytes 1572864 | tf_op jit(solution)/shard_map/all_gather | solution.py:729
  143.2 124.6 %reduce-scatter.5.cloned.1.call-start = ((), (), s32[]{:S(2)}) async-start(), calls=%async_computation.11 | async-start | bytes 2785280 | tf_op jit(solution)/shard_map/reduce_scatter | solution.py:733
  178.8 46.4 %all-to-all-start.3 = ((bf16[4,128,256]{2,1,0:T(8,128)(2,1)}), bf16[4,128,256]{2,1,0:T(8,128)(2,1)S(1)}, u32[]{:S(2)}, u32[]{:S(2)}) async-start(bf16[4,128,256]{2,1,0:T(8,128)(2,1)} %bitcast.17), calls=%async_computation.3 | async-start | bytes 524288 | tf_op jit(solution)/shard_map/all_to_all | solution.py:717
  225.2 1.2 copy-start.2
Sparse Core Ops, SparseCore 0:
  10.8 49.4 all-gather.4
  109.0 67.6 reduce-scatter.2
  178.3 21.7 all-gather.6
  204.1 63.6 reduce-scatter.4

commit v2 on v1

--- a/solution.py
+++ b/solution.py
@@ -347,7 +347,7 @@
 
 
 def layer_kernel(
-    lengths_ref, times_ref, emb_ref, ctx_ref, cot_ref, w_ref, wout_ref, small_ref, gain_in_ref, bout_ref,
+    lengths_ref, times_ref, emb_ref, ctx_ref, cot_ref, w_ref, small_ref, gain_in_ref, bout_ref,
     mixed_ref, grad_start_ref, grad_w_ref, grad_small_ref,
     slope_ref, qkv_ref, w_att_ref, sm_ref, gs_ref, grad_pre_ref, att_ref,
 ):
@@ -400,7 +400,7 @@
             if g == 0:
                 gates.append(act)
             elif g == 2:
-                qkv_ref[hf, 1] = (act * 0.125).astype(BF16).astype(BF16)
+                qkv_ref[hf, 1] = (act * 0.125).astype(BF16)
             else:
                 qkv_ref[hf, {1: 0, 3: 2}[g]] = act.astype(BF16)
     gate = jnp.concatenate(gates, axis=1)
@@ -412,6 +412,11 @@
         zero = jnp.zeros_like(tile)
         return jnp.where(low_half, tile, zero), jnp.where(low_half, zero, tile)
 
+    turn = ((lane + row) % group == 0).astype(F32)
+    rel_back = jnp.dot(
+        jnp.concatenate([small_ref[0, 4:8, :], small_ref[1, 4:8, :]], axis=0),
+        turn, preferred_element_type=F32, precision=lax.Precision.HIGHEST,
+    )
     for hf in range(2):
         for pair in range(half // 128):
             cols = slice(pair * 128, (pair + 1) * 128)
@@ -422,10 +427,7 @@
             for sub in range(2):
                 head_in = pair * 2 + sub
                 head = hf * (half // 64) + head_in
-                rel = pltpu.roll(
-                    jnp.broadcast_to(small_ref[hf, 4 + head_in : 5 + head_in, :], (group, group)),
-                    0, 1, stride=1, stride_axis=0,
-                )
+                rel = skew(jnp.broadcast_to(rel_back[head : head + 1], (group, group)))
                 table = small_ref[hf, 8 + head_in // 2 : 9 + head_in // 2, (head_in % 2) * buckets : (head_in % 2 + 1) * buckets]
                 table = jnp.broadcast_to(table, (group, buckets))
                 scores = mm_nt(queries[sub], keys) + rel + jnp.concatenate(
@@ -450,11 +452,20 @@
     unit_out = centered * inv_out
     gain_out = jnp.concatenate([small_ref[0, 10:11, :], small_ref[1, 10:11, :]], axis=1)
     mixed_in = (unit_out * gain_out * gate).astype(BF16)
-    mixed_ref[...] = (mm(mixed_in, wout_ref[...]) + bout_ref[...] + start).astype(BF16)
+    projected = None
+    for hf in range(2):
+        part = mm_nt(mixed_in[:, hf * half : (hf + 1) * half], w_ref[hf, :, 4 * half : 5 * half])
+        projected = part if projected is None else projected + part
+    mixed_ref[...] = (projected + bout_ref[...] + start).astype(BF16)
     cot = cot_ref[...]
-    grad_mixed = mm_nt(cot, wout_ref[...])
+    grad_mixed = jnp.concatenate([mm(cot, w_ref[hf, :, 4 * half : 5 * half]) for hf in range(2)], axis=1)
+    blocks = grad_w_ref.shape[1:4]
+
+    def put_grad_w(hf, g, value):
+        grad_w_ref[hf, :, :, :, g * half : (g + 1) * half] = value.astype(BF16).reshape(blocks + (half,))
+
     for hf in range(2):
-        grad_w_ref[hf, :, 4 * half : 5 * half] = mm_tn(cot, mixed_in[:, hf * half : (hf + 1) * half]).astype(grad_w_ref.dtype)
+        put_grad_w(hf, 4, mm_tn(cot, mixed_in[:, hf * half : (hf + 1) * half]))
     grad_unit_raw = grad_mixed * unit_out
     grad_gate = grad_unit_raw * gain_out
     grad_gain_out = jnp.sum(grad_unit_raw * gate, axis=0, keepdims=True)
@@ -521,7 +532,7 @@
     grad_normed = None
     for hf in range(2):
         grad_pre = grad_pre_ref[hf]
-        part = mm_nt(grad_pre, w_ref[hf])
+        part = mm_nt(grad_pre, w_ref[hf, :, 0 : 4 * half])
         grad_normed = part if grad_normed is None else grad_normed + part
     grad_unit_in = grad_normed * gain_in_ref[...]
     first = jnp.mean(grad_unit_in, axis=1, keepdims=True)
@@ -535,7 +546,7 @@
         sums = jnp.sum(grad_pre.astype(F32), axis=0, keepdims=True)
         for g in range(4):
             grad_small_ref[hf, g : g + 1, :] = sums[:, g * half : (g + 1) * half]
-            grad_w_ref[hf, :, g * half : (g + 1) * half] = mm_tn(normed, grad_pre[:, g * half : (g + 1) * half]).astype(grad_w_ref.dtype)
+            put_grad_w(hf, g, mm_tn(normed, grad_pre[:, g * half : (g + 1) * half]))
         grad_small_ref[hf, 11:12, :] = gain_grad[:, hf * half : (hf + 1) * half]
         grad_small_ref[hf, 12:13, :] = bout_grad[:, hf * half : (hf + 1) * half]
         grad_small_ref[hf, 13:16, :] = jnp.zeros((3, half), F32)
@@ -545,7 +556,7 @@
     return pltpu.roll(tile, 0, 1, stride=1, stride_axis=0)
 
 
-def layer(lengths, times, emb, ctx, cot, w, wout, small, gain_in, bout, grad_dtype=F32):
+def layer(lengths, times, emb, ctx, cot, w, small, gain_in, bout, grad_shape):
     group, width = ctx.shape
     half = width // 2
     heads = width // 64
@@ -555,10 +566,10 @@
         out_shape=(
             jax.ShapeDtypeStruct((group, width), BF16),
             jax.ShapeDtypeStruct((group, width), BF16),
-            jax.ShapeDtypeStruct((2, width, 5 * half), grad_dtype),
+            jax.ShapeDtypeStruct((2,) + grad_shape + (5 * half,), BF16),
             jax.ShapeDtypeStruct((2, 16, half), F32),
         ),
-        in_specs=[pl.BlockSpec(memory_space=pltpu.SMEM)] + [vmem] * 9,
+        in_specs=[pl.BlockSpec(memory_space=pltpu.SMEM)] + [vmem] * 8,
         out_specs=(vmem,) * 4,
         scratch_shapes=[
             pltpu.VMEM((2, group, 4 * half), F32),
@@ -570,7 +581,231 @@
             pltpu.VMEM((group, width), F32),
         ],
         compiler_params=pltpu.CompilerParams(vmem_limit_bytes=56 * 1024 * 1024),
-    )(lengths, times, emb, ctx, cot, w, wout, small, gain_in, bout)
+    )(lengths, times, emb, ctx, cot, w, small, gain_in, bout)
+
+
+MESH = pl.DeviceIdType.MESH
+
+
+def remote(src, dst, send_sem, recv_sem, device):
+    return pltpu.make_async_remote_copy(
+        src_ref=src, dst_ref=dst, send_sem=send_sem, recv_sem=recv_sem, device_id=device, device_id_type=MESH
+    )
+
+
+def greet(devices):
+    barrier = pltpu.get_barrier_semaphore()
+    for device in devices:
+        pl.semaphore_signal(barrier, inc=1, device_id=device, device_id_type=MESH)
+    pl.semaphore_wait(barrier, len(devices))
+
+
+def back_kernel(
+    place_ref, mixed_ref, grad_start_ref, grad_w_ref, grad_small_ref,
+    incoming_ref, grad_rows_ref, mixed_rows_ref, grad_w_out_ref, small_out_ref,
+    outgoing, stage1, core_in, hop_in_x, hop_in_y, stage2, hop_in2, stage3, z_in, small_mine, small_in,
+    rows_send, rows_recv, mixed_send, mixed_recv, item_send, item_recv, pass_send, pass_recv,
+    core_send, core_recv, hop_send, hop_recv, z_send, z_recv, small_send, small_recv,
+):
+    pbs, kas = lax.axis_size("pb"), lax.axis_size("ka")
+    owners = pbs * kas
+    zs = pbs // 2
+    pb, ka, ha = lax.axis_index("pb"), lax.axis_index("ka"), lax.axis_index("ha")
+    z, core = pb // 2, pb % 2
+    me = pb * kas + ka
+    stream = 2 * ka + ha
+    tok = mixed_ref.shape[0] // 2
+    half = mixed_ref.shape[1] // 2
+    wide = grad_w_ref.shape[-1] // 2
+    x_peer = (pb, ka, 1 - ha)
+    y_peer = (pb, 1 - ka, ha)
+    xy_peer = (pb, 1 - ka, 1 - ha)
+    core_peer = (2 * z + 1 - core, ka, ha)
+
+    def owner(index):
+        return (index // kas, index % kas, ha)
+
+    greet([owner(lax.rem(me + d, owners)) for d in range(1, owners)] + [x_peer, xy_peer])
+
+    quads = [(y_peer, 1 - ka, ha), (x_peer, ka, 1 - ha), (xy_peer, 1 - ka, 1 - ha)]
+    row_copies, mixed_copies = [], []
+    for i, (device, to_ka, to_ha) in enumerate(quads):
+        copy = remote(
+            grad_start_ref.at[pl.ds(to_ka * tok, tok)], grad_rows_ref.at[stream], rows_send.at[i], rows_recv.at[i], device
+        )
+        copy.start()
+        row_copies.append(copy)
+    core_copies = []
+    for part in range(2):
+        cols = pl.ds(part * wide, wide)
+        copy = remote(
+            grad_w_ref.at[:, :, 1 - core, :, cols], core_in.at[part], core_send.at[part], core_recv.at[part], core_peer
+        )
+        copy.start()
+        core_copies.append(copy)
+    small_copies = [remote(grad_small_ref, small_in.at[0], small_send.at[0], small_recv.at[0], core_peer)]
+    small_copies[0].start()
+    for i, (device, to_ka, to_ha) in enumerate(quads):
+        copy = remote(
+            mixed_ref.at[pl.ds(to_ka * tok, tok), pl.ds(pl.multiple_of(to_ha * half, half), half)],
+            mixed_rows_ref.at[stream], mixed_send.at[i], mixed_recv.at[i], device,
+        )
+        copy.start()
+        mixed_copies.append(copy)
+    grad_rows_ref[stream] = grad_start_ref[pl.ds(pl.multiple_of(ka * tok, tok), tok)]
+    mixed_rows_ref[stream] = mixed_ref[
+        pl.ds(pl.multiple_of(ka * tok, tok), tok), pl.ds(pl.multiple_of(ha * half, half), half)
+    ]
+    for copy in row_copies:
+        copy.wait_recv()
+
+    count = grad_rows_ref.shape[0] * tok
+    share = count // owners
+    slot = lax.broadcasted_iota(jnp.int32, (count, count), 1)
+    hot = (place_ref[...] == slot).astype(F32).astype(BF16)
+    rows = grad_rows_ref[...].reshape(count, 2 * half)
+    outgoing[...] = mm_tn(hot, rows).astype(BF16).reshape(outgoing.shape)
+    item_copies = []
+    for d in range(1, owners):
+        to = lax.rem(me + d, owners)
+        copy = remote(outgoing.at[to], incoming_ref.at[ha, me], item_send.at[d], item_recv.at[d], owner(to))
+        copy.start()
+        item_copies.append(copy)
+    incoming_ref[ha, me] = outgoing[me]
+    pass_copies = []
+
+    def hand_on(index):
+        copy = remote(
+            incoming_ref.at[ha, index], incoming_ref.at[ha, index],
+            pass_send.at[len(pass_copies)], pass_recv.at[len(pass_copies)], x_peer,
+        )
+        copy.start()
+        pass_copies.append(copy)
+
+    hand_on(me)
+
+    hop_copies = []
+    for part in range(2):
+        cols = slice(part * wide, (part + 1) * wide)
+        core_copies[part].wait_recv()
+        for h in range(2):
+            total = grad_w_ref[h, :, core, :, cols].astype(F32) + core_in[part, h].astype(F32)
+            stage1[part, h] = total.astype(BF16).reshape(stage1.shape[2:])
+        if part == 0:
+            copy = remote(stage1.at[0, 1 - ha], hop_in_x, hop_send.at[0], hop_recv.at[0], x_peer)
+        else:
+            copy = remote(stage1.at[1, :, :, 1 - ka], hop_in_y, hop_send.at[1], hop_recv.at[1], y_peer)
+        copy.start()
+        hop_copies.append(copy)
+    small_copies[0].wait_recv()
+    small_mine[0] = grad_small_ref[...] + small_in[0]
+    small_copies.append(remote(small_mine.at[0], small_in.at[1], small_send.at[1], small_recv.at[1], x_peer))
+    small_copies[1].start()
+
+    def take(first, last):
+        for d in range(first, last):
+            item_copies[d - 1].wait_recv()
+            hand_on(lax.rem(me - d + owners, owners))
+
+    take(1, 6)
+    hop_copies[0].wait_recv()
+    stage2[0] = (stage1[0, ha].astype(F32) + hop_in_x[...].astype(F32)).astype(BF16)
+    hop_copies.append(remote(stage2.at[0, :, 1 - ka], hop_in2.at[0], hop_send.at[2], hop_recv.at[2], y_peer))
+    hop_copies[2].start()
+    hop_copies[1].wait_recv()
+    for h in range(2):
+        stage2[1, :, h] = (stage1[1, h, :, ka].astype(F32) + hop_in_y[h].astype(F32)).astype(BF16)
+    hop_copies.append(remote(stage2.at[1, :, 1 - ha], hop_in2.at[1], hop_send.at[3], hop_recv.at[3], x_peer))
+    hop_copies[3].start()
+    small_copies[1].wait_recv()
+    small_mine[1] = small_mine[0] + small_in[1]
+    small_copies.append(remote(small_mine.at[1], small_in.at[2], small_send.at[2], small_recv.at[2], y_peer))
+    small_copies[2].start()
+
+    take(6, 11)
+    z_copies = []
+    for part in range(2):
+        hop_copies[2 + part].wait_recv()
+        kept = stage2[0, :, ka] if part == 0 else stage2[1, :, ha]
+        stage3[part] = (kept.astype(F32) + hop_in2[part].astype(F32)).astype(BF16)
+    small_copies[2].wait_recv()
+    small_mine[2] = small_mine[1] + small_in[2]
+    for d in range(1, zs):
+        to = lax.rem(z + d, zs)
+        device = (2 * to + core, ka, ha)
+        for part in range(2):
+            i = (d - 1) * 2 + part
+            copy = remote(stage3.at[part, to], z_in.at[part, d - 1], z_send.at[i], z_recv.at[i], device)
+            copy.start()
+            z_copies.append(copy)
+        i = 2 + d
+        copy = remote(small_mine.at[2], small_in.at[i], small_send.at[i], small_recv.at[i], device)
+        copy.start()
+        small_copies.append(copy)
+    take(11, owners)
+    for copy in z_copies:
+        copy.wait_recv()
+    for part in range(2):
+        total = stage3[part, z].astype(F32)
+        for d in range(zs - 1):
+            total = total + z_in[part, d].astype(F32)
+        grad_w_out_ref[:, part * wide : (part + 1) * wide] = total
+    total = small_mine[2]
+    for copy in small_copies[3:]:
+        copy.wait_recv()
+    for d in range(1, zs):
+        total = total + small_in[2 + d]
+    small_out_ref[...] = total
+    for copy in mixed_copies + pass_copies:
+        copy.wait_recv()
+    for copies in (row_copies, mixed_copies, item_copies, pass_copies, core_copies, hop_copies, z_copies, small_copies):
+        for copy in copies:
+            copy.wait_send()
+
+
+def back(place, mixed, grad_start, grad_w, grad_small):
+    pbs, kas = lax.axis_size("pb"), lax.axis_size("ka")
+    owners, zs = pbs * kas, pbs // 2
+    group, width = mixed.shape
+    tok, half = group // 2, width // 2
+    count = MB * tok
+    share = count // owners
+    block = grad_w.shape[3] // 2
+    wide = grad_w.shape[4] // 2
+    vmem = pl.BlockSpec(memory_space=pltpu.VMEM)
+    dma = pltpu.SemaphoreType.DMA
+    return pl.pallas_call(
+        back_kernel,
+        out_shape=(
+            jax.ShapeDtypeStruct((2, owners, share, width), BF16),
+            jax.ShapeDtypeStruct((MB, tok, width), BF16),
+            jax.ShapeDtypeStruct((MB, tok, half), BF16),
+            jax.ShapeDtypeStruct((block, 2 * wide), F32),
+            jax.ShapeDtypeStruct(grad_small.shape, F32),
+        ),
+        in_specs=[vmem] * 5,
+        out_specs=(vmem,) * 5,
+        scratch_shapes=[
+            pltpu.VMEM((owners, share, width), BF16),
+            pltpu.VMEM((2, 2, zs, 2, block, wide), BF16),
+            pltpu.VMEM((2, 2, zs, 2 * block, wide), BF16),
+            pltpu.VMEM((zs, 2, block, wide), BF16),
+            pltpu.VMEM((2, zs, block, wide), BF16),
+            pltpu.VMEM((2, zs, 2, block, wide), BF16),
+            pltpu.VMEM((2, zs, block, wide), BF16),
+            pltpu.VMEM((2, zs, block, wide), BF16),
+            pltpu.VMEM((2, zs - 1, block, wide), BF16),
+            pltpu.VMEM((3,) + grad_small.shape, F32),
+            pltpu.VMEM((2 + zs,) + grad_small.shape, F32),
+            dma((3,)), dma((3,)), dma((3,)), dma((3,)),
+            dma((owners,)), dma((owners,)), dma((owners,)), dma((owners,)),
+            dma((2,)), dma((2,)), dma((4,)), dma((4,)),
+            dma((2 * (zs - 1),)), dma((2 * (zs - 1),)), dma((2 + zs,)), dma((2 + zs,)),
+        ],
+        compiler_params=pltpu.CompilerParams(
+            collective_id=1, has_side_effects=True, vmem_limit_bytes=48 * 1024 * 1024
+        ),
+    )(place, mixed, grad_start, grad_w, grad_small)
 
 
 def gather_kernel(ids_ref, table_ref, out_ref, total):
@@ -688,14 +923,12 @@
 
     ctx = both_halves(context)
     cot = both_halves(cotangent)
-    w_full = lax.all_gather(w_uvqk.reshape(w_uvqk.shape[0], 4 * half), ("ha", "pb"), axis=0, tiled=True)
-    w_full = w_full.reshape(2, width, 4 * half)
-    w_final = lax.all_gather(w_out, "pb", axis=1, tiled=True)
-    w_final = lax.all_gather(w_final, "ha", axis=0, tiled=True)
+    shard = jnp.concatenate([w_uvqk.reshape(w_uvqk.shape[0], 4 * half), w_out.T], axis=1)
+    w_all = lax.all_gather(shard, ("ha", "pb"), axis=0, tiled=True).reshape(2, width, 5 * half)
     small = jnp.concatenate(
         [
             b_uvqk,
-            jnp.roll(rel_bias[:, ::-1], 1, axis=1),
+            rel_bias,
             time_bias.reshape(2, half),
             ln_out_gain.reshape(1, half),
         ],
@@ -708,34 +941,22 @@
         emb,
         ctx,
         cot,
-        w_full,
-        w_final,
+        w_all,
         small,
         ln_in_gain.reshape(1, width),
         b_out.reshape(1, width),
-    )
-    mixed_out = lax.all_to_all(
-        mixed.reshape(2, TOK_DEV, 2, half).transpose(0, 2, 1, 3).reshape(4, TOK_DEV, half),
-        ("ka", "ha"), split_axis=0, concat_axis=0, tiled=True,
-    ).reshape(row_count, half)
-    grad_rows = lax.all_to_all(
-        jnp.broadcast_to(grad_start.reshape(2, 1, TOK_DEV, width), (2, 2, TOK_DEV, width)).reshape(4, TOK_DEV, width),
-        ("ka", "ha"), split_axis=0, concat_axis=0, tiled=True,
-    ).reshape(row_count, width)
-    outgoing = lax.dot_general(hot, grad_rows, (((0,), (0,)), ((), ())), preferred_element_type=F32).astype(BF16)
-    incoming = lax.all_to_all(
-        outgoing.reshape(owners, share, width), ("pb", "ka"), split_axis=0, concat_axis=0, tiled=True
-    ).reshape(owners * share, width)
-    incoming = lax.all_gather(incoming, "ha", axis=0, tiled=True)
+        (pbs // 2, 2, 2 * width // owners),
+    )
+    incoming, grad_rows, mixed_rows, grad_w, grad_small = back(
+        place[:, None], mixed, grad_start, grad_w, grad_small
+    )
+    incoming = incoming.reshape(2 * owners * share, width)
     ids = arrived.reshape(owners, 2, share).transpose(1, 0, 2).reshape(1, 2 * owners * share)
     table_grad = scatter_rows(ids, incoming, table.shape[0])
-    grad_w = lax.psum_scatter(grad_w, "ha", scatter_dimension=0, tiled=True)
-    grad_w = lax.psum_scatter(grad_w[0], ("pb", "ka"), scatter_dimension=0, tiled=True)
-    grad_small = lax.psum(grad_small, ("pb", "ka", "ha"))
     mine = lax.dynamic_index_in_dim(grad_small, ha, 0, False)
     return (
-        mixed_out,
-        grad_rows,
+        mixed_rows.reshape(row_count, half),
+        grad_rows.reshape(row_count, width),
         table_grad,
         grad_small[:, 11].reshape(width),
         grad_w[:, : 4 * half].reshape(-1, 4, half),

time: 280 us -> 164 us (0.59)
  blocking collectives: 109 us -> 4.52 us
  waiting for transfers between devices: 72.5 us -> 23 us
  Pallas kernels: 33.9 us -> 75.5 us
  starting transfers between devices: 20.3 us -> 16.8 us
    reduce_scatter x2 -> x0, waiting for transfers between devices: 60.6 us -> none  [the longest x1 33.4 us: local_streams(): grad_w = lax.psum_scatter(grad_w, 'ha', scatter_dimension=0, tiled=True)]
    pallas_call x0 -> x1, Pallas kernels: none -> 42.3 us  [back(): pl.pallas_call(back_kernel, out_shape=(jax.ShapeDtypeStruct((2, owners, s...]
    psum x1 -> x0, blocking collectives: 40.6 us -> none  [local_streams(): grad_small = lax.psum(grad_small, ('pb', 'ka', 'ha'))]
    all_to_all x2 -> x0, blocking collectives: 32.8 us -> none  [the longest x1 19.1 us: local_streams(): lax.all_to_all(outgoing.reshape(owners, share, width), ('pb', 'ka'), spli...]
    all_gather x2 -> x0, blocking collectives: 30.9 us -> none  [the longest x1 22.7 us: local_streams(): w_final = lax.all_gather(w_out, 'pb', axis=1, tiled=True)]
    all_to_all x1, waiting for transfers between devices: 0.01 us -> 8.78 us  [local_streams(): lax.all_to_all(fetched, ('pb', 'ka'), split_axis=0, concat_axis=0, tiled=...]
    all_to_all x1 -> x0, starting transfers between devices: 3.41 us -> none  [local_streams(): lax.all_to_all(mixed.reshape(2, TOK_DEV, 2, half).transpose(0, 2, 1, 3).r...]
    unnamed x33 -> x29, local copies, waits for them, and re-layouts: 9.66 us -> 11.1 us
  transfers between devices with their start and end apart: 10 -> 6, of which waited for: 4 -> 3; matrix products, arithmetic and copies ran while one was open for 6% -> 8% of each run, Pallas kernels for 8% -> 5%
where the time goes in v2:
time: 164 us; the launch traced here: 163 us
  Pallas kernels  75.5 us (46%)
  waiting for transfers between devices  23 us (14%)
  local copies, waits for them, and re-layouts  21.6 us (13%)
  starting transfers between devices  16.8 us (10%)
  between operations  14.3 us (9%)
  other arithmetic  6.62 us (4%)
  blocking collectives  4.52 us (3%)
    pallas_call x1, Pallas kernels, back(): pl.pallas_call(back_kernel, out_shape=(jax.ShapeDtypeStruct((2, owners, s...  42.3 us
    pallas_call x1, Pallas kernels, scatter_rows(): pl.pallas_call(scatter_kernel, grid=(table_rows // tile,), out_shape=jax....  14.2 us
    pallas_call x1, Pallas kernels, layer(): pl.pallas_call(layer_kernel, out_shape=(jax.ShapeDtypeStruct((group, widt...  11.3 us
    unnamed x29, local copies, waits for them, and re-layouts  11.1 us
    all_to_all x1, waiting for transfers between devices, local_streams(): lax.all_to_all(fetched, ('pb', 'ka'), split_axis=0, concat_axis=0, tiled=...  8.78 us
    all_to_all x1, waiting for transfers between devices, local_streams(): lax.all_to_all(embedded.reshape(MB, TOK_DEV, width), ('ka', 'ha'), split_...  7.78 us
    pallas_call x1, Pallas kernels, gather_rows(): pl.pallas_call(gather_kernel, grid=(table.shape[0] // tile,), out_shape=j...  7.69 us
    all_to_all x1, starting transfers between devices, local_streams(): lax.all_to_all(requests.reshape(owners, capacity), ('pb', 'ka'), split_ax...  7.39 us
  transfers between devices with their start and end apart: 6, of which 3 were waited for; matrix products, arithmetic and copies ran while one was open for 8% of the time, Pallas kernels for 5%

profile of v2, /device:TPU:0, one launch (start us, length us, event | category | flops | bytes accessed | tf_op | source)
XLA Modules:
  0.0 163.5 jit_solution(8492763756422763327)
XLA Ops:
  7.2 0.0 copy-start
  7.2 0.0 copy-start.7
  7.2 0.0 copy-start.8
  7.2 0.0 copy-start.11
  7.2 0.0 copy-start.12
  7.2 0.0 copy-start.9
  7.2 0.0 copy-start.10
  7.3 0.0 all-gather.4.cloned.1.call-start
  7.3 1.0 copy.62
  8.3 1.4 pad_maximum_fusion.2
  9.7 0.0 all-gather.4.cloned.1.call-update
  9.8 0.7 fusion.5
  10.5 1.1 reduce-window.6
  11.6 0.2 slice_reduce_fusion
  11.8 0.8 fusion.4
  12.6 0.1 copy.49
  12.8 0.7 broadcast_multiply_fusion.1
  13.5 0.1 copy.53
  13.6 0.1 copy.52
  13.8 0.2 fusion.10
  14.0 2.6 %scatter_custom_fusion = s32[1024]{0:T(1024)S(1)} fusion(s32[512]{0:T(512)S(1)} %get-tuple-element.35, s32[512]{0:T(512)} %param.17, s32[]{:T(128)} %constant.16.clone.1), kind=kCustom, calls=%fused_computation.34 | custom fusion | bytes 4608 | tf_op jit(solution)/shard_map/scatter | solution.py:900
  16.6 0.7 all_to_all.12
  17.3 7.4 %all-to-all-start = ((s32[16,1,64]{2,1,0:T(1,128)}), s32[16,1,64]{2,1,0:T(1,128)S(1)}, u32[]{:S(2)}, u32[]{:S(2)}) async-start(s32[16,1,64]{2,1,0:T(1,128)} %all_to_all.12), calls=%async_computation | async-start | bytes 16384 | tf_op jit(solution)/shard_map/all_to_all | solution.py:901
  24.7 6.4 %all-to-all-done = s32[16,1,64]{2,1,0:T(1,128)S(1)} async-done(((s32[16,1,64]{2,1,0:T(1,128)}), s32[16,1,64]{2,1,0:T(1,128)S(1)}, u32[]{:S(2)}, u32[]{:S(2)}) %all-to-all-start) | async-done | bytes 4128 | tf_op jit(solution)/shard_map/all_to_all | solution.py:901
  31.1 0.1 dynamic-slice_reduce_fusion
  31.2 0.3 reshape.155.ids_ref
  31.4 0.0 copy-start.1
  31.4 3.4 %copy-done.1 = bf16[8192,512]{1,0:T(8,128)(2,1)S(1)} copy-done((bf16[8192,512]{1,0:T(8,128)(2,1)S(1)}, bf16[8192,512]{1,0:T(8,128)(2,1)}, u32[]{:S(2)}) %copy-start.1) | copy-done | bytes 8388632
  34.8 7.7 %shard_map.230 = bf16[512,512]{1,0:T(8,128)(2,1)} custom-call(s32[512,1]{1,0:T(8,128)S(1)} %reshape.155.ids_ref, bf16[8192,512]{1,0:T(8,128)(2,1)S(1)} %copy-done.1), custom_call_target="tpu_custom_call" | custom-call | tf_op jit(solution)/shard_map/pallas_call | solution.py:833
  42.5 3.6 %all-to-all-start.1 = ((bf16[16,32,512]{2,1,0:T(8,128)(2,1)}), bf16[16,32,512]{2,1,0:T(8,128)(2,1)S(1)}, u32[]{:S(2)}, u32[]{:S(2)}) async-start(bf16[16,32,512]{2,1,0:T(8,128)(2,1)} %bitcast.6), calls=%async_computation.1 | async-start | bytes 1048576 | tf_op jit(solution)/shard_map/all_to_all | solution.py:906
  46.1 1.9 %collective-permute-start.1 = (bf16[128,512]{1,0:T(8,128)(2,1)S(1)}, bf16[128,512]{1,0:T(8,128)(2,1)S(1)}, u32[]{:S(2)}, u32[]{:S(2)}) collective-permute-start(bf16[128,512]{1,0:T(8,128)(2,1)S(1)} %constant_dynamic-slice_fusion.2), channel_id=1, source_target_pairs={{0,2},{2,0},{1,3},{3,1},{4,6},{6,4},{5,7},{7,5},{8,10},{10,8},{9,1... | collective-permute-start | bytes 393224 | tf_op jit(solution)/shard_map/ppermute | solution.py:919
  48.0 0.3 collective-permute-start
  48.4 4.5 %all-gather.1.small_ref = f32[2,11,256]{2,1,0:T(8,128)} all-gather(f32[1,11,256]{2,1,0:T(8,128)S(1)} %maximum_bitcast_fusion), channel_id=2, replica_groups=mesh['pb'=8,'ka'=2,'ha'=2] {'ha'}, dimensions={0}, use_global_device_ids=true | all-gather | bytes 33792 | tf_op jit(solution)/shard_map/all_gather | solution.py:937
  52.9 1.2 fusion.9.lengths_ref
  54.1 0.6 fusion.8.times_ref
  54.6 0.5 broadcast.67
  55.2 0.7 reduce.12
  55.8 0.1 reshape.138
  55.9 0.1 reshape.139.ids_ref
  56.0 8.8 %all-to-all-done.1 = bf16[16,32,512]{2,1,0:T(8,128)(2,1)S(1)} async-done(((bf16[16,32,512]{2,1,0:T(8,128)(2,1)}), bf16[16,32,512]{2,1,0:T(8,128)(2,1)S(1)}, u32[]{:S(2)}, u32[]{:S(2)}) %all-to-all-start.1) | async-done | bytes 524320 | tf_op jit(solution)/shard_map/all_to_all | solution.py:906
  64.8 1.3 convolution_convert_fusion
  66.0 3.7 %all-to-all-start.2 = ((bf16[4,128,512]{2,1,0:T(8,128)(2,1)}), bf16[4,128,512]{2,1,0:T(8,128)(2,1)S(1)}, u32[]{:S(2)}, u32[]{:S(2)}) async-start(bf16[4,128,512]{2,1,0:T(8,128)(2,1)} %bitcast.8), calls=%async_computation.2 | async-start | bytes 1048576 | tf_op jit(solution)/shard_map/all_to_all | solution.py:912
  69.7 0.0 collective-permute-done.1
  69.7 0.1 broadcast_select_fusion.1
  69.8 0.0 collective-permute-done
  69.8 0.1 broadcast_select_fusion.3
  69.9 0.8 pad_maximum_fusion
  70.7 7.8 %all-to-all-done.2.emb_ref = bf16[4,128,512]{2,1,0:T(8,128)(2,1)S(1)} async-done(((bf16[4,128,512]{2,1,0:T(8,128)(2,1)}), bf16[4,128,512]{2,1,0:T(8,128)(2,1)S(1)}, u32[]{:S(2)}, u32[]{:S(2)}) %all-to-all-start.2) | async-done | bytes 524320 | tf_op jit(solution)/shard_map/all_to_all | solution.py:912
  78.5 0.8 copy-done.6
  79.3 11.3 %shard_map.231 = (bf16[256,512]{1,0:T(8,128)(2,1)}, bf16[256,512]{1,0:T(8,128)(2,1)}, bf16[2,4,2,64,1280]{4,3,2,1,0:T(8,128)(2,1)}, f32[2,16,256]{2,1,0:T(8,128)}) custom-call(s32[4]{0:T(128)} %fusion.9.lengths_ref, s32[1,256]{1,0:T(1,128)} %fusion.8.times_ref, bf16[4,128,512]{2,1,0:T(8,128)(2,1)} %copy-done.6, bf16[256,512]{1,0:T(8,128)(2,1)} %get-tuple-element.42.ctx_ref, ...), custom_call_target="tpu_custom_call" | custom-call | tf_op jit(solution)/shard_map/pallas_call | solution.py:564
  90.5 1.7 %copy-done.2 = bf16[2,4,2,64,1280]{4,3,2,1,0:T(8,128)(2,1)S(1)} copy-done((bf16[2,4,2,64,1280]{4,3,2,1,0:T(8,128)(2,1)S(1)}, bf16[2,4,2,64,1280]{4,3,2,1,0:T(8,128)(2,1)}, u32[]{:S(2)}) %copy-start.2) | copy-done | bytes 2621464
  92.3 0.9 copy-done.3
  93.2 0.9 copy-done.4
  94.2 0.8 copy-done.5
  94.9 42.3 %shard_map.232 = (bf16[2,16,32,512]{3,2,1,0:T(8,128)(2,1)S(1)}, bf16[4,128,512]{2,1,0:T(8,128)(2,1)S(1)}, bf16[4,128,256]{2,1,0:T(8,128)(2,1)S(1)}, f32[32,1280]{1,0:T(8,128)S(1)}, f32[2,16,256]{2,1,0:T(8,128)S(1)}) custom-call(s32[512,1]{1,0:T(8,128)S(1)} %get-tuple-element.30.place_ref, bf16[256,512]{1,0:T(8,128)(2,1)S(1)} %copy-done.3, ...), custom_call_target="tpu_custom_call" | custom-call | tf_op jit(solution)/shard_map/pallas_call | solution.py:777
  137.3 0.6 slice_bitcast_fusion
  137.9 0.6 fusion.11
  138.5 0.6 constant_dynamic-slice_fusion.1
  139.1 0.6 reshape.142
  139.7 0.6 dynamic-slice_bitcast_fusion
  140.3 0.7 reshape.141
  141.0 14.2 %shard_map.233 = f32[8192,512]{1,0:T(8,128)} custom-call(s32[1,1024]{1,0:T(1,128)S(1)} %reshape.139.ids_ref, bf16[1024,512]{1,0:T(8,128)(2,1)S(1)} %bitcast.53), custom_call_target="tpu_custom_call" | custom-call | tf_op jit(solution)/shard_map/pallas_call | solution.py:856
  155.2 0.7 copy.66
  155.9 0.8 copy.67
  (22 shorter events, 0.1 us)
Async XLA Ops:
  7.2 46.9 %copy-start = (s32[1,4,256]{2,1,0:T(4,128)S(1)}, s32[1,4,256]{2,1,0:T(4,128)}, u32[]{:S(2)}) copy-start(s32[1,4,256]{2,1,0:T(4,128)} %param.19) | copy-start | bytes 12292
  7.2 38.9 %copy-start.7 = (bf16[512,512]{1,0:T(8,128)(2,1)S(1)}, bf16[512,512]{1,0:T(8,128)(2,1)}, u32[]{:S(2)}) copy-start(bf16[512,512]{1,0:T(8,128)(2,1)} %param.21) | copy-start | bytes 1572868
  7.2 40.8 %copy-start.8 = (bf16[512,512]{1,0:T(8,128)(2,1)S(1)}, bf16[512,512]{1,0:T(8,128)(2,1)}, u32[]{:S(2)}) copy-start(bf16[512,512]{1,0:T(8,128)(2,1)} %param.15) | copy-start | bytes 1572868
  7.2 41.1 %copy-start.11 = (f32[4,128]{1,0:T(4,128)S(1)}, f32[4,128]{1,0:T(4,128)}, u32[]{:S(2)}) copy-start(f32[4,128]{1,0:T(4,128)} %param.26) | copy-start | bytes 6148
  7.2 41.1 %copy-start.12 = (f32[256]{0:T(256)S(1)}, f32[256]{0:T(256)}, u32[]{:S(2)}) copy-start(f32[256]{0:T(256)} %param.27) | copy-start | bytes 3076
  7.2 41.1 %copy-start.9 = (f32[4,256]{1,0:T(4,128)S(1)}, f32[4,256]{1,0:T(4,128)}, u32[]{:S(2)}) copy-start(f32[4,256]{1,0:T(4,128)} %param.25) | copy-start | bytes 12292
  7.2 41.1 %copy-start.10 = (f32[4,256]{1,0:T(4,128)S(1)}, f32[4,256]{1,0:T(4,128)}, u32[]{:S(2)}) copy-start(f32[4,256]{1,0:T(4,128)} %param.24) | copy-start | bytes 12292
  7.3 71.2 %all-gather.4.cloned.1.call-start = ((), (), s32[]{:S(2)}) async-start(), calls=%async_computation.3 | async-start | bytes 2785280 | tf_op jit(solution)/shard_map/all_gather | solution.py:927
  17.3 13.8 %all-to-all-start = ((s32[16,1,64]{2,1,0:T(1,128)}), s32[16,1,64]{2,1,0:T(1,128)S(1)}, u32[]{:S(2)}, u32[]{:S(2)}) async-start(s32[16,1,64]{2,1,0:T(1,128)} %all_to_all.12), calls=%async_computation | async-start | bytes 16384 | tf_op jit(solution)/shard_map/all_to_all | solution.py:901
  31.4 3.4 %copy-start.1 = (bf16[8192,512]{1,0:T(8,128)(2,1)S(1)}, bf16[8192,512]{1,0:T(8,128)(2,1)}, u32[]{:S(2)}) copy-start(bf16[8192,512]{1,0:T(8,128)(2,1)} %table_ref.1) | copy-start | bytes 25165828
  42.5 22.3 %all-to-all-start.1 = ((bf16[16,32,512]{2,1,0:T(8,128)(2,1)}), bf16[16,32,512]{2,1,0:T(8,128)(2,1)S(1)}, u32[]{:S(2)}, u32[]{:S(2)}) async-start(bf16[16,32,512]{2,1,0:T(8,128)(2,1)} %bitcast.6), calls=%async_computation.1 | async-start | bytes 1048576 | tf_op jit(solution)/shard_map/all_to_all | solution.py:906
  46.1 23.6 %collective-permute-start.1 = (bf16[128,512]{1,0:T(8,128)(2,1)S(1)}, bf16[128,512]{1,0:T(8,128)(2,1)S(1)}, u32[]{:S(2)}, u32[]{:S(2)}) collective-permute-start(bf16[128,512]{1,0:T(8,128)(2,1)S(1)} %constant_dynamic-slice_fusion.2), channel_id=1, source_target_pairs={{0,2},{2,0},{1,3},{3,1},{4,6},{6,4},{5,7},{7,5},{8,10},{10,8},{9,1... | collective-permute-start | bytes 393224 | tf_op jit(solution)/shard_map/ppermute | solution.py:919
  48.0 21.8 %collective-permute-start = (bf16[128,512]{1,0:T(8,128)(2,1)S(1)}, bf16[128,512]{1,0:T(8,128)(2,1)S(1)}, u32[]{:S(2)}, u32[]{:S(2)}) collective-permute-start(bf16[128,512]{1,0:T(8,128)(2,1)S(1)} %constant_dynamic-slice_fusion.3), channel_id=1, source_target_pairs={{0,2},{2,0},{1,3},{3,1},{4,6},{6,4},{5,7},{7,5},{8,10},{10,8},{9,1... | collective-permute-start | bytes 393224 | tf_op jit(solution)/shard_map/ppermute | solution.py:919
  66.0 12.4 %all-to-all-start.2 = ((bf16[4,128,512]{2,1,0:T(8,128)(2,1)}), bf16[4,128,512]{2,1,0:T(8,128)(2,1)S(1)}, u32[]{:S(2)}, u32[]{:S(2)}) async-start(bf16[4,128,512]{2,1,0:T(8,128)(2,1)} %bitcast.8), calls=%async_computation.2 | async-start | bytes 1048576 | tf_op jit(solution)/shard_map/all_to_all | solution.py:912
  78.5 0.8 copy-start.6
  90.5 1.7 %copy-start.2 = (bf16[2,4,2,64,1280]{4,3,2,1,0:T(8,128)(2,1)S(1)}, bf16[2,4,2,64,1280]{4,3,2,1,0:T(8,128)(2,1)}, u32[]{:S(2)}) copy-start(bf16[2,4,2,64,1280]{4,3,2,1,0:T(8,128)(2,1)} %get-tuple-element.22.grad_w_ref) | copy-start | bytes 7864324
  92.3 0.9 copy-start.3
  93.2 0.9 copy-start.4
  94.2 0.8 copy-start.5
Sparse Core Ops, SparseCore 0:
  11.0 52.9 all-gather.3

commit v3 on v0

--- a/solution.py
+++ b/solution.py
@@ -1,12 +1,18 @@
+import functools
+
 import jax
 import jax.numpy as jnp
 from jax import lax
+from jax.experimental import pallas as pl
+from jax.experimental.pallas import tpu as pltpu
 from jax.sharding import PartitionSpec as P
 
 DH = 64
 TOK_DEV = 128
 MB = 4
 SEQ_GRP = 4
+F32 = jnp.float32
+BF16 = jnp.bfloat16
 
 
 epsilon = 1e-05
@@ -116,7 +122,7 @@
     ).astype(jnp.bfloat16)
 
 
-def local(
+def local_general(
     context,
     item_owner,
     item_offset,
@@ -324,9 +330,794 @@
     )
 
 
+MESH = pl.DeviceIdType.MESH
+
+
+def remote(src, dst, send_sem, recv_sem, device):
+    return pltpu.make_async_remote_copy(
+        src_ref=src, dst_ref=dst, send_sem=send_sem, recv_sem=recv_sem, device_id=device, device_id_type=MESH
+    )
+
+
+def mm(a, b):
+    return jnp.dot(a, b, preferred_element_type=F32)
+
+
+def mm_nt(a, b):
+    return lax.dot_general(a, b, (((1,), (1,)), ((), ())), preferred_element_type=F32)
+
+
+def mm_tn(a, b):
+    return lax.dot_general(a, b, (((0,), (0,)), ((), ())), preferred_element_type=F32)
+
+
+def mm_exact(a, b):
+    return jnp.dot(a, b, preferred_element_type=F32, precision=lax.Precision.HIGHEST)
+
+
+def sigmoid(v):
+    return 0.5 * jnp.tanh(0.5 * v) + 0.5
+
+
+def skew(tile):
+    return pltpu.roll(tile, 0, 1, stride=1, stride_axis=0)
+
+
+def iota(shape, dim):
+    return lax.broadcasted_iota(jnp.int32, shape, dim)
+
+
+def one_hot(equal):
+    return equal.astype(F32).astype(BF16)
+
+
+def layer_norm(values):
+    centered = values - jnp.mean(values, axis=1, keepdims=True)
+    inverse = lax.rsqrt(jnp.mean(centered * centered, axis=1, keepdims=True) + epsilon)
+    return centered * inverse, inverse
+
+
+def layer_norm_back(grad_unit, unit, inverse):
+    first = jnp.mean(grad_unit, axis=1, keepdims=True)
+    second = jnp.mean(grad_unit * unit, axis=1, keepdims=True)
+    return inverse * (grad_unit - first - unit * second)
+
+
+class Place:
+    def __init__(self):
+        self.pbs, self.kas = lax.axis_size("pb"), lax.axis_size("ka")
+        self.owners, self.zs = self.pbs * self.kas, self.pbs // 2
+        self.pb, self.ka, self.ha = lax.axis_index("pb"), lax.axis_index("ka"), lax.axis_index("ha")
+        self.z, self.core = self.pb // 2, self.pb % 2
+        self.me = self.pb * self.kas + self.ka
+        self.stream = 2 * self.ka + self.ha
+        self.x_peer = (self.pb, self.ka, 1 - self.ha)
+        self.y_peer = (self.pb, 1 - self.ka, self.ha)
+        self.xy_peer = (self.pb, 1 - self.ka, 1 - self.ha)
+        self.core_peer = (2 * self.z + 1 - self.core, self.ka, self.ha)
+        self.quads = [
+            (self.x_peer, self.ka, 1 - self.ha),
+            (self.y_peer, 1 - self.ka, self.ha),
+            (self.xy_peer, 1 - self.ka, 1 - self.ha),
+        ]
+
+    def owner(self, index):
+        return (index // self.kas, index % self.kas, self.ha)
+
+    def owner_to(self, d):
+        return lax.rem(self.me + d, self.owners)
+
+    def owner_from(self, d):
+        return lax.rem(self.me - d + self.owners, self.owners)
+
+    def z_to(self, d):
+        return lax.rem(self.z + d, self.zs)
+
+    def z_device(self, d):
+        return (2 * self.z_to(d) + self.core, self.ka, self.ha)
+
+    def z_from(self, d):
+        return 2 * lax.rem(self.z - d + self.zs, self.zs) + self.core
+
+
+class Copies:
+    def __init__(self, send, recv):
+        self.send, self.recv, self.copies = send, recv, []
+
+    def start(self, src, dst, device):
+        i = len(self.copies)
+        copy = remote(src, dst, self.send.at[i], self.recv.at[i], device)
+        copy.start()
+        self.copies.append(copy)
+
+    def arrive(self, i):
+        self.copies[i].wait_recv()
+
+    def sent(self):
+        for copy in self.copies:
+            copy.wait_send()
+
+
+class WeightSum:
+    def __init__(self, at, own, first, s, name):
+        self.at, self.own, self.first = at, own, first
+        self.core_in, self.stage1, self.hop1 = s[name + "core_in"], s[name + "stage1"], s[name + "hop1"]
+        self.stage2, self.hop2, self.stage3, self.z_in = s[name + "stage2"], s[name + "hop2"], s[name + "stage3"], s[name + "z_in"]
+        self.copies = Copies(s[name + "send"], s[name + "recv"])
+
+    def cores(self):
+        self.copies.start(self.own.at[:, :, 1 - self.at.core], self.core_in, self.at.core_peer)
+
+    def hop_one(self):
+        at = self.at
+        self.copies.arrive(0)
+        for h in range(2):
+            total = self.own[h, :, at.core].astype(F32) + self.core_in[h].astype(F32)
+            self.stage1[h] = total.astype(BF16).reshape(self.stage1.shape[1:])
+        if self.first == "x":
+            self.copies.start(self.stage1.at[1 - at.ha], self.hop1, at.x_peer)
+        else:
+            self.copies.start(self.stage1.at[:, :, 1 - at.ka], self.hop1, at.y_peer)
+
+    def hop_two(self):
+        at = self.at
+        self.copies.arrive(1)
+        if self.first == "x":
+            self.stage2[...] = (self.stage1[at.ha].astype(F32) + self.hop1[...].astype(F32)).astype(BF16)
+            self.copies.start(self.stage2.at[:, 1 - at.ka], self.hop2, at.y_peer)
+        else:
+            for h in range(2):
+                self.stage2[h] = (self.stage1[h, :, at.ka].astype(F32) + self.hop1[h].astype(F32)).astype(BF16)
+            self.copies.start(self.stage2.at[1 - at.ha], self.hop2, at.x_peer)
+
+    def hop_z(self):
+        at = self.at
+        self.copies.arrive(2)
+        kept = self.stage2[:, at.ka] if self.first == "x" else self.stage2[at.ha]
+        self.stage3[...] = (kept.astype(F32) + self.hop2[...].astype(F32)).astype(BF16)
+        for d in range(1, at.zs):
+            self.copies.start(self.stage3.at[at.z_to(d)], self.z_in.at[d - 1], at.z_device(d))
+
+    def finish(self):
+        total = self.stage3[self.at.z].astype(F32)
+        for d in range(1, self.at.zs):
+            self.copies.arrive(2 + d)
+            total = total + self.z_in[d - 1].astype(F32)
+        return total
+
+
+def weight_sum_scratch(name, first, zs, block, cols):
+    dma = pltpu.SemaphoreType.DMA
+    hop1 = (zs, 2, block, cols) if first == "x" else (2, zs, block, cols)
+    return {
+        name + "own": pltpu.VMEM((2, zs, 2, 2 * block, cols), BF16),
+        name + "core_in": pltpu.VMEM((2, zs, 2 * block, cols), BF16),
+        name + "stage1": pltpu.VMEM((2, zs, 2, block, cols), BF16),
+        name + "hop1": pltpu.VMEM(hop1, BF16),
+        name + "stage2": pltpu.VMEM(hop1, BF16),
+        name + "hop2": pltpu.VMEM((zs, block, cols), BF16),
+        name + "stage3": pltpu.VMEM((zs, block, cols), BF16),
+        name + "z_in": pltpu.VMEM((zs - 1, block, cols), BF16),
+        name + "send": dma((2 + zs,)),
+        name + "recv": dma((2 + zs,)),
+    }
+
+
+def main_kernel(in_names, out_names, scratch_names, *refs):
+    names = in_names + out_names + scratch_names
+    s = dict(zip(names, refs, strict=True))
+    at = Place()
+    owners, zs, ka, ha = at.owners, at.zs, at.ka, at.ha
+    count, width = s["context"].shape
+    half = width // 2
+    tok = count // MB
+    group = 2 * tok
+    share = count // owners
+    capacity = 2 * share
+    block = s["w_uvqk"].shape[0] // 2
+    heads_half = half // 64
+    heads = 2 * heads_half
+    pairs = half // 128
+    buckets = s["time"].shape[1]
+    gates_cols = 2 * half
+
+    table, table_buf, table_sem = s["table"], s["table_buf"], s["table_sem"]
+    chunks = table_sem.shape[0]
+    chunk = table.shape[0] // chunks
+
+    def local(i, src, dst):
+        copy = pltpu.make_async_copy(src, dst, s["load_sem"].at[i])
+        copy.start()
+        return copy
+
+    mine = pl.ds(pl.multiple_of(at.stream * tok, tok), tok)
+    away = pl.ds(pl.multiple_of((2 * (1 - ka) + ha) * tok, tok), tok)
+    loads = {}
+    for i, name in enumerate(
+        ("owner", "offset", "w_uvqk", "w_out", "b", "rel", "time", "gain_out", "gain_in", "b_out", "lengths", "times")
+    ):
+        loads[name] = local(i, s[name], s[name + "_v"])
+    loads["ctx"] = local(12, s["context"].at[mine], s["ctx_v"].at[ka])
+    loads["cot"] = local(13, s["cot"].at[mine], s["cot_v"].at[ka])
+    for i in range(chunks):
+        rows = pl.ds(i * chunk, chunk)
+        pltpu.make_async_copy(table.at[rows], table_buf.at[rows], table_sem.at[i]).start()
+    barrier = pltpu.get_barrier_semaphore()
+    partners = [at.owner(at.owner_to(d)) for d in range(1, owners)] + [at.x_peer, at.xy_peer]
+    for device in partners:
+        pl.semaphore_signal(barrier, inc=1, device_id=device, device_id_type=MESH)
+
+    loads["owner"].wait()
+    loads["offset"].wait()
+    owner_row, offset_row = s["owner_v"][...], s["offset_v"][...]
+    hits = (owner_row == iota((owners, count), 0)).astype(F32)
+    earlier = mm(hits.astype(BF16), one_hot(iota((count, count), 0) < iota((count, count), 1)))
+    rank = jnp.sum(hits * earlier, axis=0, keepdims=True).astype(jnp.int32)
+    rank_hot = one_hot(rank == iota((128, count), 0))
+    high = (offset_row // 64).astype(F32)
+    low = (offset_row % 64 + 1).astype(F32)
+    asked = 64.0 * mm_nt((hits * high).astype(BF16), rank_hot) + mm_nt((hits * low).astype(BF16), rank_hot) - 1.0
+    asked = asked.astype(jnp.int32)
+    for o in range(owners):
+        s["requests"][o] = jnp.broadcast_to(asked[o : o + 1], (8, 128))
+    place = rank - ha * share
+    place = jnp.where((place >= 0) & (place < share), owner_row * share + place, -1)
+
+    shard, w, small = s["shard"], s["w"], s["small"]
+    loads["w_uvqk"].wait()
+    for g in range(4):
+        shard[:, g * half : (g + 1) * half] = s["w_uvqk_v"][:, g, :]
+    loads["w_out"].wait()
+    shard[:, 4 * half :] = s["w_out_v"][...]
+    w[ha, at.pb] = shard[...]
+    for name in ("b", "rel", "time", "gain_out"):
+        loads[name].wait()
+    small[ha, 0:4] = s["b_v"][...]
+    small[ha, 4:8] = s["rel_v"][...]
+    for i in range(2):
+        for j in range(2):
+            small[ha, 8 + i : 9 + i, j * buckets : (j + 1) * buckets] = s["time_v"][2 * i + j : 2 * i + j + 1]
+    small[ha, 10:11] = s["gain_out_v"][...]
+
+    pl.semaphore_wait(barrier, len(partners))
+
+    def copies(name):
+        return Copies(s[name + "_send"], s[name + "_recv"])
+
+    requests, arrived = s["requests"], s["arrived"]
+    req, item, emb_c, row_c, small_c = copies("req"), copies("item"), copies("emb"), copies("row"), copies("small")
+    wz, wx, wy, wc = copies("wz"), copies("wx"), copies("wy"), copies("wc")
+    for d in range(1, owners):
+        to = at.owner_to(d)
+        req.start(requests.at[to], arrived.at[at.me], at.owner(to))
+    arrived[at.me] = requests[at.me]
+    my_half = pl.ds(pl.multiple_of(ka * block, block), block)
+    for d in range(1, zs):
+        wz.start(shard.at[my_half], w.at[ha, at.pb, my_half], at.z_device(d))
+    wx.start(shard, w.at[ha, at.pb], at.x_peer)
+    small_c.start(small.at[ha], small.at[ha], at.x_peer)
+    row_c.start(s["context"].at[away], s["ctx_v"].at[ka], at.y_peer)
+    row_c.start(s["cot"].at[away], s["cot_v"].at[ka], at.y_peer)
+    wc.start(shard, w.at[ha, at.pb], at.core_peer)
+
+    for i in range(owners - 1):
+        req.arrive(i)
+    pick = iota((share, 128), 1) == iota((share, 128), 0) + ha * share
+    columns = []
+    for o in range(owners):
+        tile = jnp.broadcast_to(arrived[o, 0:1], (share, 128)).astype(F32)
+        columns.append(jnp.sum(jnp.where(pick, tile, 0.0), axis=1, keepdims=True))
+    column = jnp.concatenate(columns, axis=0).astype(jnp.int32)
+    low_lanes = iota((1, 128), 1) < capacity
+    for i in range(owners // 2):
+        first, second = arrived[2 * i, 0:1], arrived[2 * i + 1, 0:1]
+        s["ids"][:, i * 128 : (i + 1) * 128] = jnp.where(low_lanes, first, pltpu.roll(second, capacity, 1))
+    total = s["total"]
+    total[...] = jnp.zeros_like(total)
+
+    def look_up(i, carry):
+        rows = pl.ds(pl.multiple_of(i * chunk, chunk), chunk)
+        pltpu.make_async_copy(table.at[rows], table_buf.at[rows], table_sem.at[i]).wait()
+        total[...] += mm(one_hot(column == iota((owners * share, chunk), 1) + i * chunk), table_buf[rows])
+        return carry
+
+    lax.fori_loop(0, chunks // 2, look_up, 0)
+    for d in range(1, zs):
+        wz.arrive(d - 1)
+        there = w.at[ha, at.z_from(d), my_half]
+        wx.start(there, there, at.x_peer)
+        wy.start(there, there, at.y_peer)
+    lax.fori_loop(chunks // 2, chunks, look_up, 0)
+    fetched, returned, parts, emb = s["fetched"], s["returned"], s["parts"], s["emb"]
+    fetched[...] = total[...].astype(BF16).reshape(fetched.shape)
+    for d in range(1, owners):
+        to = at.owner_to(d)
+        item.start(fetched.at[to], returned.at[at.me], at.owner(to))
+    returned[at.me] = fetched[at.me]
+    wx.arrive(0)
+    there = w.at[1 - ha, at.pb]
+    wc.start(there, there, at.core_peer)
+    for d in range(1, zs):
+        wx.arrive(d)
+        there = w.at[1 - ha, at.z_from(d), my_half]
+        wy.start(there, there, at.y_peer)
+
+    loads["lengths"].wait()
+    loads["times"].wait()
+    small_c.arrive(0)
+    lane, row = iota((group, group), 1), iota((group, group), 0)
+    lengths = s["lengths_v"][pl.ds(at.stream, 1), :]
+    ends = jnp.zeros((1, 1), jnp.int32)
+    member_row = jnp.zeros((group, group), jnp.int32)
+    member_col = jnp.zeros((group, group), jnp.int32)
+    inv_count = jnp.zeros((group, group), F32)
+    for i in range(SEQ_GRP):
+        length = lengths[:, i : i + 1]
+        inside = (row >= ends) & (row < ends + length)
+        inv_count = jnp.where(inside, 1.0 / jnp.maximum(length, 1).astype(F32), inv_count)
+        ends = ends + length
+        member_row = member_row + (ends <= row).astype(jnp.int32)
+        member_col = member_col + (ends <= lane).astype(jnp.int32)
+    allowed = (member_row == member_col) & (member_row < SEQ_GRP) & (lane <= row)
+    maskscale = s["maskscale"]
+    maskscale[...] = jnp.where(allowed, inv_count, 0.0)
+    times_row = jnp.broadcast_to(s["times_v"][pl.ds(at.stream, 1), :], (group, group))
+    times_col = jnp.sum(jnp.where(lane == row, times_row, 0).astype(F32), axis=1, keepdims=True).astype(jnp.int32)
+    time_index = jnp.clip(times_col - times_row, 0, buckets - 1)
+    turn = ((lane + row) % group == 0).astype(F32)
+    rel_back = mm_exact(jnp.concatenate([small[0, 4:8, :], small[1, 4:8, :]], axis=0), turn)
+    bias = s["bias"]
+    for head in range(heads):
+        hf, head_in = divmod(head, heads_half)
+        begin = (head_in % 2) * buckets
+        bucket_row = jnp.broadcast_to(small[hf, 8 + head_in // 2 : 9 + head_in // 2, begin : begin + buckets], (group, buckets))
+        by_time = [
+            jnp.take_along_axis(bucket_row, time_index[:, c : c + buckets], axis=1, mode="promise_in_bounds")
+            for c in range(0, group, buckets)
+        ]
+        bias[head] = skew(jnp.broadcast_to(rel_back[head : head + 1], (group, group))) + jnp.concatenate(by_time, axis=1)
+
+    for i in range(owners - 1):
+        item.arrive(i)
+    slot_hot = one_hot(place == iota((count, count), 0))
+    parts[...] = mm_tn(slot_hot, returned[...].reshape(count, width)).astype(BF16).reshape(parts.shape)
+    for device, to_ka, to_ha in at.quads:
+        emb_c.start(parts.at[2 * to_ka + to_ha], emb.at[at.stream], device)
+    emb[at.stream] = parts[at.stream]
+    for d in range(1, zs):
+        wy.arrive(d - 1)
+        there = w.at[ha, at.z_from(d)]
+        wc.start(there, there, at.core_peer)
+    for d in range(1, zs):
+        wy.arrive(zs - 2 + d)
+        there = w.at[1 - ha, at.z_from(d)]
+        wc.start(there, there, at.core_peer)
+    for i in range(2 * zs):
+        wc.arrive(i)
+
+    def w_half(hf, cols):
+        return w[hf, :, :, cols].reshape(width, cols.stop - cols.start)
+
+    out_cols = slice(4 * half, 5 * half)
+    loads["cot"].wait()
+    row_c.arrive(1)
+    cot = s["cot_v"][...].reshape(group, width)
+    grad_mixed = jnp.concatenate([mm(cot, w_half(hf, out_cols)) for hf in range(2)], axis=1)
+    loads["gain_in"].wait()
+    loads["b_out"].wait()
+    loads["ctx"].wait()
+    row_c.arrive(0)
+    for i in range(3):
+        emb_c.arrive(i)
+
+    embedded = jnp.concatenate(
+        [emb[0].astype(F32) + emb[1].astype(F32), emb[2].astype(F32) + emb[3].astype(F32)], axis=0
+    )
+    start = s["ctx_v"][...].reshape(group, width).astype(F32) + embedded
+    unit_in, inv_in = layer_norm(start)
+    gain_in = s["gain_in_v"][...]
+    normed = (unit_in * gain_in).astype(BF16)
+    slope, qkv, w_att, sm = s["slope"], s["qkv"], s["w_att"], s["sm"]
+    gates = []
+    for hf in range(2):
+        for g in range(4):
+            cols = slice(g * half, (g + 1) * half)
+            pre = mm(normed, w_half(hf, cols)) + small[hf, g : g + 1, :]
+            sig = sigmoid(pre)
+            act = pre * sig
+            slope[hf, :, cols] = sig + act * (1.0 - sig)
+            if g == 0:
+                gates.append(act)
+            else:
+                qkv[hf, g - 1] = (act * 0.125 if g == 2 else act).astype(BF16)
+    gate = jnp.concatenate(gates, axis=1)
+    low_half = iota((group, 128), 1) < 64
+
+    def split(tile):
+        zero = jnp.zeros_like(tile)
+        return jnp.where(low_half, tile, zero), jnp.where(low_half, zero, tile)
+
+    attended = []
+    for hf in range(2):
+        for pair in range(pairs):
+            cols = slice(pair * 128, (pair + 1) * 128)
+            values, queries = split(qkv[hf, 0, :, cols]), split(qkv[hf, 1, :, cols])
+            keys = qkv[hf, 2, :, cols]
+            both = None
+            for sub in range(2):
+                head = hf * heads_half + pair * 2 + sub
+                scores = mm_nt(queries[sub], keys) + bias[head]
+                sig = sigmoid(scores)
+                act = scores * sig
+                weights = (act * maskscale[...]).astype(BF16)
+                w_att[head] = weights
+                sm[head] = (sig + act * (1.0 - sig)) * maskscale[...]
+                part = mm(weights, values[sub])
+                both = part if both is None else both + part
+            attended.append(both)
+    unit_out, inv_out = layer_norm(jnp.concatenate(attended, axis=1))
+    gain_out = jnp.concatenate([small[0, 10:11, :], small[1, 10:11, :]], axis=1)
+    mixed_in = (unit_out * gain_out * gate).astype(BF16)
+    projected = None
+    for hf in range(2):
+        part = mm_nt(mixed_in[:, hf * half : (hf + 1) * half], w_half(hf, out_cols))
+        projected = part if projected is None else projected + part
+    mixed, mixed_rows = s["mixed"], s["mixed_rows"]
+    mixed[...] = (projected + s["b_out_v"][...] + start).astype(BF16)
+    mixed_c = copies("mixed")
+    for device, to_ka, to_ha in at.quads:
+        here = mixed.at[pl.ds(to_ka * tok, tok), pl.ds(pl.multiple_of(to_ha * half, half), half)]
+        mixed_c.start(here, mixed_rows.at[at.stream], device)
+    own_rows = pl.ds(pl.multiple_of(ka * tok, tok), tok)
+    mixed_rows[at.stream] = mixed[own_rows, pl.ds(pl.multiple_of(ha * half, half), half)]
+
+    grad_pre, grad_small = s["grad_pre"], s["grad_small"]
+    grad_raw = grad_mixed * unit_out
+    grad_gate = grad_raw * gain_out
+    grad_gain_out = jnp.sum(grad_raw * gate, axis=0, keepdims=True)
+    grad_att = layer_norm_back(grad_mixed * gate * gain_out, unit_out, inv_out).astype(BF16)
+    sum_a = WeightSum(at, s["a_own"], "x", s, "a_")
+    sums_b = [WeightSum(at, s[f"b{i}_own"], "y", s, f"b{i}_") for i in range(pairs)]
+
+    def put(own, hf, first, value):
+        cols = value.shape[1]
+        own[hf, :, :, :, first : first + cols] = value.astype(BF16).reshape(own.shape[1:4] + (cols,))
+
+    for hf in range(2):
+        cols = slice(hf * half, (hf + 1) * half)
+        grad_pre[hf, :, 0:half] = (grad_gate[:, cols] * slope[hf, :, 0:half]).astype(BF16)
+        grad_small[hf, 10:11, :] = grad_gain_out[:, cols]
+        put(s["a_own"], hf, 0, mm_tn(normed, grad_pre[hf, :, 0:half]))
+        put(s["a_own"], hf, half, mm_tn(cot, mixed_in[:, cols]))
+    sum_a.cores()
+
+    gs = s["gs"]
+    for pair in range(pairs):
+        for hf in range(2):
+            cols = slice(pair * 128, (pair + 1) * 128)
+            values = qkv[hf, 0, :, cols]
+            queries, keys = split(qkv[hf, 1, :, cols]), split(qkv[hf, 2, :, cols])
+            grads = split(grad_att[:, hf * half + pair * 128 : hf * half + (pair + 1) * 128])
+            sums = None
+            for sub in range(2):
+                head = hf * heads_half + pair * 2 + sub
+                grad_scores = (mm_nt(grads[sub], values) * sm[head]).astype(BF16)
+                gs[:, head * group : (head + 1) * group] = grad_scores
+                found = (
+                    mm_tn(w_att[head], grads[sub]),
+                    mm(grad_scores, keys[sub]),
+                    mm_tn(grad_scores, queries[sub]),
+                )
+                sums = found if sums is None else [a + b for a, b in zip(sums, found)]
+            for g, part in ((1, sums[0]), (2, sums[1] * 0.125), (3, sums[2])):
+                there = slice(g * half + pair * 128, g * half + (pair + 1) * 128)
+                grad_pre[hf, :, there] = (part * slope[hf, :, there]).astype(BF16)
+        if pair == 0:
+            sum_a.hop_one()
+        if pair < pairs - 1:
+            for hf in range(2):
+                for g in range(1, 4):
+                    there = slice(g * half + pair * 128, g * half + (pair + 1) * 128)
+                    put(s[f"b{pair}_own"], hf, (g - 1) * 128, mm_tn(normed, grad_pre[hf, :, there]))
+            sums_b[pair].cores()
+    grad_normed = None
+    for hf in range(2):
+        part = mm_nt(grad_pre[hf], w_half(hf, slice(0, 4 * half)))
+        grad_normed = part if grad_normed is None else grad_normed + part
+    cot32 = cot.astype(F32)
+    grad_start, grad_rows = s["grad_start"], s["grad_rows"]
+    grad_start[...] = (cot32 + layer_norm_back(grad_normed * gain_in, unit_in, inv_in)).astype(BF16)
+    back_c = copies("back")
+    for device, to_ka, to_ha in at.quads:
+        back_c.start(grad_start.at[pl.ds(to_ka * tok, tok)], grad_rows.at[at.stream], device)
+    grad_rows[at.stream] = grad_start[own_rows]
+    for hf in range(2):
+        for g in range(1, 4):
+            there = slice(g * half + (pairs - 1) * 128, g * half + pairs * 128)
+            put(s[f"b{pairs - 1}_own"], hf, (g - 1) * 128, mm_tn(normed, grad_pre[hf, :, there]))
+    sums_b[-1].cores()
+    for i in range(pairs - 1):
+        sums_b[i].hop_one()
+    gain_grad = jnp.sum(grad_normed * unit_in, axis=0, keepdims=True)
+    bout_grad = jnp.sum(cot32, axis=0, keepdims=True)
+    for hf in range(2):
+        sums = jnp.sum(grad_pre[hf].astype(F32), axis=0, keepdims=True)
+        for g in range(4):
+            grad_small[hf, g : g + 1, :] = sums[:, g * half : (g + 1) * half]
+        grad_small[hf, 11:12, :] = gain_grad[:, hf * half : (hf + 1) * half]
+        grad_small[hf, 12:13, :] = bout_grad[:, hf * half : (hf + 1) * half]
+        grad_small[hf, 13:16, :] = jnp.zeros((3, half), F32)
+    flip = (lane + row == group - 1).astype(F32)
+    kept_pairs = lane + row <= group - 1
+    hot_cols = one_hot(times_row == row)
+    hot_back = one_hot(times_row == group - 1 - row)
+    folded = mm(jnp.concatenate([flip.astype(BF16), hot_back], axis=0), gs[...])
+    rel_rows, time_rows, early_rows = [], [], []
+    for head in range(heads):
+        places = slice(head * group, (head + 1) * group)
+        rel_rows.append(jnp.sum(skew(folded[:group, places]), axis=0, keepdims=True))
+        pairs_sum = mm_nt(folded[group:, places].astype(BF16), hot_cols)
+        kept = jnp.where(kept_pairs, pairs_sum, 0.0)
+        time_rows.append(jnp.sum(skew(kept), axis=0, keepdims=True))
+        early_rows.append(jnp.sum(pairs_sum - kept, axis=0, keepdims=True))
+    flipped = mm_exact(jnp.concatenate(rel_rows + time_rows, axis=0), flip)
+    early = jnp.sum(jnp.concatenate(early_rows, axis=0), axis=1, keepdims=True)
+    late = jnp.sum(flipped[heads:, buckets:], axis=1, keepdims=True)
+    place_in = iota((heads, buckets), 1)
+    time_grad = flipped[heads:, :buckets] + jnp.where(place_in == 0, early, 0.0) + jnp.where(place_in == buckets - 1, late, 0.0)
+    for head in range(heads):
+        hf, head_in = divmod(head, heads_half)
+        begin = (head_in % 2) * buckets
+        grad_small[hf, 4 + head_in : 5 + head_in, :] = flipped[head : head + 1]
+        grad_small[hf, 8 + head_in // 2 : 9 + head_in // 2, begin : begin + buckets] = time_grad[head : head + 1]
+    small_in, small_mine = s["small_in"], s["small_mine"]
+    sum_c = copies("sum")
+    sum_c.start(grad_small, small_in.at[0], at.core_peer)
+    sum_a.hop_two()
+
+    for i in range(3):
+        back_c.arrive(i)
+    outgoing, incoming = s["outgoing"], s["incoming"]
+    slot_hot = one_hot(place == iota((count, count), 0))
+    outgoing[...] = mm(slot_hot, grad_rows[...].reshape(count, width)).astype(BF16).reshape(outgoing.shape)
+    give, hand = copies("give"), copies("hand")
+    for d in range(1, owners):
+        to = at.owner_to(d)
+        give.start(outgoing.at[to], incoming.at[at.me, ha], at.owner(to))
+    incoming[at.me, ha] = outgoing[at.me]
+    hand.start(incoming.at[at.me, ha], incoming.at[at.me, ha], at.x_peer)
+
+    def take(first, last):
+        for d in range(first, last):
+            give.arrive(d - 1)
+            there = incoming.at[at.owner_from(d), ha]
+            hand.start(there, there, at.x_peer)
+
+    third = owners // 3
+    sums_b[-1].hop_one()
+    sum_c.arrive(0)
+    small_mine[0] = grad_small[...] + small_in[0]
+    sum_c.start(small_mine.at[0], small_in.at[1], at.x_peer)
+    for i in range(pairs - 1):
+        sums_b[i].hop_two()
+    sum_a.hop_z()
+    take(1, third)
+    sums_b[-1].hop_two()
+    sum_c.arrive(1)
+    small_mine[1] = small_mine[0] + small_in[1]
+    sum_c.start(small_mine.at[1], small_in.at[2], at.y_peer)
+    for i in range(pairs - 1):
+        sums_b[i].hop_z()
+    take(third, 2 * third)
+    sum_c.arrive(2)
+    small_mine[2] = small_mine[1] + small_in[2]
+    for d in range(1, zs):
+        sum_c.start(small_mine.at[2], small_in.at[2 + d], at.z_device(d))
+    sums_b[-1].hop_z()
+    take(2 * third, owners)
+    grad_w = s["grad_w"]
+    grad_w[:, 0:gates_cols] = sum_a.finish()
+    for i in range(pairs):
+        first = gates_cols + i * 384
+        grad_w[:, first : first + 384] = sums_b[i].finish()
+    summed = small_mine[2]
+    for d in range(1, zs):
+        sum_c.arrive(2 + d)
+        summed = summed + small_in[2 + d]
+    s["small_sum"][...] = summed
+    for i in range(3):
+        mixed_c.arrive(i)
+    for i in range(owners):
+        hand.arrive(i)
+    for kind in (req, item, emb_c, row_c, small_c, wz, wx, wy, wc, mixed_c, back_c, give, hand, sum_c):
+        kind.sent()
+    for part in [sum_a] + sums_b:
+        part.copies.sent()
+
+
+def run_main(inputs):
+    pbs, kas = lax.axis_size("pb"), lax.axis_size("ka")
+    owners, zs = pbs * kas, pbs // 2
+    count, width = inputs["context"].shape
+    half, tok, share = width // 2, count // MB, count // owners
+    group, heads = 2 * tok, width // 64
+    shard_rows = inputs["w_uvqk"].shape[0]
+    block = shard_rows // 2
+    dma = pltpu.SemaphoreType.DMA
+    outs = {
+        "incoming": jax.ShapeDtypeStruct((owners, 2, share, width), BF16),
+        "ids": jax.ShapeDtypeStruct((1, 2 * count), jnp.int32),
+        "grad_rows": jax.ShapeDtypeStruct((MB, tok, width), BF16),
+        "mixed_rows": jax.ShapeDtypeStruct((MB, tok, half), BF16),
+        "grad_w": jax.ShapeDtypeStruct((block, 5 * half), F32),
+        "small_sum": jax.ShapeDtypeStruct((2, 16, half), F32),
+    }
+    scratch = {
+        "ctx_v": pltpu.VMEM((2, tok, width), BF16),
+        "cot_v": pltpu.VMEM((2, tok, width), BF16),
+        "requests": pltpu.VMEM((owners, 8, 128), jnp.int32),
+        "arrived": pltpu.VMEM((owners, 8, 128), jnp.int32),
+        "table_buf": pltpu.VMEM(inputs["table"].shape, BF16),
+        "total": pltpu.VMEM((count, width), F32),
+        "fetched": pltpu.VMEM((owners, share, width), BF16),
+        "returned": pltpu.VMEM((owners, share, width), BF16),
+        "parts": pltpu.VMEM((MB, tok, width), BF16),
+        "emb": pltpu.VMEM((MB, tok, width), BF16),
+        "shard": pltpu.VMEM((shard_rows, 5 * half), BF16),
+        "w": pltpu.VMEM((2, pbs, shard_rows, 5 * half), BF16),
+        "small": pltpu.VMEM((2, 16, half), F32),
+        "maskscale": pltpu.VMEM((group, group), F32),
+        "bias": pltpu.VMEM((heads, group, group), F32),
+        "slope": pltpu.VMEM((2, group, 4 * half), F32),
+        "qkv": pltpu.VMEM((2, 3, group, half), BF16),
+        "w_att": pltpu.VMEM((heads, group, group), BF16),
+        "sm": pltpu.VMEM((heads, group, group), F32),
+        "gs": pltpu.VMEM((group, heads * group), BF16),
+        "grad_pre": pltpu.VMEM((2, group, 4 * half), BF16),
+        "mixed": pltpu.VMEM((group, width), BF16),
+        "grad_start": pltpu.VMEM((group, width), BF16),
+        "grad_small": pltpu.VMEM((2, 16, half), F32),
+        "outgoing": pltpu.VMEM((owners, share, width), BF16),
+        "small_mine": pltpu.VMEM((3, 2, 16, half), F32),
+        "small_in": pltpu.VMEM((2 + zs, 2, 16, half), F32),
+        "load_sem": dma((14,)),
+        "table_sem": dma((8,)),
+    }
+    for name in ("owner", "offset", "w_uvqk", "w_out", "b", "rel", "time", "gain_out", "gain_in", "b_out", "lengths", "times"):
+        scratch[name + "_v"] = pltpu.VMEM(inputs[name].shape, inputs[name].dtype)
+    for name, number in (
+        ("req", owners - 1), ("item", owners - 1), ("emb", 3), ("row", 2), ("small", 1), ("wz", zs - 1), ("wx", zs),
+        ("wy", 2 * zs - 2), ("wc", 2 * zs), ("mixed", 3), ("back", 3), ("give", owners - 1), ("hand", owners), ("sum", 2 + zs),
+    ):
+        scratch[name + "_send"] = dma((number,))
+        scratch[name + "_recv"] = dma((number,))
+    scratch |= weight_sum_scratch("a_", "x", zs, block, 2 * half)
+    for i in range(half // 128):
+        scratch |= weight_sum_scratch(f"b{i}_", "y", zs, block, 384)
+    vmem = pl.BlockSpec(memory_space=pltpu.VMEM)
+    found = pl.pallas_call(
+        functools.partial(main_kernel, tuple(inputs), tuple(outs), tuple(scratch)),
+        out_shape=tuple(outs.values()),
+        in_specs=[pl.BlockSpec(memory_space=pltpu.HBM)] * len(inputs),
+        out_specs=(vmem,) * len(outs),
+        scratch_shapes=list(scratch.values()),
+        compiler_params=pltpu.CompilerParams(
+            collective_id=1, has_side_effects=True, vmem_limit_bytes=58 * 1024 * 1024
+        ),
+    )(*inputs.values())
+    return dict(zip(outs, found, strict=True))
+
+
+def scatter_kernel(ids_ref, rows_ref, grad_w_ref, small_ref, out_ref, w_ref, w_out_ref, b_ref, rel_ref, time_ref, gain_in_ref, gain_out_ref, b_out_ref):
+    tile = out_ref.shape[0]
+    row = iota((tile, ids_ref.shape[1]), 0) + pl.program_id(0) * tile
+    out_ref[...] = mm(one_hot(ids_ref[...] == row), rows_ref[...])
+
+    @pl.when(pl.program_id(0) == 0)
+    def _():
+        half = w_ref.shape[2]
+        buckets = time_ref.shape[1]
+        w_ref[:, 0, :] = grad_w_ref[:, 0:half]
+        w_out_ref[...] = grad_w_ref[:, half : 2 * half]
+        for pair in range(half // 128):
+            for g in range(1, 4):
+                first = 2 * half + pair * 384 + (g - 1) * 128
+                w_ref[:, g, pair * 128 : (pair + 1) * 128] = grad_w_ref[:, first : first + 128]
+        ha = lax.axis_index("ha")
+        b_ref[...] = small_ref[ha, 0:4, :]
+        rel_ref[...] = small_ref[ha, 4:8, :]
+        for i in range(2):
+            for j in range(2):
+                time_ref[2 * i + j : 2 * i + j + 1, :] = small_ref[ha, 8 + i : 9 + i, j * buckets : (j + 1) * buckets]
+        gain_out_ref[...] = small_ref[ha, 10:11, :]
+        for hf in range(2):
+            gain_in_ref[:, hf * half : (hf + 1) * half] = small_ref[hf, 11:12, :]
+            b_out_ref[:, hf * half : (hf + 1) * half] = small_ref[hf, 12:13, :]
+
+
+def scatter_rows(ids, rows, grad_w, small, table_rows, buckets, tile=512):
+    count, width = rows.shape
+    half, block = width // 2, grad_w.shape[0]
+
+    def whole(shape):
+        return pl.BlockSpec(shape, lambda i: (0,) * len(shape))
+
+    shapes = [(block, 4, half), (block, half), (4, half), (4, half), (4, buckets), (1, width), (1, half), (1, width)]
+    return pl.pallas_call(
+        scatter_kernel,
+        grid=(table_rows // tile,),
+        out_shape=[jax.ShapeDtypeStruct(shape, F32) for shape in [(table_rows, width)] + shapes],
+        in_specs=[whole((1, count)), whole((count, width)), whole(grad_w.shape), whole(small.shape)],
+        out_specs=[pl.BlockSpec((tile, width), lambda i: (i, 0))] + [whole(shape) for shape in shapes],
+        compiler_params=pltpu.CompilerParams(vmem_limit_bytes=40 * 1024 * 1024),
+    )(ids, rows, grad_w, small)
+
+
+def local_streams(
+    context,
+    item_owner,
+    item_offset,
+    lengths,
+    times,
+    table,
+    cotangent,
+    ln_in_gain,
+    w_uvqk,
+    b_uvqk,
+    rel_bias,
+    time_bias,
+    ln_out_gain,
+    w_out,
+    b_out,
+):
+    row_count, width = context.shape
+    half = width // 2
+    found = run_main(
+        {
+            "owner": item_owner.reshape(1, row_count),
+            "offset": item_offset.reshape(1, row_count),
+            "context": context,
+            "cot": cotangent,
+            "table": table,
+            "w_uvqk": w_uvqk,
+            "w_out": w_out.T,
+            "b": b_uvqk,
+            "rel": rel_bias,
+            "time": time_bias,
+            "gain_out": ln_out_gain.reshape(1, half),
+            "gain_in": ln_in_gain.reshape(1, width),
+            "b_out": b_out.reshape(1, width),
+            "lengths": lengths[0],
+            "times": times[0],
+        }
+    )
+    table_grad, grad_w, grad_w_out, grad_b, grad_rel, grad_time, grad_gain_in, grad_gain_out, grad_b_out = scatter_rows(
+        found["ids"],
+        found["incoming"].reshape(2 * row_count, width),
+        found["grad_w"],
+        found["small_sum"],
+        table.shape[0],
+        time_bias.shape[1],
+    )
+    return (
+        found["mixed_rows"].reshape(row_count, half),
+        found["grad_rows"].reshape(row_count, width),
+        table_grad,
+        grad_gain_in.reshape(width),
+        grad_w,
+        grad_b,
+        grad_rel,
+        grad_time,
+        grad_gain_out.reshape(half),
+        grad_w_out.T,
+        grad_b_out.reshape(width),
+    )
+
+
 def solution(mesh):
+    one_stream = mesh.shape["ka"] * mesh.shape["ha"] == MB and mesh.shape["ka"] == 2
     return jax.shard_map(
-        local,
+        local_streams if one_stream else local_general,
         mesh=mesh,
         in_specs=(
             P(("pb", "ka"), None),

time: 593 us -> 108 us (0.18)
  matrix products: 132 us -> 0 us
  blocking collectives: 125 us -> 0 us
  other arithmetic: 112 us -> 0 us
  Pallas kernels: 0 us -> 99.5 us
  waiting for transfers between devices: 91.2 us -> 0 us
  local copies, waits for them, and re-layouts: 89.8 us -> 7.11 us
  starting transfers between devices: 19.9 us -> 0 us
  between operations: 16.6 us -> 0.68 us
    dot_general x56 -> x0, matrix products: 132 us -> none  [the longest x4 41.4 us: bucket_lookup(): jnp.einsum('phb,qkb->phqk', jnp.stack([high, middle, lowest]), bucket_hot...]
    pallas_call x0 -> x2, Pallas kernels: none -> 99.5 us  [the longest x1 85.2 us: run_main(): pl.pallas_call(functools.partial(main_kernel, tuple(inputs), tuple(outs),...]
    psum x5 -> x0, blocking collectives: 85.9 us -> none  [the longest x1 64.7 us: local(): lax.psum((grad_gain_in, grad_bias_proj, grad_rel, grad_time, grad_gain_ou...]
    reduce_scatter x10 -> x0, waiting for transfers between devices: 59.8 us -> none  [the longest x1 41.1 us: local(): lax.psum_scatter(local_pair[1], ('pb', 'ka'), scatter_dimension=1, tiled=...]
    all_gather x5 -> x0, blocking collectives: 39.5 us -> none  [the longest x4 24.1 us: local(): lax.all_gather(jnp.stack([key_rows, values]), 'ka', axis=1, tiled=True)]
    eq x4 -> x0, other arithmetic: 24 us -> none  [tile_scores(): time_index[:, :, None]]
    reduce_sum x25 -> x0, other arithmetic: 23.9 us -> none  [the longest x4 9.07 us: local(): jnp.sum(grad_pre.astype(jnp.float32), axis=0)]
    another operation x21 -> x0, local copies, waits for them, and re-layouts: 20.8 us -> none  [the longest x8 11 us: local(): jnp.stack([key_part.reshape(group, half_cols), value_part.reshape(group,...]
  transfers between devices with their start and end apart: 16 -> 0, of which waited for: 7 -> 0; matrix products, arithmetic and copies ran while one was open for 40% -> 0% of each run, Pallas kernels for 0% -> 0%
where the time goes in v3:
time: 108 us; the launch traced here: 107 us
  Pallas kernels  99.5 us (92%)
  local copies, waits for them, and re-layouts  7.11 us (7%)
    pallas_call x1, Pallas kernels, run_main(): pl.pallas_call(functools.partial(main_kernel, tuple(inputs), tuple(outs),...  85.2 us
    pallas_call x1, Pallas kernels, scatter_rows(): pl.pallas_call(scatter_kernel, grid=(table_rows // tile,), out_shape=[jax...  14.3 us
    unnamed x10, local copies, waits for them, and re-layouts  7.11 us

profile of v3, /device:TPU:0, one launch (start us, length us, event | category | flops | bytes accessed | tf_op | source)
XLA Modules:
  0.0 107.3 jit_solution(12837715112546879456)
XLA Ops:
  0.6 85.2 %shard_map.230 = (bf16[16,2,32,512]{3,2,1,0:T(8,128)(2,1)}, s32[1,1024]{1,0:T(1,128)}, bf16[4,128,512]{2,1,0:T(8,128)(2,1)}, bf16[4,128,256]{2,1,0:T(8,128)(2,1)...) custom-call(s32[1,512]{1,0:T(1,128)} %bitcast.20, s32[1,512]{1,0:T(1,128)} %bitcast.21, bf16[512,512]{1,0:T(8,128)(2,1)} %refs_2_.1, ...), custom_call_target="tpu_custom_call" | custom-call | tf_op jit(solution)/shard_map/pallas_call | solution.py:998
  85.8 0.0 copy-start
  85.8 1.2 %copy-done = bf16[16,2,32,512]{3,2,1,0:T(8,128)(2,1)S(1)} copy-done((bf16[16,2,32,512]{3,2,1,0:T(8,128)(2,1)S(1)}, bf16[16,2,32,512]{3,2,1,0:T(8,128)(2,1)}, u32[]{:S(2)}) %copy-start) | copy-done | bytes 1048600
  87.1 0.0 copy-start.1
  87.1 0.9 copy-done.1
  88.0 0.0 copy-start.2
  88.0 0.8 copy-done.2
  88.7 0.0 copy-start.3
  88.7 0.7 copy-done.3
  89.4 14.3 %shard_map.231 = (f32[8192,512]{1,0:T(8,128)}, f32[32,4,256]{2,1,0:T(4,128)}, f32[32,256]{1,0:T(8,128)}, f32[4,256]{1,0:T(4,128)}, f32[4,256]{1,0:T(4,128)}, /*i...) custom-call(s32[1,1024]{1,0:T(1,128)S(1)} %copy-done.3, ...), custom_call_target="tpu_custom_call" | custom-call | tf_op jit(solution)/shard_map/pallas_call | solution.py:1046
  103.7 1.7 %copy.28 = bf16[512,256]{1,0:T(8,128)(2,1)} copy(bf16[512,256]{1,0:T(8,128)(2,1)} %bitcast.17) | data formatting | bytes 524288
  105.4 1.9 %copy.29 = bf16[512,512]{1,0:T(8,128)(2,1)} copy(bf16[512,512]{1,0:T(8,128)(2,1)} %bitcast.16) | data formatting | bytes 1048576
Async XLA Ops:
  85.8 1.2 %copy-start = (bf16[16,2,32,512]{3,2,1,0:T(8,128)(2,1)S(1)}, bf16[16,2,32,512]{3,2,1,0:T(8,128)(2,1)}, u32[]{:S(2)}) copy-start(bf16[16,2,32,512]{3,2,1,0:T(8,128)(2,1)} %get-tuple-element.29) | copy-start | bytes 3145732
  87.1 0.9 copy-start.1
  88.0 0.8 copy-start.2
  88.7 0.7 copy-start.3

commit v4 on v3

--- a/solution.py
+++ b/solution.py
@@ -439,73 +439,81 @@
 
 
 class WeightSum:
-    def __init__(self, at, own, first, s, name):
-        self.at, self.own, self.first = at, own, first
-        self.core_in, self.stage1, self.hop1 = s[name + "core_in"], s[name + "stage1"], s[name + "hop1"]
-        self.stage2, self.hop2, self.stage3, self.z_in = s[name + "stage2"], s[name + "hop2"], s[name + "stage3"], s[name + "z_in"]
+    def __init__(self, at, order, s, name):
+        self.at, self.order = at, order
+        self.own, self.core_in = s[name + "own"], s[name + "core_in"]
+        self.mine = [s[f"{name}mine{i}"] for i in range(3)]
+        self.other = [s[f"{name}other{i}"] for i in range(3)]
         self.copies = Copies(s[name + "send"], s[name + "recv"])
+        self.begun = [0]
+
+    def pick(self, ref, axis, index):
+        left = [a for a in "xzy" if a not in self.order[: self.order.index(axis)]]
+        return ref.at[(slice(None),) * left.index(axis) + (index,)]
+
+    def peers(self, axis):
+        at = self.at
+        if axis == "x":
+            return [(at.x_peer, 1 - at.ha)]
+        if axis == "y":
+            return [(at.y_peer, 1 - at.ka)]
+        return [(at.z_device(d), at.z_to(d)) for d in range(1, at.zs)]
+
+    def own_index(self, axis):
+        return {"x": self.at.ha, "y": self.at.ka, "z": self.at.z}[axis]
 
     def cores(self):
         self.copies.start(self.own.at[:, :, 1 - self.at.core], self.core_in, self.at.core_peer)
 
-    def hop_one(self):
-        at = self.at
-        self.copies.arrive(0)
-        for h in range(2):
-            total = self.own[h, :, at.core].astype(F32) + self.core_in[h].astype(F32)
-            self.stage1[h] = total.astype(BF16).reshape(self.stage1.shape[1:])
-        if self.first == "x":
-            self.copies.start(self.stage1.at[1 - at.ha], self.hop1, at.x_peer)
+    def send(self, i):
+        axis = self.order[i]
+        self.begun.append(len(self.copies.copies))
+        for k, (device, index) in enumerate(self.peers(axis)):
+            self.copies.start(self.pick(self.mine[i], axis, index), self.other[i].at[k], device)
+
+    def received(self, i):
+        axis = self.order[i]
+        total = self.pick(self.mine[i], axis, self.own_index(axis))[...].astype(F32)
+        for k in range(len(self.peers(axis))):
+            self.copies.arrive(self.begun[i + 1] + k)
+            total = total + self.other[i][k].astype(F32)
+        return total
+
+    def hop(self, i):
+        if i == 0:
+            self.copies.arrive(0)
+            for h in range(2):
+                total = self.own[h, :, self.at.core].astype(F32) + self.core_in[h].astype(F32)
+                self.mine[0][h] = total.astype(BF16).reshape(self.mine[0].shape[1:])
         else:
-            self.copies.start(self.stage1.at[:, :, 1 - at.ka], self.hop1, at.y_peer)
-
-    def hop_two(self):
-        at = self.at
-        self.copies.arrive(1)
-        if self.first == "x":
-            self.stage2[...] = (self.stage1[at.ha].astype(F32) + self.hop1[...].astype(F32)).astype(BF16)
-            self.copies.start(self.stage2.at[:, 1 - at.ka], self.hop2, at.y_peer)
-        else:
-            for h in range(2):
-                self.stage2[h] = (self.stage1[h, :, at.ka].astype(F32) + self.hop1[h].astype(F32)).astype(BF16)
-            self.copies.start(self.stage2.at[1 - at.ha], self.hop2, at.x_peer)
-
-    def hop_z(self):
-        at = self.at
-        self.copies.arrive(2)
-        kept = self.stage2[:, at.ka] if self.first == "x" else self.stage2[at.ha]
-        self.stage3[...] = (kept.astype(F32) + self.hop2[...].astype(F32)).astype(BF16)
-        for d in range(1, at.zs):
-            self.copies.start(self.stage3.at[at.z_to(d)], self.z_in.at[d - 1], at.z_device(d))
+            self.mine[i][...] = self.received(i - 1).astype(BF16)
+        self.send(i)
 
     def finish(self):
-        total = self.stage3[self.at.z].astype(F32)
-        for d in range(1, self.at.zs):
-            self.copies.arrive(2 + d)
-            total = total + self.z_in[d - 1].astype(F32)
-        return total
-
-
-def weight_sum_scratch(name, first, zs, block, cols):
+        return self.received(2)
+
+
+def weight_sum_scratch(name, order, zs, block, cols):
     dma = pltpu.SemaphoreType.DMA
-    hop1 = (zs, 2, block, cols) if first == "x" else (2, zs, block, cols)
-    return {
+    sizes = {"x": 2, "z": zs, "y": 2}
+    found = {
         name + "own": pltpu.VMEM((2, zs, 2, 2 * block, cols), BF16),
         name + "core_in": pltpu.VMEM((2, zs, 2 * block, cols), BF16),
-        name + "stage1": pltpu.VMEM((2, zs, 2, block, cols), BF16),
-        name + "hop1": pltpu.VMEM(hop1, BF16),
-        name + "stage2": pltpu.VMEM(hop1, BF16),
-        name + "hop2": pltpu.VMEM((zs, block, cols), BF16),
-        name + "stage3": pltpu.VMEM((zs, block, cols), BF16),
-        name + "z_in": pltpu.VMEM((zs - 1, block, cols), BF16),
-        name + "send": dma((2 + zs,)),
-        name + "recv": dma((2 + zs,)),
     }
+    for i, axis in enumerate(order):
+        before = [sizes[a] for a in "xzy" if a not in order[:i]]
+        after = [sizes[a] for a in "xzy" if a not in order[: i + 1]]
+        found[f"{name}mine{i}"] = pltpu.VMEM((*before, block, cols), BF16)
+        found[f"{name}other{i}"] = pltpu.VMEM((sizes[axis] - 1, *after, block, cols), BF16)
+    found[name + "send"] = dma((2 + zs,))
+    found[name + "recv"] = dma((2 + zs,))
+    return found
 
 
 def main_kernel(in_names, out_names, scratch_names, *refs):
     names = in_names + out_names + scratch_names
     s = dict(zip(names, refs, strict=True))
+    s["limit_rows"] = 256
     at = Place()
     owners, zs, ka, ha = at.owners, at.zs, at.ka, at.ha
     count, width = s["context"].shape
@@ -602,38 +610,43 @@
 
     for i in range(owners - 1):
         req.arrive(i)
-    pick = iota((share, 128), 1) == iota((share, 128), 0) + ha * share
-    columns = []
-    for o in range(owners):
-        tile = jnp.broadcast_to(arrived[o, 0:1], (share, 128)).astype(F32)
-        columns.append(jnp.sum(jnp.where(pick, tile, 0.0), axis=1, keepdims=True))
-    column = jnp.concatenate(columns, axis=0).astype(jnp.int32)
-    low_lanes = iota((1, 128), 1) < capacity
-    for i in range(owners // 2):
-        first, second = arrived[2 * i, 0:1], arrived[2 * i + 1, 0:1]
-        s["ids"][:, i * 128 : (i + 1) * 128] = jnp.where(low_lanes, first, pltpu.roll(second, capacity, 1))
+    def column_of(source, first):
+        tile = jnp.broadcast_to(arrived[source, 0:1], (share, 128)).astype(F32)
+        there = iota((share, 128), 1) == iota((share, 128), 0) + first
+        return jnp.sum(jnp.where(there, tile, 0.0), axis=1, keepdims=True)
+
+    fetched, returned, parts, emb = s["fetched"], s["returned"], s["parts"], s["emb"]
     total = s["total"]
-    total[...] = jnp.zeros_like(total)
-
-    def look_up(i, carry):
-        rows = pl.ds(pl.multiple_of(i * chunk, chunk), chunk)
-        pltpu.make_async_copy(table.at[rows], table_buf.at[rows], table_sem.at[i]).wait()
-        total[...] += mm(one_hot(column == iota((owners * share, chunk), 1) + i * chunk), table_buf[rows])
-        return carry
-
-    lax.fori_loop(0, chunks // 2, look_up, 0)
+    askers = owners // 2
+
+    def look_up(part):
+        wanted = [column_of(at.owner_to(part * askers + d + 1), ha * share) for d in range(askers)]
+        column = jnp.concatenate(wanted, axis=0).astype(jnp.int32)
+        total[...] = jnp.zeros_like(total)
+
+        def step(i, carry):
+            rows = pl.ds(pl.multiple_of(i * chunk, chunk), chunk)
+            if part == 0:
+                pltpu.make_async_copy(table.at[rows], table_buf.at[rows], table_sem.at[i]).wait()
+            total[...] += mm(one_hot(column == iota((askers * share, chunk), 1) + i * chunk), table_buf[rows])
+            return carry
+
+        lax.fori_loop(0, chunks, step, 0)
+        fetched[part] = total[...].astype(BF16).reshape(fetched.shape[1:])
+        for d in range(askers):
+            to = at.owner_to(part * askers + d + 1)
+            if part * askers + d + 1 < owners:
+                item.start(fetched.at[part, d], returned.at[at.me], at.owner(to))
+            else:
+                returned[at.me] = fetched[part, d]
+
+    look_up(0)
     for d in range(1, zs):
         wz.arrive(d - 1)
         there = w.at[ha, at.z_from(d), my_half]
         wx.start(there, there, at.x_peer)
         wy.start(there, there, at.y_peer)
-    lax.fori_loop(chunks // 2, chunks, look_up, 0)
-    fetched, returned, parts, emb = s["fetched"], s["returned"], s["parts"], s["emb"]
-    fetched[...] = total[...].astype(BF16).reshape(fetched.shape)
-    for d in range(1, owners):
-        to = at.owner_to(d)
-        item.start(fetched.at[to], returned.at[at.me], at.owner(to))
-    returned[at.me] = fetched[at.me]
+    look_up(1)
     wx.arrive(0)
     there = w.at[1 - ha, at.pb]
     wc.start(there, there, at.core_peer)
@@ -677,6 +690,29 @@
         ]
         bias[head] = skew(jnp.broadcast_to(rel_back[head : head + 1], (group, group))) + jnp.concatenate(by_time, axis=1)
 
+    slots = 2 * count
+    ids = []
+    for h in range(2):
+        for block_at in range(owners * share // 128):
+            piece = jnp.zeros((1, 128), jnp.int32)
+            for k in range(128 // share):
+                turned = pltpu.roll(arrived[block_at * (128 // share) + k, 0:1], (k - h) * share % 128, 1)
+                piece = jnp.where(iota((1, 128), 1) // share == k, turned, piece)
+            ids.append(piece)
+    ids_row = jnp.concatenate(ids, axis=1)
+    ids_col = jnp.concatenate([column_of(o, h * share) for h in range(2) for o in range(owners)], axis=0).astype(jnp.int32)
+    last = table.shape[0]
+    ids_row = jnp.where(ids_row < 0, last, ids_row)
+    ids_col = jnp.where(ids_col < 0, last, ids_col)
+    keys_row, keys_col = ids_row * slots + iota((1, slots), 1), ids_col * slots + iota((slots, 1), 0)
+    order = jnp.sum((keys_col < keys_row).astype(F32), axis=0, keepdims=True).astype(jnp.int32)
+    s["turn"][...] = one_hot(order == iota((slots, slots), 0))
+    digits = jnp.concatenate([ids_row // 64, ids_row % 64] + [jnp.zeros((1, slots), jnp.int32)] * 6, axis=0)
+    found = mm_nt(digits.astype(F32).astype(BF16), s["turn"][...])
+    s["sorted_v"][...] = (64.0 * found[0:1] + found[1:2]).astype(jnp.int32)
+    limits = iota((slots, 128), 1) * s["limit_rows"]
+    s["limits_v"][...] = jnp.sum((ids_col < jnp.minimum(limits, last)).astype(F32), axis=0, keepdims=True).astype(jnp.int32)
+    out_copies = [local(14, s["sorted_v"], s["sorted"]), local(15, s["limits_v"], s["limits"])]
     for i in range(owners - 1):
         item.arrive(i)
     slot_hot = one_hot(place == iota((count, count), 0))
@@ -762,7 +798,7 @@
     for hf in range(2):
         part = mm_nt(mixed_in[:, hf * half : (hf + 1) * half], w_half(hf, out_cols))
         projected = part if projected is None else projected + part
-    mixed, mixed_rows = s["mixed"], s["mixed_rows"]
+    mixed, mixed_rows = s["mixed"], s["mixed_v"]
     mixed[...] = (projected + s["b_out_v"][...] + start).astype(BF16)
     mixed_c = copies("mixed")
     for device, to_ka, to_ha in at.quads:
@@ -776,8 +812,8 @@
     grad_gate = grad_raw * gain_out
     grad_gain_out = jnp.sum(grad_raw * gate, axis=0, keepdims=True)
     grad_att = layer_norm_back(grad_mixed * gate * gain_out, unit_out, inv_out).astype(BF16)
-    sum_a = WeightSum(at, s["a_own"], "x", s, "a_")
-    sums_b = [WeightSum(at, s[f"b{i}_own"], "y", s, f"b{i}_") for i in range(pairs)]
+    sum_a = WeightSum(at, "zxy", s, "a_")
+    sums_b = [WeightSum(at, "yxz", s, f"b{i}_") for i in range(pairs)]
 
     def put(own, hf, first, value):
         cols = value.shape[1]
@@ -813,7 +849,7 @@
                 there = slice(g * half + pair * 128, g * half + (pair + 1) * 128)
                 grad_pre[hf, :, there] = (part * slope[hf, :, there]).astype(BF16)
         if pair == 0:
-            sum_a.hop_one()
+            sum_a.hop(0)
         if pair < pairs - 1:
             for hf in range(2):
                 for g in range(1, 4):
@@ -825,7 +861,7 @@
         part = mm_nt(grad_pre[hf], w_half(hf, slice(0, 4 * half)))
         grad_normed = part if grad_normed is None else grad_normed + part
     cot32 = cot.astype(F32)
-    grad_start, grad_rows = s["grad_start"], s["grad_rows"]
+    grad_start, grad_rows = s["grad_start"], s["grad_rows_v"]
     grad_start[...] = (cot32 + layer_norm_back(grad_normed * gain_in, unit_in, inv_in)).astype(BF16)
     back_c = copies("back")
     for device, to_ka, to_ha in at.quads:
@@ -837,7 +873,7 @@
             put(s[f"b{pairs - 1}_own"], hf, (g - 1) * 128, mm_tn(normed, grad_pre[hf, :, there]))
     sums_b[-1].cores()
     for i in range(pairs - 1):
-        sums_b[i].hop_one()
+        sums_b[i].hop(0)
     gain_grad = jnp.sum(grad_normed * unit_in, axis=0, keepdims=True)
     bout_grad = jnp.sum(cot32, axis=0, keepdims=True)
     for hf in range(2):
@@ -873,49 +909,60 @@
     small_in, small_mine = s["small_in"], s["small_mine"]
     sum_c = copies("sum")
     sum_c.start(grad_small, small_in.at[0], at.core_peer)
-    sum_a.hop_two()
+    sum_a.hop(1)
 
     for i in range(3):
         back_c.arrive(i)
+    out_copies.append(local(16, grad_rows, s["grad_rows"]))
     outgoing, incoming = s["outgoing"], s["incoming"]
     slot_hot = one_hot(place == iota((count, count), 0))
     outgoing[...] = mm(slot_hot, grad_rows[...].reshape(count, width)).astype(BF16).reshape(outgoing.shape)
     give, hand = copies("give"), copies("hand")
     for d in range(1, owners):
         to = at.owner_to(d)
-        give.start(outgoing.at[to], incoming.at[at.me, ha], at.owner(to))
-    incoming[at.me, ha] = outgoing[at.me]
-    hand.start(incoming.at[at.me, ha], incoming.at[at.me, ha], at.x_peer)
+        give.start(outgoing.at[to], incoming.at[ha, at.me], at.owner(to))
+    incoming[ha, at.me] = outgoing[at.me]
+    hand.start(incoming.at[ha, at.me], incoming.at[ha, at.me], at.x_peer)
 
     def take(first, last):
         for d in range(first, last):
             give.arrive(d - 1)
-            there = incoming.at[at.owner_from(d), ha]
+            there = incoming.at[ha, at.owner_from(d)]
             hand.start(there, there, at.x_peer)
 
     third = owners // 3
-    sums_b[-1].hop_one()
+    sums_b[-1].hop(0)
     sum_c.arrive(0)
     small_mine[0] = grad_small[...] + small_in[0]
     sum_c.start(small_mine.at[0], small_in.at[1], at.x_peer)
     for i in range(pairs - 1):
-        sums_b[i].hop_two()
-    sum_a.hop_z()
+        sums_b[i].hop(1)
+    sum_a.hop(2)
     take(1, third)
-    sums_b[-1].hop_two()
+    sums_b[-1].hop(1)
     sum_c.arrive(1)
     small_mine[1] = small_mine[0] + small_in[1]
     sum_c.start(small_mine.at[1], small_in.at[2], at.y_peer)
     for i in range(pairs - 1):
-        sums_b[i].hop_z()
+        sums_b[i].hop(2)
     take(third, 2 * third)
     sum_c.arrive(2)
     small_mine[2] = small_mine[1] + small_in[2]
     for d in range(1, zs):
         sum_c.start(small_mine.at[2], small_in.at[2 + d], at.z_device(d))
-    sums_b[-1].hop_z()
+    sums_b[-1].hop(2)
     take(2 * third, owners)
-    grad_w = s["grad_w"]
+    ordered = s["ordered"]
+
+    def in_order(h):
+        cols = pl.ds(pl.multiple_of(h * count, count), count)
+        return mm(s["turn"][:, cols], incoming[h].reshape(count, width))
+
+    ordered[...] = in_order(ha)
+    for i in range(3):
+        mixed_c.arrive(i)
+    out_copies.append(local(17, mixed_rows, s["mixed_rows"]))
+    grad_w = s["grad_w_v"]
     grad_w[:, 0:gates_cols] = sum_a.finish()
     for i in range(pairs):
         first = gates_cols + i * 384
@@ -924,11 +971,14 @@
     for d in range(1, zs):
         sum_c.arrive(2 + d)
         summed = summed + small_in[2 + d]
-    s["small_sum"][...] = summed
-    for i in range(3):
-        mixed_c.arrive(i)
+    s["small_v"][...] = summed
+    out_copies += [local(18, grad_w, s["grad_w"]), local(19, s["small_v"], s["small_sum"])]
     for i in range(owners):
         hand.arrive(i)
+    s["rows_v"][...] = (ordered[...] + in_order(1 - ha)).astype(BF16)
+    out_copies.append(local(20, s["rows_v"], s["rows"]))
+    for copy in out_copies:
+        copy.wait()
     for kind in (req, item, emb_c, row_c, small_c, wz, wx, wy, wc, mixed_c, back_c, give, hand, sum_c):
         kind.sent()
     for part in [sum_a] + sums_b:
@@ -945,8 +995,9 @@
     block = shard_rows // 2
     dma = pltpu.SemaphoreType.DMA
     outs = {
-        "incoming": jax.ShapeDtypeStruct((owners, 2, share, width), BF16),
-        "ids": jax.ShapeDtypeStruct((1, 2 * count), jnp.int32),
+        "rows": jax.ShapeDtypeStruct((2 * count, width), BF16),
+        "sorted": jax.ShapeDtypeStruct((1, 2 * count), jnp.int32),
+        "limits": jax.ShapeDtypeStruct((1, 128), jnp.int32),
         "grad_rows": jax.ShapeDtypeStruct((MB, tok, width), BF16),
         "mixed_rows": jax.ShapeDtypeStruct((MB, tok, half), BF16),
         "grad_w": jax.ShapeDtypeStruct((block, 5 * half), F32),
@@ -958,8 +1009,8 @@
         "requests": pltpu.VMEM((owners, 8, 128), jnp.int32),
         "arrived": pltpu.VMEM((owners, 8, 128), jnp.int32),
         "table_buf": pltpu.VMEM(inputs["table"].shape, BF16),
-        "total": pltpu.VMEM((count, width), F32),
-        "fetched": pltpu.VMEM((owners, share, width), BF16),
+        "total": pltpu.VMEM((count // 2, width), F32),
+        "fetched": pltpu.VMEM((2, owners // 2, share, width), BF16),
         "returned": pltpu.VMEM((owners, share, width), BF16),
         "parts": pltpu.VMEM((MB, tok, width), BF16),
         "emb": pltpu.VMEM((MB, tok, width), BF16),
@@ -980,7 +1031,17 @@
         "outgoing": pltpu.VMEM((owners, share, width), BF16),
         "small_mine": pltpu.VMEM((3, 2, 16, half), F32),
         "small_in": pltpu.VMEM((2 + zs, 2, 16, half), F32),
-        "load_sem": dma((14,)),
+        "incoming": pltpu.VMEM((2, owners, share, width), BF16),
+        "rows_v": pltpu.VMEM((2 * count, width), BF16),
+        "ordered": pltpu.VMEM((2 * count, width), F32),
+        "turn": pltpu.VMEM((2 * count, 2 * count), BF16),
+        "sorted_v": pltpu.VMEM((1, 2 * count), jnp.int32),
+        "limits_v": pltpu.VMEM((1, 128), jnp.int32),
+        "grad_rows_v": pltpu.VMEM((MB, tok, width), BF16),
+        "mixed_v": pltpu.VMEM((MB, tok, half), BF16),
+        "grad_w_v": pltpu.VMEM((block, 5 * half), F32),
+        "small_v": pltpu.VMEM((2, 16, half), F32),
+        "load_sem": dma((21,)),
         "table_sem": dma((8,)),
     }
     for name in ("owner", "offset", "w_uvqk", "w_out", "b", "rel", "time", "gain_out", "gain_in", "b_out", "lengths", "times"):
@@ -991,15 +1052,15 @@
     ):
         scratch[name + "_send"] = dma((number,))
         scratch[name + "_recv"] = dma((number,))
-    scratch |= weight_sum_scratch("a_", "x", zs, block, 2 * half)
+    scratch |= weight_sum_scratch("a_", "zxy", zs, block, 2 * half)
     for i in range(half // 128):
-        scratch |= weight_sum_scratch(f"b{i}_", "y", zs, block, 384)
-    vmem = pl.BlockSpec(memory_space=pltpu.VMEM)
+        scratch |= weight_sum_scratch(f"b{i}_", "yxz", zs, block, 384)
+    hbm = pl.BlockSpec(memory_space=pltpu.HBM)
     found = pl.pallas_call(
         functools.partial(main_kernel, tuple(inputs), tuple(outs), tuple(scratch)),
         out_shape=tuple(outs.values()),
-        in_specs=[pl.BlockSpec(memory_space=pltpu.HBM)] * len(inputs),
-        out_specs=(vmem,) * len(outs),
+        in_specs=[hbm] * len(inputs),
+        out_specs=(hbm,) * len(outs),
         scratch_shapes=list(scratch.values()),
         compiler_params=pltpu.CompilerParams(
             collective_id=1, has_side_effects=True, vmem_limit_bytes=58 * 1024 * 1024
@@ -1008,49 +1069,116 @@
     return dict(zip(outs, found, strict=True))
 
 
-def scatter_kernel(ids_ref, rows_ref, grad_w_ref, small_ref, out_ref, w_ref, w_out_ref, b_ref, rel_ref, time_ref, gain_in_ref, gain_out_ref, b_out_ref):
-    tile = out_ref.shape[0]
-    row = iota((tile, ids_ref.shape[1]), 0) + pl.program_id(0) * tile
-    out_ref[...] = mm(one_hot(ids_ref[...] == row), rows_ref[...])
-
-    @pl.when(pl.program_id(0) == 0)
-    def _():
-        half = w_ref.shape[2]
-        buckets = time_ref.shape[1]
-        w_ref[:, 0, :] = grad_w_ref[:, 0:half]
-        w_out_ref[...] = grad_w_ref[:, half : 2 * half]
-        for pair in range(half // 128):
-            for g in range(1, 4):
-                first = 2 * half + pair * 384 + (g - 1) * 128
-                w_ref[:, g, pair * 128 : (pair + 1) * 128] = grad_w_ref[:, first : first + 128]
-        ha = lax.axis_index("ha")
-        b_ref[...] = small_ref[ha, 0:4, :]
-        rel_ref[...] = small_ref[ha, 4:8, :]
-        for i in range(2):
-            for j in range(2):
-                time_ref[2 * i + j : 2 * i + j + 1, :] = small_ref[ha, 8 + i : 9 + i, j * buckets : (j + 1) * buckets]
-        gain_out_ref[...] = small_ref[ha, 10:11, :]
-        for hf in range(2):
-            gain_in_ref[:, hf * half : (hf + 1) * half] = small_ref[hf, 11:12, :]
-            b_out_ref[:, hf * half : (hf + 1) * half] = small_ref[hf, 12:13, :]
-
-
-def scatter_rows(ids, rows, grad_w, small, table_rows, buckets, tile=512):
-    count, width = rows.shape
+def scatter_kernel(
+    limits_in, sorted_in, rows_in, grad_w_in, small_in, mixed_in, grad_rows_in,
+    out_ref, w_ref, w_out_ref, b_ref, rel_ref, time_ref, gain_in_ref, gain_out_ref, b_out_ref, mixed_out, grad_rows_out,
+    limits, ids, rows, grad_w_ref, small_ref, mixed, grad_rows, tiles, load_sem, tile_sem, pass_sem,
+):
+    pairs_in = [
+        (limits_in, limits), (sorted_in, ids), (rows_in, rows), (grad_w_in, grad_w_ref), (small_in, small_ref),
+        (mixed_in, mixed), (grad_rows_in, grad_rows),
+    ]
+    loads = [pltpu.make_async_copy(src, dst, load_sem.at[i]) for i, (src, dst) in enumerate(pairs_in)]
+    for load in loads:
+        load.start()
+    for load in loads[:3]:
+        load.wait()
+    slots, tile = tiles.shape[0], tiles.shape[1]
+    count = out_ref.shape[0] // tile
+    per_tile = tile // 256
+    depth = 256
+
+    def write(i, slot):
+        there = pl.ds(pl.multiple_of(i * tile, tile), tile)
+        return pltpu.make_async_copy(tiles.at[slot], out_ref.at[there], tile_sem.at[slot])
+
+    def step(i, carry):
+        slot = lax.rem(i, slots)
+
+        @pl.when(i >= slots)
+        def _():
+            write(i - slots, slot).wait()
+
+        first = limits[0, i * per_tile] // depth
+        end = (limits[0, (i + 1) * per_tile] + depth - 1) // depth
+
+        def product(j):
+            here = pl.ds(pl.multiple_of(j * depth, depth), depth)
+            return mm(one_hot(ids[:, here] == iota((tile, depth), 0) + i * tile), rows[here, :])
+
+        tiles[slot] = product(jnp.minimum(first, rows.shape[0] // depth - 1))
+
+        def more(j, carry):
+            tiles[slot] += product(j)
+            return carry
+
+        lax.fori_loop(first + 1, end, more, 0)
+        write(i, slot).start()
+        return carry
+
+    lax.fori_loop(0, 2, step, 0)
+    for load in loads[3:]:
+        load.wait()
+    passed = [
+        pltpu.make_async_copy(mixed, mixed_out, pass_sem.at[0]),
+        pltpu.make_async_copy(grad_rows, grad_rows_out, pass_sem.at[1]),
+    ]
+    for copy in passed:
+        copy.start()
+    lax.fori_loop(2, count, step, 0)
+    half = w_ref.shape[2]
+    buckets = time_ref.shape[1]
+    w_ref[:, 0, :] = grad_w_ref[:, 0:half]
+    w_out_ref[...] = grad_w_ref[:, half : 2 * half]
+    for pair in range(half // 128):
+        for g in range(1, 4):
+            first = 2 * half + pair * 384 + (g - 1) * 128
+            w_ref[:, g, pair * 128 : (pair + 1) * 128] = grad_w_ref[:, first : first + 128]
+    ha = lax.axis_index("ha")
+    b_ref[...] = small_ref[ha, 0:4, :]
+    rel_ref[...] = small_ref[ha, 4:8, :]
+    for i in range(2):
+        for j in range(2):
+            time_ref[2 * i + j : 2 * i + j + 1, :] = small_ref[ha, 8 + i : 9 + i, j * buckets : (j + 1) * buckets]
+    gain_out_ref[...] = small_ref[ha, 10:11, :]
+    for hf in range(2):
+        gain_in_ref[:, hf * half : (hf + 1) * half] = small_ref[hf, 11:12, :]
+        b_out_ref[:, hf * half : (hf + 1) * half] = small_ref[hf, 12:13, :]
+    for k in range(slots):
+        write(count - slots + k, (count - slots + k) % slots).wait()
+    for copy in passed:
+        copy.wait()
+
+
+def scatter_rows(found, table_rows, buckets, tile=512, slots=4):
+    rows, grad_w = found["rows"], found["grad_w"]
+    width = rows.shape[1]
     half, block = width // 2, grad_w.shape[0]
-
-    def whole(shape):
-        return pl.BlockSpec(shape, lambda i: (0,) * len(shape))
-
+    names = ("limits", "sorted", "rows", "grad_w", "small_sum", "mixed_rows", "grad_rows")
     shapes = [(block, 4, half), (block, half), (4, half), (4, half), (4, buckets), (1, width), (1, half), (1, width)]
+    hbm, vmem = pl.BlockSpec(memory_space=pltpu.HBM), pl.BlockSpec(memory_space=pltpu.VMEM)
+    outs = [jax.ShapeDtypeStruct(shape, F32) for shape in [(table_rows, width)] + shapes]
+    outs += [jax.ShapeDtypeStruct(found[name].shape, BF16) for name in ("mixed_rows", "grad_rows")]
     return pl.pallas_call(
         scatter_kernel,
-        grid=(table_rows // tile,),
-        out_shape=[jax.ShapeDtypeStruct(shape, F32) for shape in [(table_rows, width)] + shapes],
-        in_specs=[whole((1, count)), whole((count, width)), whole(grad_w.shape), whole(small.shape)],
-        out_specs=[pl.BlockSpec((tile, width), lambda i: (i, 0))] + [whole(shape) for shape in shapes],
-        compiler_params=pltpu.CompilerParams(vmem_limit_bytes=40 * 1024 * 1024),
-    )(ids, rows, grad_w, small)
+        out_shape=outs,
+        in_specs=[hbm] * len(names),
+        out_specs=[hbm] + [vmem] * len(shapes) + [hbm] * 2,
+        scratch_shapes=[
+            pltpu.SMEM(found["limits"].shape, jnp.int32),
+            pltpu.VMEM(found["sorted"].shape, jnp.int32),
+            pltpu.VMEM(rows.shape, BF16),
+            pltpu.VMEM(grad_w.shape, F32),
+            pltpu.VMEM(found["small_sum"].shape, F32),
+            pltpu.VMEM(found["mixed_rows"].shape, BF16),
+            pltpu.VMEM(found["grad_rows"].shape, BF16),
+            pltpu.VMEM((slots, tile, width), F32),
+            pltpu.SemaphoreType.DMA((len(names),)),
+            pltpu.SemaphoreType.DMA((slots,)),
+            pltpu.SemaphoreType.DMA((2,)),
+        ],
+        compiler_params=pltpu.CompilerParams(vmem_limit_bytes=58 * 1024 * 1024),
+    )(*(found[name] for name in names))
 
 
 def local_streams(
@@ -1091,17 +1219,12 @@
             "times": times[0],
         }
     )
-    table_grad, grad_w, grad_w_out, grad_b, grad_rel, grad_time, grad_gain_in, grad_gain_out, grad_b_out = scatter_rows(
-        found["ids"],
-        found["incoming"].reshape(2 * row_count, width),
-        found["grad_w"],
-        found["small_sum"],
-        table.shape[0],
-        time_bias.shape[1],
-    )
+    (
+        table_grad, grad_w, grad_w_out, grad_b, grad_rel, grad_time, grad_gain_in, grad_gain_out, grad_b_out, mixed, grad_rows,
+    ) = scatter_rows(found, table.shape[0], time_bias.shape[1])
     return (
-        found["mixed_rows"].reshape(row_count, half),
-        found["grad_rows"].reshape(row_count, width),
+        mixed.reshape(row_count, half),
+        grad_rows.reshape(row_count, width),
         table_grad,
         grad_gain_in.reshape(width),
         grad_w,

time: 108 us -> 92.6 us (0.86)
  Pallas kernels: 99.5 us -> 90.4 us
  local copies, waits for them, and re-layouts: 7.11 us -> 0 us
    unnamed x10 -> x0, local copies, waits for them, and re-layouts: 7.11 us -> none
    pallas_call x1, Pallas kernels: 14.3 us -> 8.45 us  [scatter_rows(): pl.pallas_call(scatter_kernel, out_shape=outs, in_specs=[hbm] * len(names...]
    pallas_call x1, Pallas kernels: 85.2 us -> 82 us  [run_main(): pl.pallas_call(functools.partial(main_kernel, tuple(inputs), tuple(outs),...]
where the time goes in v4:
time: 92.6 us; the launch traced here: 91.3 us
  Pallas kernels  90.4 us (98%)
    pallas_call x1, Pallas kernels, run_main(): pl.pallas_call(functools.partial(main_kernel, tuple(inputs), tuple(outs),...  82 us
    pallas_call x1, Pallas kernels, scatter_rows(): pl.pallas_call(scatter_kernel, out_shape=outs, in_specs=[hbm] * len(names...  8.45 us

profile of v4, /device:TPU:0, one launch (start us, length us, event | category | flops | bytes accessed | tf_op | source)
XLA Modules:
  0.0 91.3 jit_solution(15218669674581976367)
XLA Ops:
  0.6 82.0 %shard_map.230 = (bf16[1024,512]{1,0:T(8,128)(2,1)}, s32[1,1024]{1,0:T(1,128)}, s32[1,128]{1,0:T(1,128)}, bf16[4,128,512]{2,1,0:T(8,128)(2,1)}, bf16[4,128,256]{...) custom-call(s32[1,512]{1,0:T(1,128)} %bitcast.16, s32[1,512]{1,0:T(1,128)} %bitcast.17, ...), custom_call_target="tpu_custom_call" | custom-call | tf_op jit(solution)/shard_map/pallas_call | solution.py:1059
  82.6 8.5 %shard_map.231 = (f32[8192,512]{1,0:T(8,128)}, f32[32,4,256]{2,1,0:T(4,128)}, f32[32,256]{1,0:T(8,128)}, f32[4,256]{1,0:T(4,128)}, f32[4,256]{1,0:T(4,128)}, /*i...) custom-call(s32[1,128]{1,0:T(1,128)} %get-tuple-element.29.limits_in, ...), custom_call_target="tpu_custom_call" | custom-call | tf_op jit(solution)/shard_map/pallas_call | solution.py:1162

commit v5 on v4

--- a/solution.py
+++ b/solution.py
@@ -396,19 +396,21 @@
         self.xy_peer = (self.pb, 1 - self.ka, 1 - self.ha)
         self.core_peer = (2 * self.z + 1 - self.core, self.ka, self.ha)
         self.quads = [
+            (self.xy_peer, 1 - self.ka, 1 - self.ha),
             (self.x_peer, self.ka, 1 - self.ha),
             (self.y_peer, 1 - self.ka, self.ha),
-            (self.xy_peer, 1 - self.ka, 1 - self.ha),
         ]
 
-    def owner(self, index):
-        return (index // self.kas, index % self.kas, self.ha)
+    def partner(self, k):
+        dz, dc, dk = k // 4, k // 2 % 2, k % 2
+        z = [self.z, self.z + 1 - 2 * (self.z % 2), (self.z + 2) % 4, 3 - self.z][dz]
+        core = 1 - self.core if dc else self.core
+        ka = 1 - self.ka if dk else self.ka
+        return (2 * z + core) * 2 + ka, (2 * z + core, ka, self.ha)
 
     def owner_to(self, d):
-        return lax.rem(self.me + d, self.owners)
-
-    def owner_from(self, d):
-        return lax.rem(self.me - d + self.owners, self.owners)
+        index = lax.rem(self.me + d, self.owners)
+        return index, (index // self.kas, index % self.kas, self.ha)
 
     def z_to(self, d):
         return lax.rem(self.z + d, self.zs)
@@ -442,44 +444,49 @@
     def __init__(self, at, order, s, name):
         self.at, self.order = at, order
         self.own, self.core_in = s[name + "own"], s[name + "core_in"]
-        self.mine = [s[f"{name}mine{i}"] for i in range(3)]
-        self.other = [s[f"{name}other{i}"] for i in range(3)]
+        self.mine = [s[f"{name}mine{i}"] for i in range(len(order))]
+        self.other = [s[f"{name}other{i}"] for i in range(len(order))]
         self.copies = Copies(s[name + "send"], s[name + "recv"])
         self.begun = [0]
 
-    def pick(self, ref, axis, index):
-        left = [a for a in "xzy" if a not in self.order[: self.order.index(axis)]]
-        return ref.at[(slice(None),) * left.index(axis) + (index,)]
-
-    def peers(self, axis):
+    def pick(self, ref, step, index):
+        done = "".join(self.order[: self.order.index(step)])
+        left = [a for a in "xzy" if a not in done]
+        at_axis = dict(zip(step, index))
+        return ref.at[tuple(at_axis.get(a, slice(None)) for a in left)]
+
+    def peers(self, step):
         at = self.at
-        if axis == "x":
-            return [(at.x_peer, 1 - at.ha)]
-        if axis == "y":
-            return [(at.y_peer, 1 - at.ka)]
-        return [(at.z_device(d), at.z_to(d)) for d in range(1, at.zs)]
-
-    def own_index(self, axis):
-        return {"x": self.at.ha, "y": self.at.ka, "z": self.at.z}[axis]
+        if step == "z":
+            return [(at.z_device(d), (at.z_to(d),)) for d in range(1, at.zs)]
+        if step == "x":
+            return [(at.x_peer, (1 - at.ha,))]
+        if step == "y":
+            return [(at.y_peer, (1 - at.ka,))]
+        return [(device, (to_ha, to_ka)) for device, to_ka, to_ha in at.quads]
+
+    def own_index(self, step):
+        return tuple({"x": self.at.ha, "y": self.at.ka, "z": self.at.z}[axis] for axis in step)
 
     def cores(self):
         self.copies.start(self.own.at[:, :, 1 - self.at.core], self.core_in, self.at.core_peer)
 
     def send(self, i):
-        axis = self.order[i]
+        step = self.order[i]
         self.begun.append(len(self.copies.copies))
-        for k, (device, index) in enumerate(self.peers(axis)):
-            self.copies.start(self.pick(self.mine[i], axis, index), self.other[i].at[k], device)
+        for k, (device, index) in enumerate(self.peers(step)):
+            self.copies.start(self.pick(self.mine[i], step, index), self.other[i].at[k], device)
 
     def received(self, i):
-        axis = self.order[i]
-        total = self.pick(self.mine[i], axis, self.own_index(axis))[...].astype(F32)
-        for k in range(len(self.peers(axis))):
+        step = self.order[i]
+        total = self.pick(self.mine[i], step, self.own_index(step))[...].astype(F32)
+        for k in range(len(self.peers(step))):
             self.copies.arrive(self.begun[i + 1] + k)
             total = total + self.other[i][k].astype(F32)
         return total
 
-    def hop(self, i):
+    def hop(self):
+        i = len(self.begun) - 1
         if i == 0:
             self.copies.arrive(0)
             for h in range(2):
@@ -490,7 +497,7 @@
         self.send(i)
 
     def finish(self):
-        return self.received(2)
+        return self.received(len(self.order) - 1)
 
 
 def weight_sum_scratch(name, order, zs, block, cols):
@@ -500,14 +507,28 @@
         name + "own": pltpu.VMEM((2, zs, 2, 2 * block, cols), BF16),
         name + "core_in": pltpu.VMEM((2, zs, 2 * block, cols), BF16),
     }
-    for i, axis in enumerate(order):
-        before = [sizes[a] for a in "xzy" if a not in order[:i]]
-        after = [sizes[a] for a in "xzy" if a not in order[: i + 1]]
+    for i, step in enumerate(order):
+        before = [sizes[a] for a in "xzy" if a not in "".join(order[:i])]
+        after = [sizes[a] for a in "xzy" if a not in "".join(order[: i + 1])]
         found[f"{name}mine{i}"] = pltpu.VMEM((*before, block, cols), BF16)
-        found[f"{name}other{i}"] = pltpu.VMEM((sizes[axis] - 1, *after, block, cols), BF16)
-    found[name + "send"] = dma((2 + zs,))
-    found[name + "recv"] = dma((2 + zs,))
+        found[f"{name}other{i}"] = pltpu.VMEM(({"xy": 3, "z": zs - 1}.get(step, 1), *after, block, cols), BF16)
+    found[name + "send"] = dma((1 + 3 + zs,))
+    found[name + "recv"] = dma((1 + 3 + zs,))
     return found
+
+
+ORDERS = {"a_": ("z", "xy"), "b0_": ("xy", "z"), "b1_": ("xy", "z")}
+STEPS = {
+    "pair 0": ("a_",),
+    "rows sent": (),
+    "tables": (),
+    "given": ("b0_", "b1_", "a_"),
+    "take 1": (),
+    "take 2": ("b0_",),
+    "take 3": (),
+    "take 4": ("b1_",),
+    "take 5": (),
+}
 
 
 def main_kernel(in_names, out_names, scratch_names, *refs):
@@ -520,8 +541,7 @@
     half = width // 2
     tok = count // MB
     group = 2 * tok
-    share = count // owners
-    capacity = 2 * share
+    capacity = 2 * count // owners
     block = s["w_uvqk"].shape[0] // 2
     heads_half = half // 64
     heads = 2 * heads_half
@@ -547,11 +567,17 @@
         loads[name] = local(i, s[name], s[name + "_v"])
     loads["ctx"] = local(12, s["context"].at[mine], s["ctx_v"].at[ka])
     loads["cot"] = local(13, s["cot"].at[mine], s["cot_v"].at[ka])
+    own_cols = pl.ds(pl.multiple_of(ha * half, half), half)
+
+    def table_copy(i):
+        rows = pl.ds(pl.multiple_of(i * chunk, chunk), chunk)
+        return pltpu.make_async_copy(table.at[rows, own_cols], table_buf.at[rows], table_sem.at[i])
+
     for i in range(chunks):
-        rows = pl.ds(i * chunk, chunk)
-        pltpu.make_async_copy(table.at[rows], table_buf.at[rows], table_sem.at[i]).start()
+        table_copy(i).start()
     barrier = pltpu.get_barrier_semaphore()
-    partners = [at.owner(at.owner_to(d)) for d in range(1, owners)] + [at.x_peer, at.xy_peer]
+    far, near = list(range(owners // 2, owners)), list(range(1, owners // 2))
+    partners = [at.partner(k)[1] for k in far + near] + [at.x_peer, at.xy_peer]
     for device in partners:
         pl.semaphore_signal(barrier, inc=1, device_id=device, device_id_type=MESH)
 
@@ -568,8 +594,7 @@
     asked = asked.astype(jnp.int32)
     for o in range(owners):
         s["requests"][o] = jnp.broadcast_to(asked[o : o + 1], (8, 128))
-    place = rank - ha * share
-    place = jnp.where((place >= 0) & (place < share), owner_row * share + place, -1)
+    place = owner_row * capacity + rank
 
     shard, w, small = s["shard"], s["w"], s["small"]
     loads["w_uvqk"].wait()
@@ -595,9 +620,9 @@
     requests, arrived = s["requests"], s["arrived"]
     req, item, emb_c, row_c, small_c = copies("req"), copies("item"), copies("emb"), copies("row"), copies("small")
     wz, wx, wy, wc = copies("wz"), copies("wx"), copies("wy"), copies("wc")
-    for d in range(1, owners):
-        to = at.owner_to(d)
-        req.start(requests.at[to], arrived.at[at.me], at.owner(to))
+    for k in far + near:
+        to, device = at.partner(k)
+        req.start(requests.at[to], arrived.at[at.me], device)
     arrived[at.me] = requests[at.me]
     my_half = pl.ds(pl.multiple_of(ka * block, block), block)
     for d in range(1, zs):
@@ -610,35 +635,36 @@
 
     for i in range(owners - 1):
         req.arrive(i)
-    def column_of(source, first):
-        tile = jnp.broadcast_to(arrived[source, 0:1], (share, 128)).astype(F32)
-        there = iota((share, 128), 1) == iota((share, 128), 0) + first
-        return jnp.sum(jnp.where(there, tile, 0.0), axis=1, keepdims=True)
+    wide_pick = iota((capacity, 128), 1) == iota((capacity, 128), 0)
+
+    def column_of(source):
+        tile = jnp.broadcast_to(arrived[source, 0:1], (capacity, 128)).astype(F32)
+        return jnp.sum(jnp.where(wide_pick, tile, 0.0), axis=1, keepdims=True)
 
     fetched, returned, parts, emb = s["fetched"], s["returned"], s["parts"], s["emb"]
     total = s["total"]
     askers = owners // 2
 
     def look_up(part):
-        wanted = [column_of(at.owner_to(part * askers + d + 1), ha * share) for d in range(askers)]
+        rounds = [(part * askers + d + 1) % owners for d in range(askers)]
+        wanted = [column_of(at.owner_to(d)[0]) for d in rounds]
         column = jnp.concatenate(wanted, axis=0).astype(jnp.int32)
         total[...] = jnp.zeros_like(total)
 
         def step(i, carry):
+            if part == 0:
+                table_copy(i).wait()
             rows = pl.ds(pl.multiple_of(i * chunk, chunk), chunk)
-            if part == 0:
-                pltpu.make_async_copy(table.at[rows], table_buf.at[rows], table_sem.at[i]).wait()
-            total[...] += mm(one_hot(column == iota((askers * share, chunk), 1) + i * chunk), table_buf[rows])
+            total[...] += mm(one_hot(column == iota((askers * capacity, chunk), 1) + i * chunk), table_buf[rows])
             return carry
 
         lax.fori_loop(0, chunks, step, 0)
         fetched[part] = total[...].astype(BF16).reshape(fetched.shape[1:])
-        for d in range(askers):
-            to = at.owner_to(part * askers + d + 1)
-            if part * askers + d + 1 < owners:
-                item.start(fetched.at[part, d], returned.at[at.me], at.owner(to))
+        for i, d in enumerate(rounds):
+            if d:
+                item.start(fetched.at[part, i], returned.at[at.me], at.owner_to(d)[1])
             else:
-                returned[at.me] = fetched[part, d]
+                returned[at.me] = fetched[part, i]
 
     look_up(0)
     for d in range(1, zs):
@@ -690,17 +716,28 @@
         ]
         bias[head] = skew(jnp.broadcast_to(rel_back[head : head + 1], (group, group))) + jnp.concatenate(by_time, axis=1)
 
+    for i in range(owners - 1):
+        item.arrive(i)
+    slot_hot = one_hot(place == iota((2 * count, count), 0))
+    parts[...] = mm_tn(slot_hot, returned[...].reshape(2 * count, half)).astype(BF16).reshape(parts.shape)
+    for device, to_ka, to_ha in at.quads:
+        emb_c.start(parts.at[2 * to_ka + to_ha], emb.at[at.stream], device)
+    emb[at.stream] = parts[at.stream]
+    for d in range(1, zs):
+        wy.arrive(d - 1)
+        there = w.at[ha, at.z_from(d)]
+        wc.start(there, there, at.core_peer)
+    for d in range(1, zs):
+        wy.arrive(zs - 2 + d)
+        there = w.at[1 - ha, at.z_from(d)]
+        wc.start(there, there, at.core_peer)
     slots = 2 * count
+    low_lanes = iota((1, 128), 1) < capacity
     ids = []
-    for h in range(2):
-        for block_at in range(owners * share // 128):
-            piece = jnp.zeros((1, 128), jnp.int32)
-            for k in range(128 // share):
-                turned = pltpu.roll(arrived[block_at * (128 // share) + k, 0:1], (k - h) * share % 128, 1)
-                piece = jnp.where(iota((1, 128), 1) // share == k, turned, piece)
-            ids.append(piece)
+    for i in range(owners // 2):
+        ids.append(jnp.where(low_lanes, arrived[2 * i, 0:1], pltpu.roll(arrived[2 * i + 1, 0:1], capacity, 1)))
     ids_row = jnp.concatenate(ids, axis=1)
-    ids_col = jnp.concatenate([column_of(o, h * share) for h in range(2) for o in range(owners)], axis=0).astype(jnp.int32)
+    ids_col = jnp.concatenate([column_of(o) for o in range(owners)], axis=0).astype(jnp.int32)
     last = table.shape[0]
     ids_row = jnp.where(ids_row < 0, last, ids_row)
     ids_col = jnp.where(ids_col < 0, last, ids_col)
@@ -713,21 +750,6 @@
     limits = iota((slots, 128), 1) * s["limit_rows"]
     s["limits_v"][...] = jnp.sum((ids_col < jnp.minimum(limits, last)).astype(F32), axis=0, keepdims=True).astype(jnp.int32)
     out_copies = [local(14, s["sorted_v"], s["sorted"]), local(15, s["limits_v"], s["limits"])]
-    for i in range(owners - 1):
-        item.arrive(i)
-    slot_hot = one_hot(place == iota((count, count), 0))
-    parts[...] = mm_tn(slot_hot, returned[...].reshape(count, width)).astype(BF16).reshape(parts.shape)
-    for device, to_ka, to_ha in at.quads:
-        emb_c.start(parts.at[2 * to_ka + to_ha], emb.at[at.stream], device)
-    emb[at.stream] = parts[at.stream]
-    for d in range(1, zs):
-        wy.arrive(d - 1)
-        there = w.at[ha, at.z_from(d)]
-        wc.start(there, there, at.core_peer)
-    for d in range(1, zs):
-        wy.arrive(zs - 2 + d)
-        there = w.at[1 - ha, at.z_from(d)]
-        wc.start(there, there, at.core_peer)
     for i in range(2 * zs):
         wc.arrive(i)
 
@@ -747,7 +769,7 @@
         emb_c.arrive(i)
 
     embedded = jnp.concatenate(
-        [emb[0].astype(F32) + emb[1].astype(F32), emb[2].astype(F32) + emb[3].astype(F32)], axis=0
+        [jnp.concatenate([emb[2 * i], emb[2 * i + 1]], axis=1).astype(F32) for i in range(2)], axis=0
     )
     start = s["ctx_v"][...].reshape(group, width).astype(F32) + embedded
     unit_in, inv_in = layer_norm(start)
@@ -812,8 +834,14 @@
     grad_gate = grad_raw * gain_out
     grad_gain_out = jnp.sum(grad_raw * gate, axis=0, keepdims=True)
     grad_att = layer_norm_back(grad_mixed * gate * gain_out, unit_out, inv_out).astype(BF16)
-    sum_a = WeightSum(at, "zxy", s, "a_")
-    sums_b = [WeightSum(at, "yxz", s, f"b{i}_") for i in range(pairs)]
+    sum_a = WeightSum(at, ORDERS["a_"], s, "a_")
+    sums_b = [WeightSum(at, ORDERS[f"b{i}_"], s, f"b{i}_") for i in range(pairs)]
+
+    hops = {"a_": sum_a} | {f"b{i}_": part for i, part in enumerate(sums_b)}
+
+    def steps_at(point):
+        for name in STEPS[point]:
+            hops[name].hop()
 
     def put(own, hf, first, value):
         cols = value.shape[1]
@@ -849,7 +877,7 @@
                 there = slice(g * half + pair * 128, g * half + (pair + 1) * 128)
                 grad_pre[hf, :, there] = (part * slope[hf, :, there]).astype(BF16)
         if pair == 0:
-            sum_a.hop(0)
+            steps_at("pair 0")
         if pair < pairs - 1:
             for hf in range(2):
                 for g in range(1, 4):
@@ -864,16 +892,19 @@
     grad_start, grad_rows = s["grad_start"], s["grad_rows_v"]
     grad_start[...] = (cot32 + layer_norm_back(grad_normed * gain_in, unit_in, inv_in)).astype(BF16)
     back_c = copies("back")
-    for device, to_ka, to_ha in at.quads:
-        back_c.start(grad_start.at[pl.ds(to_ka * tok, tok)], grad_rows.at[at.stream], device)
+    for first in (True, False):
+        for device, to_ka, to_ha in at.quads:
+            h = to_ha if first else 1 - to_ha
+            cols = pl.ds(pl.multiple_of(h * half, half), half)
+            here = grad_start.at[pl.ds(pl.multiple_of(to_ka * tok, tok), tok), cols]
+            back_c.start(here, grad_rows.at[at.stream, :, cols], device)
     grad_rows[at.stream] = grad_start[own_rows]
     for hf in range(2):
         for g in range(1, 4):
             there = slice(g * half + (pairs - 1) * 128, g * half + pairs * 128)
             put(s[f"b{pairs - 1}_own"], hf, (g - 1) * 128, mm_tn(normed, grad_pre[hf, :, there]))
     sums_b[-1].cores()
-    for i in range(pairs - 1):
-        sums_b[i].hop(0)
+    steps_at("rows sent")
     gain_grad = jnp.sum(grad_normed * unit_in, axis=0, keepdims=True)
     bout_grad = jnp.sum(cot32, axis=0, keepdims=True)
     for hf in range(2):
@@ -909,56 +940,65 @@
     small_in, small_mine = s["small_in"], s["small_mine"]
     sum_c = copies("sum")
     sum_c.start(grad_small, small_in.at[0], at.core_peer)
-    sum_a.hop(1)
-
+
+    steps_at("tables")
     for i in range(3):
         back_c.arrive(i)
-    out_copies.append(local(16, grad_rows, s["grad_rows"]))
     outgoing, incoming = s["outgoing"], s["incoming"]
-    slot_hot = one_hot(place == iota((count, count), 0))
-    outgoing[...] = mm(slot_hot, grad_rows[...].reshape(count, width)).astype(BF16).reshape(outgoing.shape)
+    slot_hot = one_hot(place == iota((2 * count, count), 0))
+    outgoing[...] = mm(slot_hot, grad_rows[:, :, own_cols].reshape(count, half)).astype(BF16).reshape(outgoing.shape)
     give, hand = copies("give"), copies("hand")
-    for d in range(1, owners):
-        to = at.owner_to(d)
-        give.start(outgoing.at[to], incoming.at[ha, at.me], at.owner(to))
+    given = {}
+
+    def start_give(*rounds):
+        for k in rounds:
+            to, device = at.partner(k)
+            given[k] = len(give.copies)
+            give.start(outgoing.at[to], incoming.at[ha, at.me], device)
+
+    start_give(8, 9, 10, 11, 1, 2, 3, 4, 5, 6, 7)
     incoming[ha, at.me] = outgoing[at.me]
     hand.start(incoming.at[ha, at.me], incoming.at[ha, at.me], at.x_peer)
 
-    def take(first, last):
-        for d in range(first, last):
-            give.arrive(d - 1)
-            there = incoming.at[ha, at.owner_from(d)]
+    def take(*rounds):
+        for k in rounds:
+            give.arrive(given[k])
+            there = incoming.at[ha, at.partner(k)[0]]
             hand.start(there, there, at.x_peer)
 
-    third = owners // 3
-    sums_b[-1].hop(0)
+    steps_at("given")
+    take(1, 2, 3)
     sum_c.arrive(0)
     small_mine[0] = grad_small[...] + small_in[0]
-    sum_c.start(small_mine.at[0], small_in.at[1], at.x_peer)
-    for i in range(pairs - 1):
-        sums_b[i].hop(1)
-    sum_a.hop(2)
-    take(1, third)
-    sums_b[-1].hop(1)
-    sum_c.arrive(1)
-    small_mine[1] = small_mine[0] + small_in[1]
-    sum_c.start(small_mine.at[1], small_in.at[2], at.y_peer)
-    for i in range(pairs - 1):
-        sums_b[i].hop(2)
-    take(third, 2 * third)
-    sum_c.arrive(2)
-    small_mine[2] = small_mine[1] + small_in[2]
+    for i, (device, _, _) in enumerate(at.quads):
+        sum_c.start(small_mine.at[0], small_in.at[1 + i], device)
+    steps_at("take 1")
+    take(8, 9)
+    start_give(12, 13)
+    steps_at("take 2")
+    take(4, 5, 6, 7)
+    steps_at("take 3")
+    take(10, 11)
+    start_give(14, 15)
+    summed = small_mine[0]
+    for i in range(1, 4):
+        sum_c.arrive(i)
+        summed = summed + small_in[i]
+    small_mine[1] = summed
     for d in range(1, zs):
-        sum_c.start(small_mine.at[2], small_in.at[2 + d], at.z_device(d))
-    sums_b[-1].hop(2)
-    take(2 * third, owners)
-    ordered = s["ordered"]
-
+        sum_c.start(small_mine.at[1], small_in.at[3 + d], at.z_device(d))
+    steps_at("take 4")
+    take(12, 13)
+    steps_at("take 5")
+    take(14, 15)
     def in_order(h):
-        cols = pl.ds(pl.multiple_of(h * count, count), count)
-        return mm(s["turn"][:, cols], incoming[h].reshape(count, width))
-
-    ordered[...] = in_order(ha)
+        cols = pl.ds(pl.multiple_of(h * half, half), half)
+        s["rows_v"][:, cols] = mm(s["turn"][...], incoming[h].reshape(slots, half)).astype(BF16)
+
+    in_order(ha)
+    for i in range(3, 6):
+        back_c.arrive(i)
+    out_copies.append(local(16, grad_rows, s["grad_rows"]))
     for i in range(3):
         mixed_c.arrive(i)
     out_copies.append(local(17, mixed_rows, s["mixed_rows"]))
@@ -967,15 +1007,15 @@
     for i in range(pairs):
         first = gates_cols + i * 384
         grad_w[:, first : first + 384] = sums_b[i].finish()
-    summed = small_mine[2]
+    summed = small_mine[1]
     for d in range(1, zs):
-        sum_c.arrive(2 + d)
-        summed = summed + small_in[2 + d]
+        sum_c.arrive(3 + d)
+        summed = summed + small_in[3 + d]
     s["small_v"][...] = summed
     out_copies += [local(18, grad_w, s["grad_w"]), local(19, s["small_v"], s["small_sum"])]
     for i in range(owners):
         hand.arrive(i)
-    s["rows_v"][...] = (ordered[...] + in_order(1 - ha)).astype(BF16)
+    in_order(1 - ha)
     out_copies.append(local(20, s["rows_v"], s["rows"]))
     for copy in out_copies:
         copy.wait()
@@ -989,7 +1029,7 @@
     pbs, kas = lax.axis_size("pb"), lax.axis_size("ka")
     owners, zs = pbs * kas, pbs // 2
     count, width = inputs["context"].shape
-    half, tok, share = width // 2, count // MB, count // owners
+    half, tok, capacity = width // 2, count // MB, 2 * count // owners
     group, heads = 2 * tok, width // 64
     shard_rows = inputs["w_uvqk"].shape[0]
     block = shard_rows // 2
@@ -1008,12 +1048,12 @@
         "cot_v": pltpu.VMEM((2, tok, width), BF16),
         "requests": pltpu.VMEM((owners, 8, 128), jnp.int32),
         "arrived": pltpu.VMEM((owners, 8, 128), jnp.int32),
-        "table_buf": pltpu.VMEM(inputs["table"].shape, BF16),
-        "total": pltpu.VMEM((count // 2, width), F32),
-        "fetched": pltpu.VMEM((2, owners // 2, share, width), BF16),
-        "returned": pltpu.VMEM((owners, share, width), BF16),
-        "parts": pltpu.VMEM((MB, tok, width), BF16),
-        "emb": pltpu.VMEM((MB, tok, width), BF16),
+        "table_buf": pltpu.VMEM((inputs["table"].shape[0], half), BF16),
+        "total": pltpu.VMEM((count, half), F32),
+        "fetched": pltpu.VMEM((2, owners // 2, capacity, half), BF16),
+        "returned": pltpu.VMEM((owners, capacity, half), BF16),
+        "parts": pltpu.VMEM((MB, tok, half), BF16),
+        "emb": pltpu.VMEM((MB, tok, half), BF16),
         "shard": pltpu.VMEM((shard_rows, 5 * half), BF16),
         "w": pltpu.VMEM((2, pbs, shard_rows, 5 * half), BF16),
         "small": pltpu.VMEM((2, 16, half), F32),
@@ -1028,12 +1068,11 @@
         "mixed": pltpu.VMEM((group, width), BF16),
         "grad_start": pltpu.VMEM((group, width), BF16),
         "grad_small": pltpu.VMEM((2, 16, half), F32),
-        "outgoing": pltpu.VMEM((owners, share, width), BF16),
-        "small_mine": pltpu.VMEM((3, 2, 16, half), F32),
-        "small_in": pltpu.VMEM((2 + zs, 2, 16, half), F32),
-        "incoming": pltpu.VMEM((2, owners, share, width), BF16),
+        "outgoing": pltpu.VMEM((owners, capacity, half), BF16),
+        "small_mine": pltpu.VMEM((2, 2, 16, half), F32),
+        "small_in": pltpu.VMEM((3 + zs, 2, 16, half), F32),
+        "incoming": pltpu.VMEM((2, owners, capacity, half), BF16),
         "rows_v": pltpu.VMEM((2 * count, width), BF16),
-        "ordered": pltpu.VMEM((2 * count, width), F32),
         "turn": pltpu.VMEM((2 * count, 2 * count), BF16),
         "sorted_v": pltpu.VMEM((1, 2 * count), jnp.int32),
         "limits_v": pltpu.VMEM((1, 128), jnp.int32),
@@ -1042,19 +1081,19 @@
         "grad_w_v": pltpu.VMEM((block, 5 * half), F32),
         "small_v": pltpu.VMEM((2, 16, half), F32),
         "load_sem": dma((21,)),
-        "table_sem": dma((8,)),
+        "table_sem": dma((4,)),
     }
     for name in ("owner", "offset", "w_uvqk", "w_out", "b", "rel", "time", "gain_out", "gain_in", "b_out", "lengths", "times"):
         scratch[name + "_v"] = pltpu.VMEM(inputs[name].shape, inputs[name].dtype)
     for name, number in (
         ("req", owners - 1), ("item", owners - 1), ("emb", 3), ("row", 2), ("small", 1), ("wz", zs - 1), ("wx", zs),
-        ("wy", 2 * zs - 2), ("wc", 2 * zs), ("mixed", 3), ("back", 3), ("give", owners - 1), ("hand", owners), ("sum", 2 + zs),
+        ("wy", 2 * zs - 2), ("wc", 2 * zs), ("mixed", 3), ("back", 6), ("give", owners - 1), ("hand", owners), ("sum", 3 + zs),
     ):
         scratch[name + "_send"] = dma((number,))
         scratch[name + "_recv"] = dma((number,))
-    scratch |= weight_sum_scratch("a_", "zxy", zs, block, 2 * half)
+    scratch |= weight_sum_scratch("a_", ORDERS["a_"], zs, block, 2 * half)
     for i in range(half // 128):
-        scratch |= weight_sum_scratch(f"b{i}_", "yxz", zs, block, 384)
+        scratch |= weight_sum_scratch(f"b{i}_", ORDERS[f"b{i}_"], zs, block, 384)
     hbm = pl.BlockSpec(memory_space=pltpu.HBM)
     found = pl.pallas_call(
         functools.partial(main_kernel, tuple(inputs), tuple(outs), tuple(scratch)),
@@ -1238,7 +1277,7 @@
 
 
 def solution(mesh):
-    one_stream = mesh.shape["ka"] * mesh.shape["ha"] == MB and mesh.shape["ka"] == 2
+    one_stream = mesh.shape["ka"] * mesh.shape["ha"] == MB and mesh.shape["ka"] == 2 and mesh.shape["pb"] == 8
     return jax.shard_map(
         local_streams if one_stream else local_general,
         mesh=mesh,

time: 92.6 us -> 89 us (0.961)
  Pallas kernels: 90.4 us -> 87.2 us
    pallas_call x1, Pallas kernels: 82 us -> 78.8 us  [run_main(): pl.pallas_call(functools.partial(main_kernel, tuple(inputs), tuple(outs),...]
where the time goes in v5:
time: 89 us; the launch traced here: 88 us
  Pallas kernels  87.2 us (98%)
    pallas_call x1, Pallas kernels, run_main(): pl.pallas_call(functools.partial(main_kernel, tuple(inputs), tuple(outs),...  78.8 us
    pallas_call x1, Pallas kernels, scatter_rows(): pl.pallas_call(scatter_kernel, out_shape=outs, in_specs=[hbm] * len(names...  8.44 us

profile of v5, /device:TPU:0, one launch (start us, length us, event | category | flops | bytes accessed | tf_op | source)
XLA Modules:
  0.0 88.0 jit_solution(15386337594153236076)
XLA Ops:
  0.6 78.8 %shard_map.230 = (bf16[1024,512]{1,0:T(8,128)(2,1)}, s32[1,1024]{1,0:T(1,128)}, s32[1,128]{1,0:T(1,128)}, bf16[4,128,512]{2,1,0:T(8,128)(2,1)}, bf16[4,128,256]{...) custom-call(s32[1,512]{1,0:T(1,128)} %bitcast.16, s32[1,512]{1,0:T(1,128)} %bitcast.17, ...), custom_call_target="tpu_custom_call" | custom-call | tf_op jit(solution)/shard_map/pallas_call | solution.py:1098
  79.4 8.4 %shard_map.231 = (f32[8192,512]{1,0:T(8,128)}, f32[32,4,256]{2,1,0:T(4,128)}, f32[32,256]{1,0:T(8,128)}, f32[4,256]{1,0:T(4,128)}, f32[4,256]{1,0:T(4,128)}, /*i...) custom-call(s32[1,128]{1,0:T(1,128)} %get-tuple-element.29.limits_in, ...), custom_call_target="tpu_custom_call" | custom-call | tf_op jit(solution)/shard_map/pallas_call | solution.py:1201

commit v6 on v5

--- a/solution.py
+++ b/solution.py
@@ -522,9 +522,9 @@
     "pair 0": ("a_",),
     "rows sent": (),
     "tables": (),
-    "given": ("b0_", "b1_", "a_"),
+    "given": ("b0_", "b1_"),
     "take 1": (),
-    "take 2": ("b0_",),
+    "take 2": ("b0_", "a_"),
     "take 3": (),
     "take 4": ("b1_",),
     "take 5": (),
@@ -625,8 +625,7 @@
         req.start(requests.at[to], arrived.at[at.me], device)
     arrived[at.me] = requests[at.me]
     my_half = pl.ds(pl.multiple_of(ka * block, block), block)
-    for d in range(1, zs):
-        wz.start(shard.at[my_half], w.at[ha, at.pb, my_half], at.z_device(d))
+    wz.start(shard.at[my_half], w.at[ha, at.pb, my_half], at.z_device(1))
     wx.start(shard, w.at[ha, at.pb], at.x_peer)
     small_c.start(small.at[ha], small.at[ha], at.x_peer)
     row_c.start(s["context"].at[away], s["ctx_v"].at[ka], at.y_peer)
@@ -635,6 +634,8 @@
 
     for i in range(owners - 1):
         req.arrive(i)
+    for d in range(2, zs):
+        wz.start(shard.at[my_half], w.at[ha, at.pb, my_half], at.z_device(d))
     wide_pick = iota((capacity, 128), 1) == iota((capacity, 128), 0)
 
     def column_of(source):
@@ -878,12 +879,6 @@
                 grad_pre[hf, :, there] = (part * slope[hf, :, there]).astype(BF16)
         if pair == 0:
             steps_at("pair 0")
-        if pair < pairs - 1:
-            for hf in range(2):
-                for g in range(1, 4):
-                    there = slice(g * half + pair * 128, g * half + (pair + 1) * 128)
-                    put(s[f"b{pair}_own"], hf, (g - 1) * 128, mm_tn(normed, grad_pre[hf, :, there]))
-            sums_b[pair].cores()
     grad_normed = None
     for hf in range(2):
         part = mm_nt(grad_pre[hf], w_half(hf, slice(0, 4 * half)))
@@ -899,11 +894,12 @@
             here = grad_start.at[pl.ds(pl.multiple_of(to_ka * tok, tok), tok), cols]
             back_c.start(here, grad_rows.at[at.stream, :, cols], device)
     grad_rows[at.stream] = grad_start[own_rows]
-    for hf in range(2):
-        for g in range(1, 4):
-            there = slice(g * half + (pairs - 1) * 128, g * half + pairs * 128)
-            put(s[f"b{pairs - 1}_own"], hf, (g - 1) * 128, mm_tn(normed, grad_pre[hf, :, there]))
-    sums_b[-1].cores()
+    for pair in range(pairs):
+        for hf in range(2):
+            for g in range(1, 4):
+                there = slice(g * half + pair * 128, g * half + (pair + 1) * 128)
+                put(s[f"b{pair}_own"], hf, (g - 1) * 128, mm_tn(normed, grad_pre[hf, :, there]))
+        sums_b[pair].cores()
     steps_at("rows sent")
     gain_grad = jnp.sum(grad_normed * unit_in, axis=0, keepdims=True)
     bout_grad = jnp.sum(cot32, axis=0, keepdims=True)
@@ -1015,8 +1011,12 @@
     out_copies += [local(18, grad_w, s["grad_w"]), local(19, s["small_v"], s["small_sum"])]
     for i in range(owners):
         hand.arrive(i)
-    in_order(1 - ha)
-    out_copies.append(local(20, s["rows_v"], s["rows"]))
+    cols = pl.ds(pl.multiple_of((1 - ha) * half, half), half)
+    handed = incoming[1 - ha].reshape(slots, half)
+    for i in range(slots // 256):
+        rows = pl.ds(i * 256, 256)
+        s["rows_v"][rows, cols] = mm(s["turn"][rows, :], handed).astype(BF16)
+        out_copies.append(local(20 + i, s["rows_v"].at[rows], s["rows"].at[rows]))
     for copy in out_copies:
         copy.wait()
     for kind in (req, item, emb_c, row_c, small_c, wz, wx, wy, wc, mixed_c, back_c, give, hand, sum_c):
@@ -1080,7 +1080,7 @@
         "mixed_v": pltpu.VMEM((MB, tok, half), BF16),
         "grad_w_v": pltpu.VMEM((block, 5 * half), F32),
         "small_v": pltpu.VMEM((2, 16, half), F32),
-        "load_sem": dma((21,)),
+        "load_sem": dma((20 + 2 * count // 256,)),
         "table_sem": dma((4,)),
     }
     for name in ("owner", "offset", "w_uvqk", "w_out", "b", "rel", "time", "gain_out", "gain_in", "b_out", "lengths", "times"):
@@ -1111,21 +1111,32 @@
 def scatter_kernel(
     limits_in, sorted_in, rows_in, grad_w_in, small_in, mixed_in, grad_rows_in,
     out_ref, w_ref, w_out_ref, b_ref, rel_ref, time_ref, gain_in_ref, gain_out_ref, b_out_ref, mixed_out, grad_rows_out,
-    limits, ids, rows, grad_w_ref, small_ref, mixed, grad_rows, tiles, load_sem, tile_sem, pass_sem,
+    limits, ids, rows, grad_w_ref, small_ref, mixed, grad_rows, tiles, load_sem, row_sem, tile_sem, pass_sem,
 ):
     pairs_in = [
-        (limits_in, limits), (sorted_in, ids), (rows_in, rows), (grad_w_in, grad_w_ref), (small_in, small_ref),
+        (limits_in, limits), (sorted_in, ids), (grad_w_in, grad_w_ref), (small_in, small_ref),
         (mixed_in, mixed), (grad_rows_in, grad_rows),
     ]
+    depth = 256
+
+    def load_rows(j):
+        here = pl.ds(j * depth, depth)
+        return pltpu.make_async_copy(rows_in.at[here], rows.at[here], row_sem.at[j])
+
+    blocks = rows.shape[0] // depth
     loads = [pltpu.make_async_copy(src, dst, load_sem.at[i]) for i, (src, dst) in enumerate(pairs_in)]
-    for load in loads:
+    for load in loads[:2]:
         load.start()
-    for load in loads[:3]:
+    for j in range(blocks):
+        load_rows(j).start()
+    for load in loads[2:]:
+        load.start()
+    for load in loads[:2]:
         load.wait()
+    load_rows(0).wait()
     slots, tile = tiles.shape[0], tiles.shape[1]
     count = out_ref.shape[0] // tile
     per_tile = tile // 256
-    depth = 256
 
     def write(i, slot):
         there = pl.ds(pl.multiple_of(i * tile, tile), tile)
@@ -1155,8 +1166,17 @@
         write(i, slot).start()
         return carry
 
-    lax.fori_loop(0, 2, step, 0)
-    for load in loads[3:]:
+    crowded = limits[0, per_tile] > depth
+
+    def other_rows():
+        for j in range(1, blocks):
+            load_rows(j).wait()
+
+    pl.when(crowded)(other_rows)
+    step(0, 0)
+    pl.when(jnp.logical_not(crowded))(other_rows)
+    lax.fori_loop(1, 3, step, 0)
+    for load in loads[2:]:
         load.wait()
     passed = [
         pltpu.make_async_copy(mixed, mixed_out, pass_sem.at[0]),
@@ -1164,7 +1184,7 @@
     ]
     for copy in passed:
         copy.start()
-    lax.fori_loop(2, count, step, 0)
+    lax.fori_loop(3, count, step, 0)
     half = w_ref.shape[2]
     buckets = time_ref.shape[1]
     w_ref[:, 0, :] = grad_w_ref[:, 0:half]
@@ -1213,6 +1233,7 @@
             pltpu.VMEM(found["grad_rows"].shape, BF16),
             pltpu.VMEM((slots, tile, width), F32),
             pltpu.SemaphoreType.DMA((len(names),)),
+            pltpu.SemaphoreType.DMA((rows.shape[0] // 256,)),
             pltpu.SemaphoreType.DMA((slots,)),
             pltpu.SemaphoreType.DMA((2,)),
         ],

time: 89 us -> 87.2 us (0.980)
  Pallas kernels: 87.2 us -> 85.8 us
    pallas_call x1, Pallas kernels: 78.8 us -> 77.5 us  [run_main(): pl.pallas_call(functools.partial(main_kernel, tuple(inputs), tuple(outs),...]
where the time goes in v6:
time: 87.2 us; the launch traced here: 86.6 us
  Pallas kernels  85.8 us (98%)
    pallas_call x1, Pallas kernels, run_main(): pl.pallas_call(functools.partial(main_kernel, tuple(inputs), tuple(outs),...  77.5 us
    pallas_call x1, Pallas kernels, scatter_rows(): pl.pallas_call(scatter_kernel, out_shape=outs, in_specs=[hbm] * len(names...  8.26 us

profile of v6, /device:TPU:0, one launch (start us, length us, event | category | flops | bytes accessed | tf_op | source)
XLA Modules:
  0.0 86.6 jit_solution(3725370100679237472)
XLA Ops:
  0.6 77.5 %shard_map.230 = (bf16[1024,512]{1,0:T(8,128)(2,1)}, s32[1,1024]{1,0:T(1,128)}, s32[1,128]{1,0:T(1,128)}, bf16[4,128,512]{2,1,0:T(8,128)(2,1)}, bf16[4,128,256]{...) custom-call(s32[1,512]{1,0:T(1,128)} %bitcast.16, s32[1,512]{1,0:T(1,128)} %bitcast.17, ...), custom_call_target="tpu_custom_call" | custom-call | tf_op jit(solution)/shard_map/pallas_call | solution.py:1098
  78.2 8.3 %shard_map.231 = (f32[8192,512]{1,0:T(8,128)}, f32[32,4,256]{2,1,0:T(4,128)}, f32[32,256]{1,0:T(8,128)}, f32[4,256]{1,0:T(4,128)}, f32[4,256]{1,0:T(4,128)}, /*i...) custom-call(s32[1,128]{1,0:T(1,128)} %get-tuple-element.29.limits_in, ...), custom_call_target="tpu_custom_call" | custom-call | tf_op jit(solution)/shard_map/pallas_call | solution.py:1221

commit v7 on v6

--- a/solution.py
+++ b/solution.py
@@ -1081,7 +1081,7 @@
         "grad_w_v": pltpu.VMEM((block, 5 * half), F32),
         "small_v": pltpu.VMEM((2, 16, half), F32),
         "load_sem": dma((20 + 2 * count // 256,)),
-        "table_sem": dma((4,)),
+        "table_sem": dma((2,)),
     }
     for name in ("owner", "offset", "w_uvqk", "w_out", "b", "rel", "time", "gain_out", "gain_in", "b_out", "lengths", "times"):
         scratch[name + "_v"] = pltpu.VMEM(inputs[name].shape, inputs[name].dtype)

time: 87.2 us -> 87.2 us (level)
  no operation moved by 1% of the time
where the time goes in v7:
time: 87.2 us; the launch traced here: 86.1 us
  Pallas kernels  85.3 us (98%)
    pallas_call x1, Pallas kernels, run_main(): pl.pallas_call(functools.partial(main_kernel, tuple(inputs), tuple(outs),...  77 us
    pallas_call x1, Pallas kernels, scatter_rows(): pl.pallas_call(scatter_kernel, out_shape=outs, in_specs=[hbm] * len(names...  8.27 us

profile of v7, /device:TPU:0, one launch (start us, length us, event | category | flops | bytes accessed | tf_op | source)
XLA Modules:
  0.0 86.1 jit_solution(10224055825938576516)
XLA Ops:
  0.6 77.0 %shard_map.230 = (bf16[1024,512]{1,0:T(8,128)(2,1)}, s32[1,1024]{1,0:T(1,128)}, s32[1,128]{1,0:T(1,128)}, bf16[4,128,512]{2,1,0:T(8,128)(2,1)}, bf16[4,128,256]{...) custom-call(s32[1,512]{1,0:T(1,128)} %bitcast.16, s32[1,512]{1,0:T(1,128)} %bitcast.17, ...), custom_call_target="tpu_custom_call" | custom-call | tf_op jit(solution)/shard_map/pallas_call | solution.py:1098
  77.7 8.3 %shard_map.231 = (f32[8192,512]{1,0:T(8,128)}, f32[32,4,256]{2,1,0:T(4,128)}, f32[32,256]{1,0:T(8,128)}, f32[4,256]{1,0:T(4,128)}, f32[4,256]{1,0:T(4,128)}, /*i...) custom-call(s32[1,128]{1,0:T(1,128)} %get-tuple-element.29.limits_in, ...), custom_call_target="tpu_custom_call" | custom-call | tf_op jit(solution)/shard_map/pallas_call | solution.py:1221
